TPU v7x, 256 devices: a whole 4x4x8 slice. The times are simulated.
256 devices in a mesh: tmpl: 32 (over x, y, core), chan: 8 (over z).
Axes of the slice: x: 4, y: 4, z: 8, core: 2. Of those that a mesh axis runs over, the one named last changes fastest.
Arguments:
- record: float32 [1024, 12288], P(None, ('tmpl', 'chan')), as said below
- channel_order: int32 [1024], replicated, may hold values from 0 to 1023, each once
- templates: float32 [256, 30, 600], P('tmpl'), as said below
- group_of_slot: int32 [256, 30, 1], replicated, may hold values from 0 to 7; in each aligned block of 240 rows (0 to 239, 240 to 479, ..., all dimensions but the last counted through in order) at most 60 rows name the same one
- place_of_slot: int32 [256, 30], replicated, may hold values from 0 to 127
Outputs:
- stack: float32 [256, 12288], P('tmpl', 'chan')
Inputs may be any that keep to these rules, and one draw needn't show every extreme that they name: Channels channel_order[g * 128] to channel_order[(g + 1) * 128 - 1] form channel group g. `group_of_slot`: among the 240 slots of one template block, at most 60 name the same channel group. `record`: real samples. `templates`: real samples.
All inputs are finite; a program needn't handle non-finite values.
Results may differ from a plain program's by a relative error of at most 0.000098.
Values sent between devices are 32-bit elements; how exact they have to be, the bound alone decides.
No kernel may reach another device: no remote copies, remote signals or barrier semaphores. Data moves between devices by JAX's collectives and lax.ppermute only.
A program may use at most 128 MiB of HBM per device.

v0:
```python
import jax
import jax.numpy as jnp
from jax import lax
from jax.sharding import PartitionSpec as P

SLOTS_PER_TMPL = 30
PATTERN_SAMPLES = 600
NSEG = 1024
HOP = 384


HIGH = lax.Precision.HIGHEST


def from_behind(value, axis, steps):
    count = lax.axis_size(axis)
    pairs = [(source, (source + steps) % count) for source in range(count)]
    return lax.ppermute(value, axis, pairs)


def dft_tables():
    half_len = NSEG // 2
    sample = jnp.arange(NSEG, dtype=jnp.int32)
    frequency = jnp.arange(half_len + 1, dtype=jnp.int32)
    lag_index = jnp.arange(HOP, dtype=jnp.int32)
    two_pi = 2.0 * jnp.pi / NSEG
    angles = (sample[:, None] * frequency[None, :] % NSEG).astype(jnp.float32) * two_pi
    forward = jnp.concatenate([jnp.cos(angles), -jnp.sin(angles[:, 1:half_len])], axis=1)
    back_angles = (frequency[:, None] * lag_index[None, :] % NSEG).astype(jnp.float32) * two_pi
    weight = (
        jnp.where((frequency == 0) | (frequency == half_len), 1.0, 2.0).astype(jnp.float32) / NSEG
    )
    inverse = jnp.concatenate(
        [jnp.cos(back_angles) * weight[:, None], -2.0 / NSEG * jnp.sin(back_angles[1:half_len])],
        axis=0,
    )
    offset = sample[:, None] - lag_index[None, :]
    window_band = ((offset >= 0) & (offset < PATTERN_SAMPLES)).astype(jnp.float32)
    return (forward, inverse, window_band)


def spectral_product(left_spec, right_spec):
    half_len = NSEG // 2
    left_real = left_spec[..., : half_len + 1]
    right_real = right_spec[..., : half_len + 1]
    left_zero = jnp.zeros_like(left_spec[..., :1])
    right_zero = jnp.zeros_like(right_spec[..., :1])
    left_imag = jnp.concatenate([left_zero, left_spec[..., half_len + 1 :], left_zero], axis=-1)
    right_imag = jnp.concatenate([right_zero, right_spec[..., half_len + 1 :], right_zero], axis=-1)
    prod_real = left_real * right_real + left_imag * right_imag
    prod_imag = left_real * right_imag - left_imag * right_real
    return jnp.concatenate([prod_real, prod_imag[..., 1:half_len]], axis=-1)


def compact(groups, places, owner_group, capacity):
    member = groups == owner_group
    slot_rank = jnp.cumsum(member.astype(jnp.int32)) - 1
    target = jnp.where(member, slot_rank, capacity)
    slot_count = groups.shape[0]
    picked_slots = (
        jnp.zeros((capacity + 1,), jnp.int32)
        .at[target]
        .set(jnp.arange(slot_count, dtype=jnp.int32))[:capacity]
    )
    slots_filled = jnp.zeros((capacity + 1,), jnp.float32).at[target].set(1.0)[:capacity]
    return (picked_slots, slots_filled, places[picked_slots])


def block_stack(tmpl_spec, positions, picked_slots, seg_spec, seg_energy, inverse, block_extent):
    chosen = seg_spec[:, positions]
    product = spectral_product(tmpl_spec[None], chosen)
    normed = jnp.einsum("smf,ft->smt", product, inverse, precision=HIGH) / seg_energy[:, positions]
    selector = (
        (picked_slots // SLOTS_PER_TMPL)[:, None]
        == jnp.arange(block_extent, dtype=jnp.int32)[None, :]
    ).astype(jnp.float32)
    return jnp.einsum("mk,smt->kst", selector, normed, precision=HIGH)


def shards(record, channel_order, templates, group_of_slot, place_of_slot):
    chan_count = lax.axis_size("chan")
    block_count = lax.axis_size("tmpl")
    block_extent = templates.shape[0]
    count_of_rows = block_extent * SLOTS_PER_TMPL
    capacity = 2 * count_of_rows // chan_count
    my_block = lax.axis_index("tmpl")
    my_group = lax.axis_index("chan")
    forward, inverse, window_band = dft_tables()
    ordered = record[channel_order]
    owned = lax.all_to_all(ordered, "chan", split_axis=0, concat_axis=1, tiled=True)
    block_span = owned.shape[1]
    needed = PATTERN_SAMPLES - 1
    pieces = [owned]
    for next_increment in range(1, (needed + block_span - 1) // block_span + 1):
        pieces.append(from_behind(owned, "tmpl", -next_increment))
    extended = jnp.concatenate(pieces, axis=1)[:, : block_span + needed]
    extended = jnp.pad(extended, ((0, 0), (0, NSEG - HOP - needed)))
    seg_count = block_span // HOP
    windows = jnp.stack([extended], axis=0)
    spectra = jnp.einsum("scu,uf->scf", windows, forward, precision=HIGH)
    energy = jnp.sqrt(
        jnp.einsum("scu,ut->sct", windows * windows, window_band, precision=HIGH) / PATTERN_SAMPLES
        + 1e-06
    )
    tmpl_waves = templates.reshape(count_of_rows, PATTERN_SAMPLES)
    template_norms = jnp.sqrt(jnp.mean(tmpl_waves * tmpl_waves, axis=1) + 1e-06)
    groups_all = group_of_slot.reshape(block_count, count_of_rows)
    places_all = place_of_slot.reshape(block_count, count_of_rows)
    own_groups = lax.dynamic_index_in_dim(groups_all, my_block, 0, keepdims=False)
    own_places = lax.dynamic_index_in_dim(places_all, my_block, 0, keepdims=False)
    picked_slots, slots_filled, positions = compact(own_groups, own_places, my_group, capacity)
    scale_factor = slots_filled / (
        template_norms[picked_slots] * jnp.sqrt(jnp.float32(PATTERN_SAMPLES * SLOTS_PER_TMPL))
    )
    tmpl_spec = (
        jnp.dot(tmpl_waves[picked_slots], forward[:PATTERN_SAMPLES], precision=HIGH)
        * scale_factor[:, None]
    )

    def per_segment(seg_item):
        seg_spec, seg_energy = seg_item
        return block_stack(
            tmpl_spec,
            positions,
            picked_slots,
            seg_spec[None],
            seg_energy[None],
            inverse,
            block_extent,
        )[:, 0, :]

    initial = jnp.zeros((block_count * seg_count, block_extent, HOP), jnp.float32)
    stacks = lax.map(
        per_segment,
        (
            lax.all_gather(spectra, "tmpl", axis=0, tiled=True),
            lax.all_gather(energy, "tmpl", axis=0, tiled=True),
        ),
        batch_size=4,
    )
    collected = lax.dynamic_update_slice_in_dim(initial, stacks, jnp.int32(0), 0)
    partial_stack = jnp.transpose(collected, (1, 0, 2)).reshape(
        block_extent, block_count * block_span
    )
    return lax.psum_scatter(partial_stack, "chan", scatter_dimension=1, tiled=True)


def solution(mesh):
    placed = (P(None, ("tmpl", "chan")), P(), P("tmpl", None, None), P(), P())
    return jax.shard_map(
        shards, mesh=mesh, in_specs=placed, out_specs=P("tmpl", "chan"), check_vma=False
    )
```

profile of v0, /device:TPU:1, one launch (start us, length us, event | category | flops | bytes accessed | tf_op | source)
XLA Modules:
  0.0 320.6 jit_solution(16568420647119892529)
XLA Ops:
  8.4 2.8 gather_fusion.4
  11.3 17.6 %all_to_all.19 = f32[8,128,48]{1,2,0:T(8,128)S(1)} all-to-all(f32[8,128,48]{1,2,0:T(8,128)S(1)} %copy.41), channel_id=1, replica_groups=mesh['tmpl'=32,'chan'=8] {'chan'}, dimensions={0} | all-to-all | bytes 393216 | tf_op jit(solution)/shard_map/all_to_all | solution.py:90
  29.0 2.6 collective-permute-start
  31.6 4.9 %collective-permute-start.1 = (f32[128,384]{0,1:T(8,128)S(1)}, f32[128,384]{0,1:T(8,128)S(1)}, u32[]{:S(2)}, u32[]{:S(2)}) collective-permute-start(f32[128,384]{0,1:T(8,128)S(1)} %bitcast.106), channel_id=1, source_target_pairs={{0,240},{8,248},{16,0},{24,8},{32,16},{40,24},{48,32},{56,40},{64,... | collective-permute-start | bytes 589832 | tf_op jit(solution)/shard_map/ppermute | solution.py:18
  36.5 1.7 collective-permute-done
  38.2 2.8 collective-permute-done.1
  41.7 1.6 fusion.46
  43.5 1.3 fusion.21
  44.8 9.4 %fusion.39 = f32[1024,513]{1,0:T(8,128)S(1)} fusion(), kind=kLoop, calls=%fused_computation.66 | loop fusion | flops 7354368 | bytes 2101248 | tf_op jit(solution)/shard_map/cos | solution.py:28
  54.2 7.3 %fusion.29 = f32[1024,511]{1,0:T(8,128)S(1)} fusion(f32[1024,513]{1,0:T(8,128)S(1)} %fusion.21), kind=kLoop, calls=%fused_computation.55 | loop fusion | flops 523264 | bytes 4186112 | tf_op jit(solution)/shard_map/neg | solution.py:28
  61.6 1.3 copy-done.1
  62.9 3.7 %fusion.15 = f32[128,1024]{1,0:T(8,128)} fusion(f32[1024,511]{1,0:T(8,128)S(1)} %fusion.29, f32[1024,513]{1,0:T(8,128)S(1)} %fusion.39, f32[128,384]{0,1:T(8,128)S(1)} %copy-done.9, f32[128,384]{0,1:T(8,128)S(1)} %copy-done.7, f32[128,384]{0,1:T(8,128)S(1)} %bitcast.108, pred[1024]{0:T(1024)(128)(4,1)S(1)} %copy-done.12), kind=kOutput, calls=%fused_computation.37 | convolution fusion | flops 1612054528 | bytes 5309440 | tf_op jit(solution)/shard_map/scu,uf->scf/dot_general | solution.py:100
  68.8 1.2 reshape.203
  70.1 1.3 scatter_custom_fusion
  74.0 1.3 scatter_custom_fusion.1
  75.8 3.0 cosine_multiply_fusion
  78.8 2.9 fusion.55
  81.7 1.3 pad_maximum_fusion.1
  83.0 1.8 fusion.36
  84.9 11.2 %all-gather.7.cloned.1.call-done = f32[4096,384]{1,0:T(8,128)} async-done(((f32[128,384]{1,0:T(8,128)}), f32[4096,384]{1,0:T(8,128)}) %all-gather.7.cloned.1.call-update) | async-done | bytes 6291472 | tf_op jit(solution)/shard_map/all_gather | solution.py:137
  96.1 79.1 %all-gather.5.cloned.1.call-done = f32[4096,1024]{1,0:T(8,128)} async-done(((f32[128,1024]{1,0:T(8,128)}), f32[4096,1024]{1,0:T(8,128)}) %all-gather.5.cloned.1.call-update) | async-done | bytes 16777232 | tf_op jit(solution)/shard_map/all_gather | solution.py:136
  175.2 107.2 %while.12 = (s32[]{:T(128)}, f32[8,4,8,384]{3,2,1,0:T(8,128)}, s32[60,1]{0,1:T(1,128)S(1)}, s32[60]{0:T(128)S(1)}, f32[60,1024]{1,0:T(8,128)S(1)}, /*index=5*/f3...) while((s32[]{:T(128)}, f32[8,4,8,384]{3,2,1,0:T(8,128)}, ...), condition=%wide.region_6.7_spmd, body=%wide.region_5.6_spmd.sunk | while | flops 1142694528 | bytes 34814304 | solution.py:133
  175.2 1.8 constant_dynamic-slice_fusion.5
  177.0 1.4 copy.59
  178.4 1.1 gather_fusion
  181.4 1.3 constant_dynamic-slice_fusion.6
  183.3 1.5 gather_fusion.1
  184.8 2.9 fusion.95
  188.6 1.8 constant_dynamic-slice_fusion.5
  190.4 1.4 copy.59
  194.9 1.3 constant_dynamic-slice_fusion.6
  196.7 1.5 gather_fusion.1
  198.2 2.9 fusion.95
  202.0 1.8 constant_dynamic-slice_fusion.5
  203.8 1.4 copy.59
  208.3 1.3 constant_dynamic-slice_fusion.6
  210.1 1.5 gather_fusion.1
  211.6 2.9 fusion.95
  215.4 1.8 constant_dynamic-slice_fusion.5
  217.2 1.4 copy.59
  221.7 1.3 constant_dynamic-slice_fusion.6
  223.5 1.5 gather_fusion.1
  225.0 2.9 fusion.95
  228.8 1.8 constant_dynamic-slice_fusion.5
  230.6 1.4 copy.59
  235.1 1.3 constant_dynamic-slice_fusion.6
  236.9 1.5 gather_fusion.1
  238.4 2.9 fusion.95
  242.2 1.8 constant_dynamic-slice_fusion.5
  244.0 1.4 copy.59
  248.5 1.3 constant_dynamic-slice_fusion.6
  250.3 1.5 gather_fusion.1
  251.8 2.9 fusion.95
  255.6 1.8 constant_dynamic-slice_fusion.5
  257.5 1.4 copy.59
  261.9 1.3 constant_dynamic-slice_fusion.6
  263.7 1.5 gather_fusion.1
  265.2 2.9 fusion.95
  269.0 1.8 constant_dynamic-slice_fusion.5
  270.9 1.4 copy.59
  275.3 1.3 constant_dynamic-slice_fusion.6
  277.1 1.5 gather_fusion.1
  278.6 2.9 fusion.95
  282.5 31.6 %reduce-scatter.2.cloned.1.call-done = f32[8,1536]{1,0:T(8,128)} async-done(((f32[8,12288]{1,0:T(8,128)}), f32[8,1536]{1,0:T(8,128)}) %reduce-scatter.2.cloned.1.call-update) | async-done | bytes 49168 | tf_op jit(solution)/shard_map/reduce_scatter | solution.py:145
  (232 shorter events, 41.9 us)
Async XLA Ops:
  6.5 89.5 %all-gather.7.cloned.1.call-start = ((), (), s32[]{:S(2)}) async-start(), calls=%async_computation.4 | async-start | bytes 6488064 | tf_op jit(solution)/shard_map/all_gather | solution.py:137
  8.4 33.3 %copy-start.12 = (pred[1024]{0:T(1024)(128)(4,1)S(1)}, pred[1024]{0:T(1024)(128)(4,1)}, u32[]{:S(2)}) copy-start(pred[1024]{0:T(1024)(128)(4,1)} %constant.119.clone.1) | copy-start | bytes 3076
  29.0 9.2 %collective-permute-start = (f32[128,384]{0,1:T(8,128)S(1)}, f32[128,384]{0,1:T(8,128)S(1)}, u32[]{:S(2)}, u32[]{:S(2)}) collective-permute-start(f32[128,384]{0,1:T(8,128)S(1)} %bitcast.105), channel_id=1, source_target_pairs={{0,248},{8,0},{16,8},{24,16},{32,24},{40,32},{48,40},{56,48},{64,5... | collective-permute-start | bytes 589832 | tf_op jit(solution)/shard_map/ppermute | solution.py:18
  31.6 9.4 %collective-permute-start.1 = (f32[128,384]{0,1:T(8,128)S(1)}, f32[128,384]{0,1:T(8,128)S(1)}, u32[]{:S(2)}, u32[]{:S(2)}) collective-permute-start(f32[128,384]{0,1:T(8,128)S(1)} %bitcast.106), channel_id=1, source_target_pairs={{0,240},{8,248},{16,0},{24,8},{32,16},{40,24},{48,32},{56,40},{64,... | collective-permute-start | bytes 589832 | tf_op jit(solution)/shard_map/ppermute | solution.py:18
  38.2 2.8 copy-start.6
  41.0 0.7 copy-start.8
  43.3 131.9 %all-gather.5.cloned.1.call-start = ((), (), s32[]{:S(2)}) async-start(), calls=%async_computation.3 | async-start | bytes 17301504 | tf_op jit(solution)/shard_map/all_gather | solution.py:136
  54.2 8.7 %copy-start.7 = (f32[128,384]{0,1:T(8,128)S(1)}, f32[128,384]{0,1:T(8,128)}, u32[]{:S(2)}) copy-start(f32[128,384]{0,1:T(8,128)} %copy-done.6) | copy-start | bytes 589828
  54.2 8.7 %copy-start.9 = (f32[128,384]{0,1:T(8,128)S(1)}, f32[128,384]{0,1:T(8,128)}, u32[]{:S(2)}) copy-start(f32[128,384]{0,1:T(8,128)} %copy-done.8) | copy-start | bytes 589828
  61.6 1.3 copy-start.1
  62.9 3.8 %copy-start.11 = (s32[256,30,1]{0,2,1:T(1,128)S(1)}, s32[256,30,1]{0,2,1:T(1,128)}, u32[]{:S(2)}) copy-start(s32[256,30,1]{0,2,1:T(1,128)} %param.10) | copy-start | bytes 92164
  62.9 4.6 %copy-start.5 = (f32[8,30,600]{2,0,1:T(8,128)S(1)}, f32[8,30,600]{2,0,1:T(8,128)}, u32[]{:S(2)}) copy-start(f32[8,30,600]{2,0,1:T(8,128)} %param.9) | copy-start | bytes 1728004
  66.7 247.4 %reduce-scatter.2.cloned.1.call-start = ((), (), s32[]{:S(2)}) async-start(), calls=%async_computation.2 | async-start | bytes 442368 | tf_op jit(solution)/shard_map/reduce_scatter | solution.py:145
  67.0 6.0 %copy-start.10 = (s32[256,30]{0,1:T(8,128)S(1)}, s32[256,30]{0,1:T(8,128)}, u32[]{:S(2)}) copy-start(s32[256,30]{0,1:T(8,128)} %param.11) | copy-start | bytes 92164
  75.8 7.2 %copy-start.2 = (f32[1024,511]{1,0:T(8,128)S(1)}, f32[1024,511]{1,0:T(8,128)}, u32[]{:S(2)}) copy-start(f32[1024,511]{1,0:T(8,128)} %copy-done.1) | copy-start | bytes 6279172
  175.2 5.3 %copy-start.3 = (f32[60,1024]{1,0:T(8,128)}, f32[60,1024]{1,0:T(8,128)S(1)}, u32[]{:S(2)}) copy-start(f32[60,1024]{1,0:T(8,128)S(1)} %get-tuple-element.267) | copy-start | bytes 737284 | tf_op jit(solution)/shard_map/while
  181.1 3.7 %copy-start = (f32[1024,384]{1,0:T(8,128)S(1)}, f32[1024,384]{1,0:T(8,128)}, u32[]{:S(2)}) copy-start(f32[1024,384]{1,0:T(8,128)} %get-tuple-element.270) | copy-start | bytes 4718596 | tf_op jit(solution)/shard_map/while
  184.8 3.8 %copy-start.4 = (f32[60,1024]{1,0:T(8,128)S(1)}, f32[60,1024]{1,0:T(8,128)}, u32[]{:S(2)}) copy-start(f32[60,1024]{1,0:T(8,128)} %copy-done.3) | copy-start | bytes 737284 | tf_op jit(solution)/shard_map/while
  188.6 5.3 %copy-start.3 = (f32[60,1024]{1,0:T(8,128)}, f32[60,1024]{1,0:T(8,128)S(1)}, u32[]{:S(2)}) copy-start(f32[60,1024]{1,0:T(8,128)S(1)} %get-tuple-element.267) | copy-start | bytes 737284 | tf_op jit(solution)/shard_map/while
  194.5 3.7 %copy-start = (f32[1024,384]{1,0:T(8,128)S(1)}, f32[1024,384]{1,0:T(8,128)}, u32[]{:S(2)}) copy-start(f32[1024,384]{1,0:T(8,128)} %get-tuple-element.270) | copy-start | bytes 4718596 | tf_op jit(solution)/shard_map/while
  198.2 3.8 %copy-start.4 = (f32[60,1024]{1,0:T(8,128)S(1)}, f32[60,1024]{1,0:T(8,128)}, u32[]{:S(2)}) copy-start(f32[60,1024]{1,0:T(8,128)} %copy-done.3) | copy-start | bytes 737284 | tf_op jit(solution)/shard_map/while
  202.0 5.3 %copy-start.3 = (f32[60,1024]{1,0:T(8,128)}, f32[60,1024]{1,0:T(8,128)S(1)}, u32[]{:S(2)}) copy-start(f32[60,1024]{1,0:T(8,128)S(1)} %get-tuple-element.267) | copy-start | bytes 737284 | tf_op jit(solution)/shard_map/while
  207.9 3.7 %copy-start = (f32[1024,384]{1,0:T(8,128)S(1)}, f32[1024,384]{1,0:T(8,128)}, u32[]{:S(2)}) copy-start(f32[1024,384]{1,0:T(8,128)} %get-tuple-element.270) | copy-start | bytes 4718596 | tf_op jit(solution)/shard_map/while
  211.6 3.8 %copy-start.4 = (f32[60,1024]{1,0:T(8,128)S(1)}, f32[60,1024]{1,0:T(8,128)}, u32[]{:S(2)}) copy-start(f32[60,1024]{1,0:T(8,128)} %copy-done.3) | copy-start | bytes 737284 | tf_op jit(solution)/shard_map/while
  215.4 5.3 %copy-start.3 = (f32[60,1024]{1,0:T(8,128)}, f32[60,1024]{1,0:T(8,128)S(1)}, u32[]{:S(2)}) copy-start(f32[60,1024]{1,0:T(8,128)S(1)} %get-tuple-element.267) | copy-start | bytes 737284 | tf_op jit(solution)/shard_map/while
  221.3 3.7 %copy-start = (f32[1024,384]{1,0:T(8,128)S(1)}, f32[1024,384]{1,0:T(8,128)}, u32[]{:S(2)}) copy-start(f32[1024,384]{1,0:T(8,128)} %get-tuple-element.270) | copy-start | bytes 4718596 | tf_op jit(solution)/shard_map/while
  225.0 3.8 %copy-start.4 = (f32[60,1024]{1,0:T(8,128)S(1)}, f32[60,1024]{1,0:T(8,128)}, u32[]{:S(2)}) copy-start(f32[60,1024]{1,0:T(8,128)} %copy-done.3) | copy-start | bytes 737284 | tf_op jit(solution)/shard_map/while
  228.8 5.3 %copy-start.3 = (f32[60,1024]{1,0:T(8,128)}, f32[60,1024]{1,0:T(8,128)S(1)}, u32[]{:S(2)}) copy-start(f32[60,1024]{1,0:T(8,128)S(1)} %get-tuple-element.267) | copy-start | bytes 737284 | tf_op jit(solution)/shard_map/while
  234.7 3.7 %copy-start = (f32[1024,384]{1,0:T(8,128)S(1)}, f32[1024,384]{1,0:T(8,128)}, u32[]{:S(2)}) copy-start(f32[1024,384]{1,0:T(8,128)} %get-tuple-element.270) | copy-start | bytes 4718596 | tf_op jit(solution)/shard_map/while
  238.4 3.8 %copy-start.4 = (f32[60,1024]{1,0:T(8,128)S(1)}, f32[60,1024]{1,0:T(8,128)}, u32[]{:S(2)}) copy-start(f32[60,1024]{1,0:T(8,128)} %copy-done.3) | copy-start | bytes 737284 | tf_op jit(solution)/shard_map/while
  242.2 5.3 %copy-start.3 = (f32[60,1024]{1,0:T(8,128)}, f32[60,1024]{1,0:T(8,128)S(1)}, u32[]{:S(2)}) copy-start(f32[60,1024]{1,0:T(8,128)S(1)} %get-tuple-element.267) | copy-start | bytes 737284 | tf_op jit(solution)/shard_map/while
  248.1 3.7 %copy-start = (f32[1024,384]{1,0:T(8,128)S(1)}, f32[1024,384]{1,0:T(8,128)}, u32[]{:S(2)}) copy-start(f32[1024,384]{1,0:T(8,128)} %get-tuple-element.270) | copy-start | bytes 4718596 | tf_op jit(solution)/shard_map/while
  251.8 3.8 %copy-start.4 = (f32[60,1024]{1,0:T(8,128)S(1)}, f32[60,1024]{1,0:T(8,128)}, u32[]{:S(2)}) copy-start(f32[60,1024]{1,0:T(8,128)} %copy-done.3) | copy-start | bytes 737284 | tf_op jit(solution)/shard_map/while
  255.6 5.3 %copy-start.3 = (f32[60,1024]{1,0:T(8,128)}, f32[60,1024]{1,0:T(8,128)S(1)}, u32[]{:S(2)}) copy-start(f32[60,1024]{1,0:T(8,128)S(1)} %get-tuple-element.267) | copy-start | bytes 737284 | tf_op jit(solution)/shard_map/while
  261.5 3.7 %copy-start = (f32[1024,384]{1,0:T(8,128)S(1)}, f32[1024,384]{1,0:T(8,128)}, u32[]{:S(2)}) copy-start(f32[1024,384]{1,0:T(8,128)} %get-tuple-element.270) | copy-start | bytes 4718596 | tf_op jit(solution)/shard_map/while
  265.2 3.8 %copy-start.4 = (f32[60,1024]{1,0:T(8,128)S(1)}, f32[60,1024]{1,0:T(8,128)}, u32[]{:S(2)}) copy-start(f32[60,1024]{1,0:T(8,128)} %copy-done.3) | copy-start | bytes 737284 | tf_op jit(solution)/shard_map/while
  269.0 5.3 %copy-start.3 = (f32[60,1024]{1,0:T(8,128)}, f32[60,1024]{1,0:T(8,128)S(1)}, u32[]{:S(2)}) copy-start(f32[60,1024]{1,0:T(8,128)S(1)} %get-tuple-element.267) | copy-start | bytes 737284 | tf_op jit(solution)/shard_map/while
  274.9 3.7 %copy-start = (f32[1024,384]{1,0:T(8,128)S(1)}, f32[1024,384]{1,0:T(8,128)}, u32[]{:S(2)}) copy-start(f32[1024,384]{1,0:T(8,128)} %get-tuple-element.270) | copy-start | bytes 4718596 | tf_op jit(solution)/shard_map/while
  278.6 3.8 %copy-start.4 = (f32[60,1024]{1,0:T(8,128)S(1)}, f32[60,1024]{1,0:T(8,128)}, u32[]{:S(2)}) copy-start(f32[60,1024]{1,0:T(8,128)} %copy-done.3) | copy-start | bytes 737284 | tf_op jit(solution)/shard_map/while
Sparse Core Ops, SparseCore 0:
  43.4 52.6 all-gather.6
  98.6 76.5 all-gather.4
  282.6 31.4 reduce-scatter.1
where the time goes:
time: 325 us; the launch traced here: 321 us
  waiting for transfers between devices  126 us (39%)
  local copies, waits for them, and re-layouts  83.6 us (26%)
  matrix products  37.5 us (12%)
  other arithmetic  33.1 us (10%)
  blocking collectives  17.6 us (5%)
  between operations  13.3 us (4%)
  starting transfers between devices  7.81 us (2%)
    all_gather x1, waiting for transfers between devices, shards(): lax.all_gather(spectra, 'tmpl', axis=0, tiled=True)  79.1 us
    dynamic_slice x32, local copies, waits for them, and re-layouts, shards(): lax.map(per_segment, (lax.all_gather(spectra, 'tmpl', axis=0, tiled=True)...  39.9 us
    reduce_scatter x1, waiting for transfers between devices, shards(): lax.psum_scatter(partial_stack, 'chan', scatter_dimension=1, tiled=True)  31.6 us
    dot_general x8, matrix products, block_stack(): jnp.einsum('smf,ft->smt', product, inverse, precision=HIGH)  23.4 us
    all_to_all x1, blocking collectives, shards(): lax.all_to_all(ordered, 'chan', split_axis=0, concat_axis=1, tiled=True)  17.6 us
    gather x16, local copies, waits for them, and re-layouts, block_stack(): chosen = seg_spec[:, positions]  13.6 us
    gather x8, local copies, waits for them, and re-layouts, block_stack(): seg_energy[:, positions]  12 us
    all_gather x1, waiting for transfers between devices, shards(): lax.all_gather(energy, 'tmpl', axis=0, tiled=True)  11.2 us
  transfers between devices with their start and end apart: 5, of which 5 were waited for; matrix products, arithmetic and copies ran while one was open for 12% of the time, Pallas kernels for 0%

commit v1 on v0

v1 whole, which is shorter than its diff:
```python
import jax
import jax.numpy as jnp
import ml_dtypes
import numpy as np
from jax import lax
from jax.experimental import pallas as pl
from jax.experimental.pallas import tpu as pltpu
from jax.sharding import PartitionSpec as P

SLOTS = 30
TAPS = 600
BLOCK = 8
LANES = 256
USED = SLOTS * BLOCK
HALF = 512
HOP = 384
GROUP = 128

F32 = jnp.float32
BF16 = jnp.bfloat16


def split_np(table):
    hi = table.astype(ml_dtypes.bfloat16)
    lo = (table - hi.astype(np.float64)).astype(ml_dtypes.bfloat16)
    return hi, lo


def tables():
    n = np.arange(HALF, dtype=np.int64)
    m = np.arange(HALF // 2, dtype=np.int64)
    even = (m[:, None] * n[None, :] % HALF) * (2 * np.pi / HALF)
    odd = ((2 * m[:, None] + 1) * n[None, :] % (2 * HALF)) * (np.pi / HALF)
    even_imag = -np.sin(even)
    even_imag[0] = 1.0 - 2.0 * (n % 2)
    f_even = np.concatenate([np.cos(even), even_imag])
    f_odd = np.concatenate([np.cos(odd), -np.sin(odd)])
    weight = np.full((HALF // 2, 1), 2.0 / HALF)
    weight[0] = 1.0 / HALF
    weight = np.concatenate([weight, weight])
    inv_even = 0.5 * weight * f_even
    inv_odd = (1.0 / HALF) * f_odd
    inverse = np.concatenate([inv_even, inv_odd])[:, :HOP].T
    out = []
    for table in (f_even, f_odd, inverse):
        hi, lo = split_np(table)
        out.append(np.concatenate([hi, hi, lo], axis=1))
    return out


def split(value):
    hi = value.astype(BF16)
    lo = (value - hi.astype(F32)).astype(BF16)
    return hi, lo


def dot3(table_ref, value):
    hi, lo = split(value)
    return jnp.dot(table_ref[...], jnp.concatenate([hi, lo, hi], axis=0), preferred_element_type=F32)


def template_kernel(waves_ref, f_even_ref, f_odd_ref, er_ref, ei_ref, en_ref, odd_ref, pad_ref):
    pad_ref[...] = jnp.zeros_like(pad_ref)
    pad_ref[:USED, :TAPS] = waves_ref[...]
    waves = pad_ref[...].T
    mean = jnp.sum(waves * waves, axis=0, keepdims=True) * (1.0 / TAPS)
    scale = 1.0 / (jnp.sqrt(mean + 1e-6) * np.float32(np.sqrt(TAPS * SLOTS)))
    waves = waves * scale
    head, tail = waves[:HALF], waves[HALF:]
    tail = jnp.concatenate([tail, jnp.zeros((HALF - tail.shape[0], LANES), F32)], axis=0)
    even = dot3(f_even_ref, head + tail)
    odd_ref[...] = dot3(f_odd_ref, head - tail)
    real, imag = even[: HALF // 2], even[HALF // 2 :]
    first = lax.broadcasted_iota(jnp.int32, real.shape, 0) == 0
    er_ref[...] = real
    ei_ref[...] = jnp.where(first, 0.0, imag)
    en_ref[...] = jnp.where(first, imag, real)


def lane_pick(source, index):
    return jnp.take_along_axis(source, index, axis=1)


def select_kernel(record_ref, order_ref, group_ref, place_ref, out_ref, chan_ref):
    groups = order_ref.shape[0]
    blocks = group_ref.shape[0]
    span = record_ref.shape[0]
    for row in range(0, blocks, 8):
        for col in range(0, LANES, GROUP):
            group = group_ref[row : row + 8, col : col + GROUP]
            place = place_ref[row : row + 8, col : col + GROUP]
            chan = jnp.zeros_like(place)
            for g in range(groups):
                names = jnp.broadcast_to(order_ref[g : g + 1, :], (8, GROUP))
                chan = jnp.where(group == g, lane_pick(names, place), chan)
            for i in range(8):
                one = jnp.broadcast_to(chan[i : i + 1], (8, GROUP))
                chan_ref[row + i, :, col : col + GROUP] = one

    def one_block(block, _):
        for col in range(0, LANES, GROUP):
            chan = chan_ref[block, :, col : col + GROUP]
            high = lax.shift_right_logical(chan, 7)
            low = jnp.bitwise_and(chan, GROUP - 1)
            for row in range(0, span, 8):
                acc = jnp.zeros((8, GROUP), F32)
                for g in range(groups):
                    picked = lane_pick(record_ref[row : row + 8, g * GROUP : (g + 1) * GROUP], low)
                    acc = jnp.where(high == g, picked, acc)
                out_ref[block, row : row + 8, col : col + GROUP] = acc
        return 0

    lax.fori_loop(0, blocks, one_block, 0)


def source_of(block):
    lane, z = divmod(block, 8)
    return lane * 8 + (z % 4) * 2 + z // 4


def halo_kernel(recv_ref, halo_ref):
    span = recv_ref.shape[1]
    rows = halo_ref.shape[0]
    for block in range(-(-rows // span)):
        count = min(span, rows - block * span)
        halo_ref[block * span : block * span + count, :] = recv_ref[source_of(block), :count, :]


def segments(x_ref, sq_ref, first, count, specs, f_even_ref, f_odd_ref, inv_ref, out_ref):
    er_ref, ei_ref, en_ref, odd_ref = specs
    quarter = HALF // 2
    lags = count * HOP
    rows = lags + TAPS
    sq = x_ref[:rows] * x_ref[:rows]
    for step in (1, 2, 4):
        sq_ref[:rows] = sq
        sq_ref[rows : rows + 8] = jnp.zeros((8, LANES), F32)
        sq = sq_ref[:rows] + sq_ref[step : rows + step]
    total = sq[74 * 8 : 74 * 8 + lags]
    length = 1
    have = rows
    at = {64: 0, 8: 64, 2: 72}
    while length < 64:
        have = have - 8 * length
        sq = sq[:have] + sq[8 * length : 8 * length + have]
        length *= 2
        if length in at:
            total = total + sq[8 * at[length] : 8 * at[length] + lags]
    scale = lax.rsqrt(total * (1.0 / TAPS) + 1e-6)
    for seg in range(count):
        base = seg * HOP
        head, tail = x_ref[base : base + HALF], x_ref[base + HALF : base + 2 * HALF]
        even = dot3(f_even_ref, head + tail)
        odd = dot3(f_odd_ref, head - tail)
        re, im = even[:quarter], even[quarter:]
        ro, io = odd[:quarter], odd[quarter:]
        tr, ti, tn = er_ref[...], ei_ref[...], en_ref[...]
        to, tp = odd_ref[:quarter], odd_ref[quarter:]
        product = jnp.concatenate(
            [re * tr + im * ti, im * tn - re * ti, ro * to + io * tp, io * to - ro * tp], axis=0
        )
        corr = dot3(inv_ref, product) * scale[base : base + HOP]
        folded = (corr[:, :GROUP] + corr[:, GROUP:]).T
        acc = folded[:BLOCK]
        for s in range(1, GROUP // BLOCK):
            acc = acc + folded[s * BLOCK : (s + 1) * BLOCK]
        out_ref[:, (first + seg) * HOP : (first + seg + 1) * HOP] = acc


def near_kernel(recv_ref, er, ei, en, od, fe, fo, inv, out_ref, x_ref, sq_ref):
    span = recv_ref.shape[1]
    for block in range(x_ref.shape[0] // span):
        x_ref[block * span : (block + 1) * span, :] = recv_ref[source_of(block)]
    out_ref[...] = jnp.zeros_like(out_ref)
    segments(x_ref, sq_ref, 0, 2, (er, ei, en, od), fe, fo, inv, out_ref)


def far_kernel(near_ref, recv_ref, halo_ref, er, ei, en, od, fe, fo, inv, out_ref, x_ref, sq_ref):
    span = recv_ref.shape[1]
    start = 2 * HOP
    blocks = recv_ref.shape[0]
    skip = start // span
    for block in range(skip, blocks):
        x_ref[(block - skip) * span : (block - skip + 1) * span, :] = recv_ref[source_of(block)]
    here = (blocks - skip) * span
    rows = halo_ref.shape[0]
    x_ref[here : here + rows, :] = halo_ref[...]
    x_ref[here + rows :, :] = jnp.zeros((x_ref.shape[0] - here - rows, LANES), F32)
    out_ref[:, :start] = near_ref[:, :start]
    segments(x_ref, sq_ref, 2, 2, (er, ei, en, od), fe, fo, inv, out_ref)


def call(kernel, out_shape, scratch, flops, nbytes, mib, name):
    return pl.pallas_call(
        kernel,
        out_shape=out_shape,
        scratch_shapes=scratch,
        compiler_params=pltpu.CompilerParams(vmem_limit_bytes=mib << 20),
        cost_estimate=pl.CostEstimate(flops=flops, bytes_accessed=nbytes, transcendentals=0),
        name=name,
    )


def by_block(slots, blocks):
    slots = slots.reshape(blocks, BLOCK, SLOTS).transpose(0, 2, 1).reshape(blocks, USED)
    return jnp.pad(slots, ((0, 0), (0, LANES - USED)))


def shards(record, channel_order, templates, group_of_slot, place_of_slot):
    blocks = lax.axis_size("tmpl")
    planes = lax.axis_size("chan")
    span = record.shape[1]
    lags = blocks * span
    f_even, f_odd, inverse = (jnp.asarray(t) for t in tables())
    moves = []
    for b in range(blocks):
        for z in range(planes):
            plane, lane = divmod(b, blocks // planes)
            moves.append((b * planes + z, source_of(lane * 8 + z) * planes + plane))
    raw = lax.ppermute(record.T, ("tmpl", "chan"), moves)

    waves = templates.transpose(1, 0, 2).reshape(USED, TAPS)
    quarter = jax.ShapeDtypeStruct((HALF // 2, LANES), F32)
    specs = call(
        template_kernel,
        (quarter, quarter, quarter, jax.ShapeDtypeStruct((HALF, LANES), F32)),
        [pltpu.VMEM((LANES, 640), F32)],
        2 * 3 * HALF * 2 * HALF * LANES,
        6 << 20,
        48,
        "template_spectra",
    )(waves, f_even, f_odd)

    sent = call(
        select_kernel,
        jax.ShapeDtypeStruct((blocks, span, LANES), F32),
        [pltpu.VMEM((blocks, 8, LANES), jnp.int32)],
        1 << 20,
        4 << 20,
        48,
        "select_channels",
    )(
        raw,
        channel_order.reshape(-1, GROUP),
        by_block(group_of_slot, blocks),
        by_block(place_of_slot, blocks),
    )
    recv = lax.all_to_all(sent, "tmpl", split_axis=0, concat_axis=0, tiled=True)
    head = call(
        halo_kernel, jax.ShapeDtypeStruct((TAPS, LANES), F32), [], 0, 1 << 20, 48, "halo"
    )(recv)
    halo = lax.ppermute(head, "chan", [((z + 1) % planes, z) for z in range(planes)])
    out = jax.ShapeDtypeStruct((BLOCK, lags), F32)
    scratch = [pltpu.VMEM((1536, LANES), F32), pltpu.VMEM((1536, LANES), F32)]
    flops = 2 * 2 * 3 * (2 * HALF * HALF + HOP * 2 * HALF) * LANES
    near = call(near_kernel, out, scratch, flops, 6 << 20, 56, "near_segments")(
        recv, *specs, f_even, f_odd, inverse
    )
    return call(far_kernel, out, scratch, flops, 6 << 20, 56, "far_segments")(
        near, recv, halo, *specs, f_even, f_odd, inverse
    )


def solution(mesh):
    placed = (P(None, ("tmpl", "chan")), P(), P("tmpl", None, None), P(), P())
    return jax.shard_map(
        shards, mesh=mesh, in_specs=placed, out_specs=P("tmpl", "chan"), check_vma=False
    )
```

time: 325 us -> 91.4 us (0.28); the launches traced: 321 us -> 91 us
  waiting for transfers between devices: 126 us -> 8.87 us
  local copies, waits for them, and re-layouts: 83.6 us -> 6.66 us
  matrix products: 37.5 us -> 0 us
  other arithmetic: 33.1 us -> 0 us
  Pallas kernels: 0 us -> 25.4 us
  blocking collectives: 17.6 us -> 42.4 us
  between operations: 13.3 us -> 0.08 us
    all_gather x2 -> x0, waiting for transfers between devices: 90.3 us -> none  [the longest x1 79.1 us: shards(): lax.all_gather(spectra, 'tmpl', axis=0, tiled=True)]
    dynamic_slice x33 -> x0, local copies, waits for them, and re-layouts: 39.9 us -> none  [the longest x32 39.9 us: shards(): lax.map(per_segment, (lax.all_gather(spectra, 'tmpl', axis=0, tiled=True)...]
    dot_general x19 -> x0, matrix products: 37.5 us -> none  [the longest x8 23.4 us: block_stack(): jnp.einsum('smf,ft->smt', product, inverse, precision=HIGH)]
    reduce_scatter x1 -> x0, waiting for transfers between devices: 31.6 us -> none  [shards(): lax.psum_scatter(partial_stack, 'chan', scatter_dimension=1, tiled=True)]
    gather x28 -> x0, local copies, waits for them, and re-layouts: 30.7 us -> none  [the longest x16 13.6 us: block_stack(): chosen = seg_spec[:, positions]]
    pallas_call x0 -> x5, Pallas kernels: none -> 25.4 us  [the longest x1 9.15 us: shards(): call(far_kernel, out, scratch, flops, 6 << 20, 56, 'far_segments')]
    all_to_all x1, blocking collectives: 17.6 us -> 42.4 us  [shards(): recv = lax.all_to_all(sent, 'tmpl', split_axis=0, concat_axis=0, tiled=True)]
    cos x1 -> x0, other arithmetic: 9.44 us -> none  [dft_tables(): jnp.cos(angles)]
  transfers between devices with their start and end apart: 5 -> 2, of which waited for: 5 -> 2; matrix products, arithmetic and copies ran while one was open for 12% -> 2% of each run, Pallas kernels for 0% -> 11%
where the time goes in v1:
time: 91.4 us; the launch traced here: 91 us
  blocking collectives  42.4 us (46%)
  Pallas kernels  25.4 us (28%)
  waiting for transfers between devices  8.87 us (10%)
  starting transfers between devices  7.63 us (8%)
  local copies, waits for them, and re-layouts  6.66 us (7%)
    all_to_all x1, blocking collectives, shards(): recv = lax.all_to_all(sent, 'tmpl', split_axis=0, concat_axis=0, tiled=True)  42.4 us
    pallas_call x1, Pallas kernels, shards(): call(far_kernel, out, scratch, flops, 6 << 20, 56, 'far_segments')  9.15 us
    pallas_call x1, Pallas kernels, shards(): call(near_kernel, out, scratch, flops, 6 << 20, 56, 'near_segments')  8.98 us
    ppermute x1, waiting for transfers between devices, shards(): raw = lax.ppermute(record.T, ('tmpl', 'chan'), moves)  8.6 us
    unnamed x22, local copies, waits for them, and re-layouts  6.22 us
    pallas_call x1, Pallas kernels, shards(): call(select_kernel, jax.ShapeDtypeStruct((blocks, span, LANES), F32), [pl...  5.88 us
    ppermute x1, starting transfers between devices, shards(): raw = lax.ppermute(record.T, ('tmpl', 'chan'), moves)  4.5 us
    ppermute x1, starting transfers between devices, shards(): lax.ppermute(head, 'chan', [((z + 1) % planes, z) for z in range(planes)])  3.13 us
  transfers between devices with their start and end apart: 2, of which 2 were waited for; matrix products, arithmetic and copies ran while one was open for 2% of the time, Pallas kernels for 11%

profile of v1, /device:TPU:1, one launch (start us, length us, event | category | flops | bytes accessed | tf_op | source)
XLA Modules:
  0.0 91.0 jit_solution(5894609591106123846)
XLA Ops:
  0.0 4.5 %collective-permute-start = (f32[48,1024]{1,0:T(8,128)}, f32[48,1024]{1,0:T(8,128)S(1)}, u32[]{:S(2)}, u32[]{:S(2)}) collective-permute-start(f32[48,1024]{1,0:T(8,128)} %bitcast.19), channel_id=1, source_target_pairs={{0,0},{1,16},{2,32},{3,48},{4,8},{5,24},{6,40},{7,56},{8,64},{9,80... | collective-permute-start | bytes 589832 | tf_op jit(solution)/shard_map/ppermute | solution.py:220
  4.5 0.9 copy.11
  5.4 0.1 copy.12
  5.5 0.1 copy.13
  5.6 0.9 copy.14
  6.5 0.1 copy.15
  6.6 0.1 copy.16
  6.7 8.6 %collective-permute-done.record_ref = f32[48,1024]{1,0:T(8,128)S(1)} collective-permute-done((f32[48,1024]{1,0:T(8,128)}, f32[48,1024]{1,0:T(8,128)S(1)}, u32[]{:S(2)}, u32[]{:S(2)}) %collective-permute-start) | collective-permute-done | bytes 196640 | tf_op jit(solution)/shard_map/ppermute | solution.py:220
  15.3 0.0 copy-start.4
  15.3 0.7 copy-done.4
  16.0 5.9 %select_channels.1 = f32[32,48,256]{2,1,0:T(8,128)S(1)} custom-call(f32[48,1024]{1,0:T(8,128)S(1)} %collective-permute-done.record_ref, s32[8,128]{1,0:T(8,128)S(1)} %bitcast.14, s32[32,256]{1,0:T(8,128)S(1)} %pad.7.group_ref, s32[32,256]{1,0:T(8,128)S(1)} %pad.8.place_ref), custom_call_target="tpu_custom_call" | custom-call | flops 1048576 | bytes 4194304 | tf_op jit(solution)/shard_map/select_channels/pallas_call | solution.py:234
  21.9 0.0 copy-start.2
  21.9 42.4 %all_to_all.5.recv_ref = f32[32,48,256]{2,1,0:T(8,128)S(1)} all-to-all(f32[32,48,256]{2,1,0:T(8,128)S(1)} %select_channels.1), channel_id=1, replica_groups=mesh['tmpl'=32,'chan'=8] {'tmpl'}, dimensions={0} | all-to-all | bytes 3145728 | tf_op jit(solution)/shard_map/all_to_all | solution.py:248
  64.3 0.0 copy-start
  64.3 0.0 copy-start.1
  64.3 0.0 copy-start.3
  64.4 3.1 %collective-permute-start.1 = (f32[600,256]{1,0:T(8,128)S(1)}, f32[600,256]{1,0:T(8,128)S(1)}, u32[]{:S(2)}, u32[]{:S(2)}) collective-permute-start(f32[600,256]{1,0:T(8,128)S(1)} %halo.1), channel_id=1, source_target_pairs={{1,0},{2,1},{3,2},{4,3},{5,4},{6,5},{7,6},{0,7},{9,8},{10,9},{11,1... | collective-permute-start | bytes 1843208 | tf_op jit(solution)/shard_map/ppermute | solution.py:252
  67.5 0.0 copy-done.2
  67.5 0.0 copy-done.1
  67.5 0.0 copy-done.3
  67.5 1.3 %template_spectra.1 = (f32[256,256]{1,0:T(8,128)S(1)}, f32[256,256]{1,0:T(8,128)S(1)}, f32[256,256]{1,0:T(8,128)S(1)}, f32[512,256]{1,0:T(8,128)S(1)}) custom-call(f32[240,600]{1,0:T(8,128)S(1)} %bitcast.13, bf16[512,1536]{1,0:T(8,128)(2,1)S(1)} %copy-done.2, bf16[512,1536]{1,0:T(8,128)(2,1)S(1)} %copy-done.1), custom_call_target="tpu_custom_call" | custom-call | flops 805306368 | bytes 6291456 | tf_op jit(solution)/shard_map/template_spectra/pallas_call | solution.py:224
  68.8 0.0 copy-done
  68.8 0.0 copy-start.5
  68.8 0.8 copy-done.5
  69.6 0.0 copy-start.6
  69.6 0.7 copy-done.6
  70.4 0.0 copy-start.7
  70.4 0.7 copy-done.7
  71.1 0.0 copy-start.8
  71.1 0.7 copy-done.8
  71.8 9.0 %near_segments.1.near_ref = f32[8,1536]{1,0:T(8,128)} custom-call(f32[32,48,256]{2,1,0:T(8,128)} %copy-done, f32[256,256]{1,0:T(8,128)} %copy-done.6, f32[256,256]{1,0:T(8,128)} %copy-done.7, f32[256,256]{1,0:T(8,128)} %copy-done.8, f32[512,256]{1,0:T(8,128)} %copy-done.5, bf16[512,1536]{1,0:T(8,128)(2,1)} %constant.8.clone.f_even_ref.fe, ...), custom_call_target="tpu_custom_call" | custom-call | flops 2818572288 | bytes 6291456 | tf_op jit(solution)/shard_map/near_segments/pallas_call | solution.py:256
  80.8 0.3 collective-permute-done.1.halo_ref
  81.0 0.0 copy-start.9
  81.0 0.8 copy-done.9
  81.9 9.1 %far_segments.1 = f32[8,1536]{1,0:T(8,128)} custom-call(f32[8,1536]{1,0:T(8,128)} %near_segments.1.near_ref, f32[32,48,256]{2,1,0:T(8,128)} %copy-done, f32[600,256]{1,0:T(8,128)} %copy-done.9, f32[256,256]{1,0:T(8,128)} %copy-done.6, f32[256,256]{1,0:T(8,128)} %copy-done.7, f32[256,256]{1,0:T(8,128)} %copy-done.8, f32[512,256]{1,0:T(8,128)} %copy-done.5, ...), custom_call_target="tpu_custom_call" | custom-call | flops 2818572288 | bytes 6291456 | tf_op jit(solution)/shard_map/far_segments/pallas_call | solution.py:259
  (3 shorter events, 0.1 us)
Async XLA Ops:
  0.0 15.3 %collective-permute-start = (f32[48,1024]{1,0:T(8,128)}, f32[48,1024]{1,0:T(8,128)S(1)}, u32[]{:S(2)}, u32[]{:S(2)}) collective-permute-start(f32[48,1024]{1,0:T(8,128)} %bitcast.19), channel_id=1, source_target_pairs={{0,0},{1,16},{2,32},{3,48},{4,8},{5,24},{6,40},{7,56},{8,64},{9,80... | collective-permute-start | bytes 589832 | tf_op jit(solution)/shard_map/ppermute | solution.py:220
  15.3 0.7 copy-start.4
  21.9 45.6 %copy-start.2 = (bf16[512,1536]{1,0:T(8,128)(2,1)S(1)}, bf16[512,1536]{1,0:T(8,128)(2,1)}, u32[]{:S(2)}) copy-start(bf16[512,1536]{1,0:T(8,128)(2,1)} %constant.8.clone.f_even_ref.fe) | copy-start | bytes 4718596
  64.3 4.5 %copy-start = (f32[32,48,256]{2,1,0:T(8,128)}, f32[32,48,256]{2,1,0:T(8,128)S(1)}, u32[]{:S(2)}) copy-start(f32[32,48,256]{2,1,0:T(8,128)S(1)} %all_to_all.5.recv_ref) | copy-start | bytes 4718596
  64.3 3.2 %copy-start.1 = (bf16[512,1536]{1,0:T(8,128)(2,1)S(1)}, bf16[512,1536]{1,0:T(8,128)(2,1)}, u32[]{:S(2)}) copy-start(bf16[512,1536]{1,0:T(8,128)(2,1)} %constant.9.clone.f_odd_ref.fo) | copy-start | bytes 4718596
  64.3 3.2 %copy-start.3 = (f32[8,30,600]{2,0,1:T(8,128)S(1)}, f32[8,30,600]{2,0,1:T(8,128)}, u32[]{:S(2)}) copy-start(f32[8,30,600]{2,0,1:T(8,128)} %param.10) | copy-start | bytes 1728004
  64.4 16.6 %collective-permute-start.1 = (f32[600,256]{1,0:T(8,128)S(1)}, f32[600,256]{1,0:T(8,128)S(1)}, u32[]{:S(2)}, u32[]{:S(2)}) collective-permute-start(f32[600,256]{1,0:T(8,128)S(1)} %halo.1), channel_id=1, source_target_pairs={{1,0},{2,1},{3,2},{4,3},{5,4},{6,5},{7,6},{0,7},{9,8},{10,9},{11,1... | collective-permute-start | bytes 1843208 | tf_op jit(solution)/shard_map/ppermute | solution.py:252
  68.8 0.8 copy-start.5
  69.6 0.7 copy-start.6
  70.4 0.7 copy-start.7
  71.1 0.7 copy-start.8
  81.0 0.8 copy-start.9

commit v2 on v1

--- a/solution.py
+++ b/solution.py
@@ -15,6 +15,8 @@
 HALF = 512
 HOP = 384
 GROUP = 128
+BACK = 304
+NEXT = 296
 
 F32 = jnp.float32
 BF16 = jnp.bfloat16
@@ -113,20 +115,31 @@
     lax.fori_loop(0, blocks, one_block, 0)
 
 
-def source_of(block):
-    lane, z = divmod(block, 8)
-    return lane * 8 + (z % 4) * 2 + z // 4
-
-
-def halo_kernel(recv_ref, halo_ref):
+def route(block, plane):
+    low, core, z = block // 16, block // 8 % 2, block % 8
+    key = z ^ (5 * core)
+    return (plane ^ key) * 4 + (low ^ (key & 1)) * 2 + core
+
+
+def load_rows(recv_ref, plane, x_ref, first, count, at):
     span = recv_ref.shape[1]
-    rows = halo_ref.shape[0]
-    for block in range(-(-rows // span)):
-        count = min(span, rows - block * span)
-        halo_ref[block * span : block * span + count, :] = recv_ref[source_of(block), :count, :]
-
-
-def segments(x_ref, sq_ref, first, count, specs, f_even_ref, f_odd_ref, inv_ref, out_ref):
+    row = first
+    while row < first + count:
+        block, low = divmod(row, span)
+        take = min(span - low, first + count - row)
+        x_ref[at : at + take, :] = recv_ref[route(block, plane), low : low + take, :]
+        row += take
+        at += take
+
+
+def ends_kernel(plane_ref, recv_ref, head_ref, tail_ref):
+    plane = plane_ref[0]
+    total = recv_ref.shape[0] * recv_ref.shape[1]
+    load_rows(recv_ref, plane, head_ref, 0, NEXT, 0)
+    load_rows(recv_ref, plane, tail_ref, total - BACK, BACK, 0)
+
+
+def segments(x_ref, sq_ref, count, specs, f_even_ref, f_odd_ref, inv_ref):
     er_ref, ei_ref, en_ref, odd_ref = specs
     quarter = HALF // 2
     lags = count * HOP
@@ -147,6 +160,7 @@
         if length in at:
             total = total + sq[8 * at[length] : 8 * at[length] + lags]
     scale = lax.rsqrt(total * (1.0 / TAPS) + 1e-6)
+    stacks = []
     for seg in range(count):
         base = seg * HOP
         head, tail = x_ref[base : base + HALF], x_ref[base + HALF : base + 2 * HALF]
@@ -164,41 +178,48 @@
         acc = folded[:BLOCK]
         for s in range(1, GROUP // BLOCK):
             acc = acc + folded[s * BLOCK : (s + 1) * BLOCK]
-        out_ref[:, (first + seg) * HOP : (first + seg + 1) * HOP] = acc
-
-
-def near_kernel(recv_ref, er, ei, en, od, fe, fo, inv, out_ref, x_ref, sq_ref):
-    span = recv_ref.shape[1]
-    for block in range(x_ref.shape[0] // span):
-        x_ref[block * span : (block + 1) * span, :] = recv_ref[source_of(block)]
-    out_ref[...] = jnp.zeros_like(out_ref)
-    segments(x_ref, sq_ref, 0, 2, (er, ei, en, od), fe, fo, inv, out_ref)
-
-
-def far_kernel(near_ref, recv_ref, halo_ref, er, ei, en, od, fe, fo, inv, out_ref, x_ref, sq_ref):
-    span = recv_ref.shape[1]
-    start = 2 * HOP
-    blocks = recv_ref.shape[0]
-    skip = start // span
-    for block in range(skip, blocks):
-        x_ref[(block - skip) * span : (block - skip + 1) * span, :] = recv_ref[source_of(block)]
-    here = (blocks - skip) * span
-    rows = halo_ref.shape[0]
-    x_ref[here : here + rows, :] = halo_ref[...]
-    x_ref[here + rows :, :] = jnp.zeros((x_ref.shape[0] - here - rows, LANES), F32)
-    out_ref[:, :start] = near_ref[:, :start]
-    segments(x_ref, sq_ref, 2, 2, (er, ei, en, od), fe, fo, inv, out_ref)
-
-
-def call(kernel, out_shape, scratch, flops, nbytes, mib, name):
-    return pl.pallas_call(
-        kernel,
-        out_shape=out_shape,
-        scratch_shapes=scratch,
-        compiler_params=pltpu.CompilerParams(vmem_limit_bytes=mib << 20),
-        cost_estimate=pl.CostEstimate(flops=flops, bytes_accessed=nbytes, transcendentals=0),
-        name=name,
-    )
+        stacks.append(acc)
+    return stacks
+
+
+def near_kernel(plane_ref, recv_ref, er, ei, en, od, fe, fo, inv, out_ref, x_ref, sq_ref):
+    load_rows(recv_ref, plane_ref[0], x_ref, HOP - BACK, HOP + 2 * HALF, 0)
+    one, two = segments(x_ref, sq_ref, 2, (er, ei, en, od), fe, fo, inv)
+    out_ref[:, :HOP] = one
+    out_ref[:, HOP:] = two
+
+
+def back_kernel(plane_ref, recv_ref, tail_ref, er, ei, en, od, fe, fo, inv, out_ref, x_ref, sq_ref):
+    x_ref[:BACK] = tail_ref[...]
+    load_rows(recv_ref, plane_ref[0], x_ref, 0, 2 * HALF - BACK, BACK)
+    (out_ref[...],) = segments(x_ref, sq_ref, 1, (er, ei, en, od), fe, fo, inv)
+
+
+def last_kernel(plane_ref, recv_ref, head_ref, er, ei, en, od, fe, fo, inv, out_ref, x_ref, sq_ref):
+    total = recv_ref.shape[0] * recv_ref.shape[1]
+    first = 3 * HOP - BACK
+    own = total - first
+    load_rows(recv_ref, plane_ref[0], x_ref, first, own, 0)
+    x_ref[own : own + NEXT] = head_ref[...]
+    x_ref[own + NEXT : 2 * HALF] = jnp.zeros((2 * HALF - own - NEXT, LANES), F32)
+    (out_ref[...],) = segments(x_ref, sq_ref, 1, (er, ei, en, od), fe, fo, inv)
+
+
+def call(kernel, out_shape, scratch, flops, nbytes, mib, name, scalars=0):
+    def run(*operands):
+        smem = pl.BlockSpec(memory_space=pltpu.SMEM)
+        vmem = pl.BlockSpec(memory_space=pltpu.VMEM)
+        return pl.pallas_call(
+            kernel,
+            out_shape=out_shape,
+            in_specs=[smem if i < scalars else vmem for i in range(len(operands))],
+            scratch_shapes=scratch,
+            compiler_params=pltpu.CompilerParams(vmem_limit_bytes=mib << 20),
+            cost_estimate=pl.CostEstimate(flops=flops, bytes_accessed=nbytes, transcendentals=0),
+            name=name,
+        )(*operands)
+
+    return run
 
 
 def by_block(slots, blocks):
@@ -212,12 +233,17 @@
     span = record.shape[1]
     lags = blocks * span
     f_even, f_odd, inverse = (jnp.asarray(t) for t in tables())
-    moves = []
+    across, along = [], []
+    per_plane = blocks // planes
     for b in range(blocks):
         for z in range(planes):
-            plane, lane = divmod(b, blocks // planes)
-            moves.append((b * planes + z, source_of(lane * 8 + z) * planes + plane))
-    raw = lax.ppermute(record.T, ("tmpl", "chan"), moves)
+            plane, lane = divmod(b, per_plane)
+            keeper = route(lane * planes + z, plane)
+            across.append((b * planes + z, keeper * planes + z))
+            along.append((keeper * planes + z, keeper * planes + plane))
+    raw = lax.ppermute(record.T, ("tmpl", "chan"), across)
+    raw = lax.ppermute(raw, ("tmpl", "chan"), along)
+    plane = lax.axis_index("chan").astype(jnp.int32).reshape(1)
 
     waves = templates.transpose(1, 0, 2).reshape(USED, TAPS)
     quarter = jax.ShapeDtypeStruct((HALF // 2, LANES), F32)
@@ -227,38 +253,42 @@
         [pltpu.VMEM((LANES, 640), F32)],
         2 * 3 * HALF * 2 * HALF * LANES,
         6 << 20,
-        48,
+        16,
         "template_spectra",
     )(waves, f_even, f_odd)
 
+    group, place, plane, specs = lax.optimization_barrier(
+        (by_block(group_of_slot, blocks), by_block(place_of_slot, blocks), plane, specs)
+    )
     sent = call(
         select_kernel,
         jax.ShapeDtypeStruct((blocks, span, LANES), F32),
         [pltpu.VMEM((blocks, 8, LANES), jnp.int32)],
         1 << 20,
         4 << 20,
-        48,
+        8,
         "select_channels",
-    )(
-        raw,
-        channel_order.reshape(-1, GROUP),
-        by_block(group_of_slot, blocks),
-        by_block(place_of_slot, blocks),
-    )
+    )(raw, channel_order.reshape(-1, GROUP), group, place)
     recv = lax.all_to_all(sent, "tmpl", split_axis=0, concat_axis=0, tiled=True)
-    head = call(
-        halo_kernel, jax.ShapeDtypeStruct((TAPS, LANES), F32), [], 0, 1 << 20, 48, "halo"
-    )(recv)
-    halo = lax.ppermute(head, "chan", [((z + 1) % planes, z) for z in range(planes)])
-    out = jax.ShapeDtypeStruct((BLOCK, lags), F32)
-    scratch = [pltpu.VMEM((1536, LANES), F32), pltpu.VMEM((1536, LANES), F32)]
-    flops = 2 * 2 * 3 * (2 * HALF * HALF + HOP * 2 * HALF) * LANES
-    near = call(near_kernel, out, scratch, flops, 6 << 20, 56, "near_segments")(
-        recv, *specs, f_even, f_odd, inverse
-    )
-    return call(far_kernel, out, scratch, flops, 6 << 20, 56, "far_segments")(
-        near, recv, halo, *specs, f_even, f_odd, inverse
-    )
+    rows = jax.ShapeDtypeStruct((BACK, LANES), F32), jax.ShapeDtypeStruct((NEXT, LANES), F32)
+    head, tail = call(ends_kernel, rows[::-1], [], 0, 1 << 20, 8, "ends", 1)(plane, recv)
+    up = [(z, (z + 1) % planes) for z in range(planes)]
+    down = [(t, s) for s, t in up]
+    after = lax.ppermute(head, "chan", down)
+    before = lax.ppermute(tail, "chan", up)
+    flops = 2 * 3 * (2 * HALF * HALF + HOP * 2 * HALF) * LANES
+    shared = (*specs, f_even, f_odd, inverse)
+
+    def part(kernel, count, name):
+        lines = pltpu.VMEM(((count - 1) * HOP + 2 * HALF + 8, LANES), F32)
+        shape = jax.ShapeDtypeStruct((BLOCK, count * HOP), F32)
+        return call(kernel, shape, [lines, lines], count * flops, 8 << 20, 24, name, 1)
+
+    middle = part(near_kernel, 2, "near_segments")(plane, recv, *shared)
+    first = part(back_kernel, 1, "back_segment")(plane, recv, before, *shared)
+    given = lax.ppermute(first[:, :BACK], "chan", down)
+    last = part(last_kernel, 1, "last_segment")(plane, recv, after, *shared)
+    return jnp.concatenate([first[:, BACK:], middle, last, given], axis=1)
 
 
 def solution(mesh):

time: 91.4 us -> 81.8 us (0.89)
  Pallas kernels: 25.4 us -> 18.8 us
  blocking collectives: 42.4 us -> 36.9 us
  starting transfers between devices: 7.63 us -> 12.8 us
  waiting for transfers between devices: 8.87 us -> 7.07 us
    pallas_call x5 -> x6, Pallas kernels: 25.4 us -> 18.8 us  [run(): pl.pallas_call(kernel, out_shape=out_shape, in_specs=[smem if i < scalars...]
    all_to_all x1, blocking collectives: 42.4 us -> 36.9 us  [shards(): recv = lax.all_to_all(sent, 'tmpl', split_axis=0, concat_axis=0, tiled=True)]
    ppermute x2 -> x5, starting transfers between devices: 7.63 us -> 12.8 us  [the longest x1 8.05 us: shards(): raw = lax.ppermute(record.T, ('tmpl', 'chan'), across)]
    ppermute x2 -> x5, waiting for transfers between devices: 8.87 us -> 7.07 us  [the longest x1 3.25 us: shards(): raw = lax.ppermute(record.T, ('tmpl', 'chan'), across)]
    unnamed x22 -> x16, local copies, waits for them, and re-layouts: 6.22 us -> 4.57 us
  transfers between devices with their start and end apart: 2 -> 5, of which waited for: 2 -> 3; matrix products, arithmetic and copies ran while one was open for 2% -> 3% of each run, Pallas kernels for 11% -> 16%
where the time goes in v2:
time: 81.8 us; the launch traced here: 81.5 us
  blocking collectives  36.9 us (45%)
  Pallas kernels  18.8 us (23%)
  starting transfers between devices  12.8 us (16%)
  waiting for transfers between devices  7.07 us (9%)
  local copies, waits for them, and re-layouts  5.79 us (7%)
    all_to_all x1, blocking collectives, shards(): recv = lax.all_to_all(sent, 'tmpl', split_axis=0, concat_axis=0, tiled=True)  36.9 us
    pallas_call x6, Pallas kernels, run(): pl.pallas_call(kernel, out_shape=out_shape, in_specs=[smem if i < scalars...  18.8 us
    ppermute x1, starting transfers between devices, shards(): raw = lax.ppermute(record.T, ('tmpl', 'chan'), across)  8.05 us
    unnamed x16, local copies, waits for them, and re-layouts  4.57 us
    ppermute x1, waiting for transfers between devices, shards(): raw = lax.ppermute(record.T, ('tmpl', 'chan'), across)  3.25 us
    ppermute x1, starting transfers between devices, shards(): after = lax.ppermute(head, 'chan', down)  2.66 us
    ppermute x1, waiting for transfers between devices, shards(): before = lax.ppermute(tail, 'chan', up)  2.57 us
    ppermute x1, starting transfers between devices, shards(): raw = lax.ppermute(raw, ('tmpl', 'chan'), along)  1.91 us
  transfers between devices with their start and end apart: 5, of which 3 were waited for; matrix products, arithmetic and copies ran while one was open for 3% of the time, Pallas kernels for 16%

profile of v2, /device:TPU:1, one launch (start us, length us, event | category | flops | bytes accessed | tf_op | source)
XLA Modules:
  0.0 81.5 jit_solution(5375386669204199517)
XLA Ops:
  0.0 0.0 copy-start.5
  0.0 8.1 %collective-permute-start = (f32[48,1024]{1,0:T(8,128)}, f32[48,1024]{1,0:T(8,128)S(1)}, u32[]{:S(2)}, u32[]{:S(2)}) collective-permute-start(f32[48,1024]{1,0:T(8,128)} %bitcast.22), channel_id=1, source_target_pairs={{0,0},{1,49},{2,66},{3,115},{4,132},{5,181},{6,198},{7,247},{8,184... | collective-permute-start | bytes 589832 | tf_op jit(solution)/shard_map/ppermute | solution.py:244
  8.1 3.3 %collective-permute-done = f32[48,1024]{1,0:T(8,128)S(1)} collective-permute-done((f32[48,1024]{1,0:T(8,128)}, f32[48,1024]{1,0:T(8,128)S(1)}, u32[]{:S(2)}, u32[]{:S(2)}) %collective-permute-start) | collective-permute-done | bytes 196640 | tf_op jit(solution)/shard_map/ppermute | solution.py:244
  11.3 1.9 %collective-permute-start.1 = (f32[48,1024]{1,0:T(8,128)S(1)}, f32[48,1024]{1,0:T(8,128)S(1)}, u32[]{:S(2)}, u32[]{:S(2)}) collective-permute-start(f32[48,1024]{1,0:T(8,128)S(1)} %collective-permute-done), channel_id=1, source_target_pairs={{0,0},{49,48},{66,64},{115,112},{132,128},{181,176},{198,192},{247... | collective-permute-start | bytes 589832 | tf_op jit(solution)/shard_map/ppermute | solution.py:245
  13.2 0.9 %copy.11 = s32[256,30,1]{1,0,2:T(8,128)S(1)} copy(s32[256,30,1]{0,2,1:T(1,128)} %param.11) | data formatting | bytes 61440 | tf_op args[3]
  14.1 0.1 copy.12
  14.2 0.1 copy.13
  14.3 0.9 %copy.14 = s32[256,30]{1,0:T(8,128)S(1)} copy(s32[256,30]{0,1:T(8,128)} %param.12) | data formatting | bytes 61440 | tf_op args[4]
  15.2 0.1 copy.15
  15.3 0.1 copy.16
  15.4 0.0 copy-done.5
  15.5 0.0 copy-start
  15.5 1.4 %copy-done = bf16[512,1536]{1,0:T(8,128)(2,1)S(1)} copy-done((bf16[512,1536]{1,0:T(8,128)(2,1)S(1)}, bf16[512,1536]{1,0:T(8,128)(2,1)}, u32[]{:S(2)}) %copy-start) | copy-done | bytes 1572888
  16.9 0.0 copy-start.2
  16.9 1.4 %copy-done.2 = bf16[512,1536]{1,0:T(8,128)(2,1)S(1)} copy-done((bf16[512,1536]{1,0:T(8,128)(2,1)S(1)}, bf16[512,1536]{1,0:T(8,128)(2,1)}, u32[]{:S(2)}) %copy-start.2) | copy-done | bytes 1572888
  18.3 0.0 copy-start.6
  18.3 1.3 %template_spectra.1 = (f32[256,256]{1,0:T(8,128)S(1)}, f32[256,256]{1,0:T(8,128)S(1)}, f32[256,256]{1,0:T(8,128)S(1)}, f32[512,256]{1,0:T(8,128)S(1)}) custom-call(f32[240,600]{1,0:T(8,128)S(1)} %bitcast.15, bf16[512,1536]{1,0:T(8,128)(2,1)S(1)} %copy-done.2, bf16[512,1536]{1,0:T(8,128)(2,1)S(1)} %copy-done), custom_call_target="tpu_custom_call" | custom-call | flops 805306368 | bytes 6291456 | tf_op jit(solution)/shard_map/template_spectra/pallas_call | solution.py:212
  19.6 1.2 %collective-permute-done.1.record_ref = f32[48,1024]{1,0:T(8,128)S(1)} collective-permute-done((f32[48,1024]{1,0:T(8,128)S(1)}, f32[48,1024]{1,0:T(8,128)S(1)}, u32[]{:S(2)}, u32[]{:S(2)}) %collective-permute-start.1) | collective-permute-done | bytes 196640 | tf_op jit(solution)/shard_map/ppermute | solution.py:245
  20.8 0.0 copy-done.6
  20.8 0.0 copy-start.4
  20.8 5.9 %select_channels.1 = f32[32,48,256]{2,1,0:T(8,128)S(1)} custom-call(f32[48,1024]{1,0:T(8,128)S(1)} %collective-permute-done.1.record_ref, s32[8,128]{1,0:T(8,128)S(1)} %bitcast.17, s32[32,256]{1,0:T(8,128)S(1)} %pad.7.group_ref, s32[32,256]{1,0:T(8,128)S(1)} %pad.8.place_ref), custom_call_target="tpu_custom_call" | custom-call | flops 1048576 | bytes 4194304 | tf_op jit(solution)/shard_map/select_channels/pallas_call | solution.py:212
  26.7 0.0 copy-start.3
  26.7 36.9 %all_to_all.5.recv_ref = f32[32,48,256]{2,1,0:T(8,128)S(1)} all-to-all(f32[32,48,256]{2,1,0:T(8,128)S(1)} %select_channels.1), channel_id=1, replica_groups=mesh['tmpl'=32,'chan'=8] {'tmpl'}, dimensions={0} | all-to-all | bytes 3145728 | tf_op jit(solution)/shard_map/all_to_all | solution.py:272
  63.6 0.0 copy-start.1
  63.7 0.1 collective-permute-start.2
  63.8 2.7 %collective-permute-start.3 = (f32[296,256]{1,0:T(8,128)S(1)}, f32[296,256]{1,0:T(8,128)S(1)}, u32[]{:S(2)}, u32[]{:S(2)}) collective-permute-start(f32[296,256]{1,0:T(8,128)S(1)} %get-tuple-element.30), channel_id=1, source_target_pairs={{1,0},{2,1},{3,2},{4,3},{5,4},{6,5},{7,6},{0,7},{9,8},{10,9},{11,1... | collective-permute-start | bytes 909320 | tf_op jit(solution)/shard_map/ppermute | solution.py:277
  66.4 0.0 copy-done.4
  66.4 0.0 copy-done.3
  66.4 0.0 copy-done.1
  66.4 5.1 %near_segments.1 = f32[8,768]{1,0:T(8,128)S(1)} custom-call(s32[1]{0:T(128)} %bitcast.6.plane_ref, f32[32,48,256]{2,1,0:T(8,128)S(1)} %all_to_all.5.recv_ref, f32[256,256]{1,0:T(8,128)S(1)} %get-tuple-element.26.er, f32[256,256]{1,0:T(8,128)S(1)} %get-tuple-element.27.ei, f32[256,256]{1,0:T(8,128)S(1)} %get-tuple-element.28.en, ...), custom_call_target="tpu_custom_call" | custom-call | flops 2818572288 | bytes 8388608 | tf_op jit(solution)/shard_map/near_segments/pallas_call | solution.py:212
  71.6 2.6 %collective-permute-done.2.tail_ref = f32[304,256]{1,0:T(8,128)S(1)} collective-permute-done((f32[304,256]{1,0:T(8,128)S(1)}, f32[304,256]{1,0:T(8,128)S(1)}, u32[]{:S(2)}, u32[]{:S(2)}) %collective-permute-start.2) | collective-permute-done | bytes 311328 | tf_op jit(solution)/shard_map/ppermute | solution.py:278
  74.1 3.2 %back_segment.1 = f32[8,384]{1,0:T(8,128)S(1)} custom-call(s32[1]{0:T(128)} %bitcast.6.plane_ref, f32[32,48,256]{2,1,0:T(8,128)S(1)} %all_to_all.5.recv_ref, f32[304,256]{1,0:T(8,128)S(1)} %collective-permute-done.2.tail_ref, f32[256,256]{1,0:T(8,128)S(1)} %get-tuple-element.26.er, f32[256,256]{1,0:T(8,128)S(1)} %get-tuple-element.27.ei, ...), custom_call_target="tpu_custom_call" | custom-call | flops 1409286144 | bytes 8388608 | tf_op jit(solution)/shard_map/back_segment/pallas_call | solution.py:212
  77.4 0.1 collective-permute-start.4
  77.5 0.0 collective-permute-done.3.head_ref
  77.5 3.2 %last_segment.1 = f32[8,384]{1,0:T(8,128)S(1)} custom-call(s32[1]{0:T(128)} %bitcast.6.plane_ref, f32[32,48,256]{2,1,0:T(8,128)S(1)} %all_to_all.5.recv_ref, f32[296,256]{1,0:T(8,128)S(1)} %collective-permute-done.3.head_ref, f32[256,256]{1,0:T(8,128)S(1)} %get-tuple-element.26.er, f32[256,256]{1,0:T(8,128)S(1)} %get-tuple-element.27.ei, ...), custom_call_target="tpu_custom_call" | custom-call | flops 1409286144 | bytes 8388608 | tf_op jit(solution)/shard_map/last_segment/pallas_call | solution.py:212
  80.7 0.1 slice.8
  80.8 0.0 collective-permute-done.4
  80.8 0.7 concatenate.3
  (3 shorter events, 0.1 us)
Async XLA Ops:
  0.0 15.4 %copy-start.5 = (f32[8,30,600]{2,0,1:T(8,128)S(1)}, f32[8,30,600]{2,0,1:T(8,128)}, u32[]{:S(2)}) copy-start(f32[8,30,600]{2,0,1:T(8,128)} %param.10) | copy-start | bytes 1728004
  0.0 11.3 %collective-permute-start = (f32[48,1024]{1,0:T(8,128)}, f32[48,1024]{1,0:T(8,128)S(1)}, u32[]{:S(2)}, u32[]{:S(2)}) collective-permute-start(f32[48,1024]{1,0:T(8,128)} %bitcast.22), channel_id=1, source_target_pairs={{0,0},{1,49},{2,66},{3,115},{4,132},{5,181},{6,198},{7,247},{8,184... | collective-permute-start | bytes 589832 | tf_op jit(solution)/shard_map/ppermute | solution.py:244
  11.3 9.5 %collective-permute-start.1 = (f32[48,1024]{1,0:T(8,128)S(1)}, f32[48,1024]{1,0:T(8,128)S(1)}, u32[]{:S(2)}, u32[]{:S(2)}) collective-permute-start(f32[48,1024]{1,0:T(8,128)S(1)} %collective-permute-done), channel_id=1, source_target_pairs={{0,0},{49,48},{66,64},{115,112},{132,128},{181,176},{198,192},{247... | collective-permute-start | bytes 589832 | tf_op jit(solution)/shard_map/ppermute | solution.py:245
  15.5 1.4 %copy-start = (bf16[512,1536]{1,0:T(8,128)(2,1)S(1)}, bf16[512,1536]{1,0:T(8,128)(2,1)}, u32[]{:S(2)}) copy-start(bf16[512,1536]{1,0:T(8,128)(2,1)} %constant.13.clone.f_odd_ref.fo) | copy-start | bytes 4718596
  16.9 1.4 %copy-start.2 = (bf16[512,1536]{1,0:T(8,128)(2,1)S(1)}, bf16[512,1536]{1,0:T(8,128)(2,1)}, u32[]{:S(2)}) copy-start(bf16[512,1536]{1,0:T(8,128)(2,1)} %constant.12.clone.f_even_ref.fe) | copy-start | bytes 4718596
  18.3 2.6 %copy-start.6 = (s32[1024]{0:T(1024)S(1)}, s32[1024]{0:T(1024)}, u32[]{:S(2)}) copy-start(s32[1024]{0:T(1024)} %param.9) | copy-start | bytes 12292
  20.8 45.6 %copy-start.4 = (bf16[384,3072]{1,0:T(8,128)(2,1)S(1)}, bf16[384,3072]{1,0:T(8,128)(2,1)}, u32[]{:S(2)}) copy-start(bf16[384,3072]{1,0:T(8,128)(2,1)} %constant.14.clone.inv) | copy-start | bytes 7077892
  26.7 39.7 %copy-start.3 = (bf16[512,1536]{1,0:T(8,128)(2,1)S(1)}, bf16[512,1536]{1,0:T(8,128)(2,1)}, u32[]{:S(2)}) copy-start(bf16[512,1536]{1,0:T(8,128)(2,1)} %constant.12.clone.f_even_ref.fe) | copy-start | bytes 4718596
  63.6 2.8 %copy-start.1 = (bf16[512,1536]{1,0:T(8,128)(2,1)S(1)}, bf16[512,1536]{1,0:T(8,128)(2,1)}, u32[]{:S(2)}) copy-start(bf16[512,1536]{1,0:T(8,128)(2,1)} %constant.13.clone.f_odd_ref.fo) | copy-start | bytes 4718596
  63.7 10.4 %collective-permute-start.2 = (f32[304,256]{1,0:T(8,128)S(1)}, f32[304,256]{1,0:T(8,128)S(1)}, u32[]{:S(2)}, u32[]{:S(2)}) collective-permute-start(f32[304,256]{1,0:T(8,128)S(1)} %get-tuple-element.25), channel_id=1, source_target_pairs={{0,1},{1,2},{2,3},{3,4},{4,5},{5,6},{6,7},{7,0},{8,9},{9,10},{10,1... | collective-permute-start | bytes 933896 | tf_op jit(solution)/shard_map/ppermute | solution.py:278
  63.8 13.7 %collective-permute-start.3 = (f32[296,256]{1,0:T(8,128)S(1)}, f32[296,256]{1,0:T(8,128)S(1)}, u32[]{:S(2)}, u32[]{:S(2)}) collective-permute-start(f32[296,256]{1,0:T(8,128)S(1)} %get-tuple-element.30), channel_id=1, source_target_pairs={{1,0},{2,1},{3,2},{4,3},{5,4},{6,5},{7,6},{0,7},{9,8},{10,9},{11,1... | collective-permute-start | bytes 909320 | tf_op jit(solution)/shard_map/ppermute | solution.py:277
  77.4 3.4 %collective-permute-start.4 = (f32[8,304]{1,0:T(8,128)S(1)}, f32[8,304]{1,0:T(8,128)S(1)}, u32[]{:S(2)}, u32[]{:S(2)}) collective-permute-start(f32[8,304]{1,0:T(8,128)S(1)} %bitcast.16), channel_id=1, source_target_pairs={{1,0},{2,1},{3,2},{4,3},{5,4},{6,5},{7,6},{0,7},{9,8},{10,9},{11,1... | collective-permute-start | bytes 29192 | tf_op jit(solution)/shard_map/ppermute | solution.py:289

commit v3 on v2

v3 whole, which is shorter than its diff:
```python
import jax
import jax.numpy as jnp
import ml_dtypes
import numpy as np
from jax import lax
from jax.experimental import pallas as pl
from jax.experimental.pallas import tpu as pltpu
from jax.sharding import PartitionSpec as P

SLOTS = 30
TAPS = 600
BLOCK = 8
LANES = 256
USED = SLOTS * BLOCK
HALF = 512
HOP = 384
MOST = 408
GROUP = 128
QUARTER = 256
ROOT = float(np.sqrt(2.0))
BACK = 232
KEEP = 128
NEXT = 368

F32 = jnp.float32
BF16 = jnp.bfloat16


def split_np(table):
    hi = table.astype(ml_dtypes.bfloat16)
    lo = (table - hi.astype(np.float64)).astype(ml_dtypes.bfloat16)
    return hi, lo


def tables():
    n = np.arange(QUARTER, dtype=np.int64)[None, :]
    m = np.arange(GROUP, dtype=np.int64)[:, None]
    forward, back = [], []
    for eighths in (0, 4, 1, 3):
        if eighths in (0, 4):
            angle = ((2 * m + eighths // 4) * n % (2 * QUARTER)) * (np.pi / QUARTER)
            imag = -np.sin(angle)
            weight = np.full((QUARTER, 1), 2.0 / QUARTER)
            if not eighths:
                imag[0] = 1.0 - 2.0 * (n[0] % 2)
                weight[0] = weight[GROUP] = 1.0 / QUARTER
            table = np.concatenate([np.cos(angle), imag])
            inverse = (weight * table).T
        else:
            angle = ((8 * m + eighths) * n % (8 * GROUP)) * (np.pi / (4 * GROUP))
            table = np.concatenate([np.cos(angle), -np.sin(angle)])
            sign = 1.0 if eighths == 1 else -1.0
            cos, sin = np.cos(angle[:, :GROUP]).T / GROUP, np.sin(angle[:, :GROUP]).T / GROUP
            root = np.sqrt(2.0)
            low = np.concatenate([cos + sign * sin, sign * cos - sin], axis=1)
            high = np.concatenate([-root * sin, -root * cos], axis=1)
            inverse = np.concatenate([low, high])
        forward.append(table)
        back.append(0.25 * inverse)
    out = []
    for stack in (forward, back):
        hi, lo = split_np(np.concatenate(stack))
        out.append(np.concatenate([hi, hi, lo], axis=1))
    return out


def split(value):
    hi = value.astype(BF16)
    lo = (value - hi.astype(F32)).astype(BF16)
    return hi, lo


def dot3(table_ref, part, value):
    hi, lo = split(value)
    both = jnp.concatenate([hi, lo, hi], axis=0)
    rows = table_ref[part * QUARTER : (part + 1) * QUARTER]
    return jnp.dot(rows, both, preferred_element_type=F32)


def transform(pieces, table_ref):
    one, two, three, four = pieces
    even, late = one + three, two + four
    odd, last = one - three, two - four
    third, fourth = last[:GROUP], last[GROUP:]
    plain = jnp.concatenate([odd[:GROUP] - third, odd[GROUP:] + fourth], axis=0)
    turned = ROOT * jnp.concatenate([fourth, -third], axis=0)
    residues = (even + late, even - late, plain - turned, plain + turned)
    return [dot3(table_ref, part, value) for part, value in enumerate(residues)]


def combine(parts):
    total, diff, left, right = parts
    plain = left + right
    turned = (left - right) * (1.0 / ROOT)
    third, fourth = turned[GROUP:], -turned[:GROUP]
    odd = jnp.concatenate([plain[:GROUP] + third, plain[GROUP:] - fourth], axis=0)
    last = jnp.concatenate([third, fourth], axis=0)
    return odd + (total + diff), last + (total - diff)


def name_channels(order_ref, group_ref, place_ref, high_ref, low_ref, names_ref):
    names_ref[...] = jnp.zeros_like(names_ref)
    names_ref[0, :SLOTS] = group_ref[...]
    names_ref[1, :SLOTS] = place_ref[...]
    blocks = high_ref.shape[0]
    width = blocks * BLOCK
    for row in range(0, blocks, 8):
        for col in range(0, width, GROUP):
            group = names_ref[0, row : row + 8, col : col + GROUP]
            place = names_ref[1, row : row + 8, col : col + GROUP]
            chan = jnp.zeros_like(place)
            for g in range(order_ref.shape[0]):
                names = jnp.broadcast_to(order_ref[g : g + 1, :], (8, GROUP))
                chan = jnp.where(group == g, lane_pick(names, place), chan)
            names_ref[0, row : row + 8, col : col + GROUP] = chan
    chan = names_ref[0]
    slot = lax.broadcasted_iota(jnp.int32, (blocks, LANES), 0)
    lane = lax.broadcasted_iota(jnp.int32, (blocks, LANES), 1)
    repeat = jnp.where(lax.shift_right_logical(lane, 3) == slot, 1.0, 0.0).astype(BF16)
    row = lax.broadcasted_iota(jnp.int32, (width, LANES), 0)
    lane = lax.broadcasted_iota(jnp.int32, (width, LANES), 1)
    own = jnp.bitwise_and(row, BLOCK - 1) == jnp.bitwise_and(lane, BLOCK - 1)
    for out_ref, part in (
        (high_ref, lax.shift_right_logical(chan, 8)),
        (low_ref, jnp.bitwise_and(chan, LANES - 1)),
    ):
        turned = part.astype(F32).T.astype(BF16)
        wide = jnp.dot(turned, repeat, preferred_element_type=F32)
        wide = jnp.where(own, wide, 0.0).reshape(blocks, BLOCK, LANES)
        out_ref[...] = jnp.sum(wide, axis=1).astype(jnp.int32)


def template_kernel(
    waves_ref, order_ref, group_ref, place_ref, table_ref, spec_ref, high_ref, low_ref, pad_ref, names_ref
):
    name_channels(order_ref, group_ref, place_ref, high_ref, low_ref, names_ref)
    pad_ref[...] = jnp.zeros_like(pad_ref)
    pad_ref[:USED, :TAPS] = waves_ref[...]
    waves = pad_ref[...].T
    mean = jnp.sum(waves * waves, axis=0, keepdims=True) * (1.0 / TAPS)
    scale = 1.0 / (jnp.sqrt(mean + 1e-6) * np.float32(np.sqrt(TAPS * SLOTS)))
    waves = waves * scale
    pieces = [waves[at : at + QUARTER] for at in range(0, 4 * QUARTER, QUARTER)]
    total, *rest = transform(pieces, table_ref)
    for part, spec in enumerate(rest):
        spec_ref[part * QUARTER : (part + 1) * QUARTER] = spec
    real, imag = total[:GROUP], total[GROUP:]
    first = lax.broadcasted_iota(jnp.int32, real.shape, 0) == 0
    at = 3 * QUARTER
    spec_ref[at : at + GROUP] = real
    spec_ref[at + GROUP : at + 2 * GROUP] = jnp.where(first, 0.0, imag)
    spec_ref[at + 2 * GROUP :] = jnp.where(first, imag, real)


def lane_pick(source, index):
    return jnp.take_along_axis(source, index, axis=1)


def select_kernel(record_ref, high_ref, low_ref, out_ref):
    blocks = high_ref.shape[0]
    span, channels = record_ref.shape
    width = LANES
    parts = []
    for at in range(0, channels, width):
        parts.extend(split(record_ref[:, at : at + width]))
    parts = jnp.concatenate(parts, axis=0)
    row = lax.broadcasted_iota(jnp.int32, (width, LANES), 0)
    for block in range(blocks):
        high = high_ref[block : block + 1, :]
        hot = jnp.where(row == low_ref[block : block + 1, :], 1.0, 0.0).astype(BF16)
        both = jnp.dot(parts, hot, preferred_element_type=F32)
        picked = jnp.zeros((span, LANES), F32)
        for g in range(channels // width):
            at = 2 * span * g
            quarter = both[at : at + span] + both[at + span : at + 2 * span]
            picked = jnp.where(high == g, quarter, picked)
        out_ref[block] = picked


def route(block, plane):
    low, core, z = block // 16, block // 8 % 2, block % 8
    key = z ^ (4 * core)
    return (plane ^ key) * 4 + (low ^ (key & 1)) * 2 + core


def load_rows(recv_ref, plane, x_ref, first, count, at):
    span = recv_ref.shape[1]
    row = first
    while row < first + count:
        block, low = divmod(row, span)
        take = min(span - low, first + count - row)
        x_ref[at : at + take, :] = recv_ref[route(block, plane), low : low + take, :]
        row += take
        at += take


def ends_kernel(plane_ref, recv_ref, head_ref, tail_ref):
    plane = plane_ref[0]
    total = recv_ref.shape[0] * recv_ref.shape[1]
    load_rows(recv_ref, plane, head_ref, 0, NEXT, 0)
    load_rows(recv_ref, plane, tail_ref, total - BACK, BACK, 0)


def window_scale(x_ref, sq_ref, lags):
    rows = lags + TAPS
    sq = x_ref[:rows] * x_ref[:rows]
    for step in (1, 2, 4):
        sq_ref[:rows] = sq
        sq_ref[rows : rows + 8] = jnp.zeros((8, LANES), F32)
        sq = sq_ref[:rows] + sq_ref[step : rows + step]
    total = sq[74 * 8 : 74 * 8 + lags]
    length = 1
    have = rows
    at = {64: 0, 8: 64, 2: 72}
    while length < 64:
        have = have - 8 * length
        sq = sq[:have] + sq[8 * length : 8 * length + have]
        length *= 2
        if length in at:
            total = total + sq[8 * at[length] : 8 * at[length] + lags]
    return lax.rsqrt(total * (1.0 / TAPS) + 1e-6)


def segments(x_ref, sq_ref, spans, spec_ref, forward_ref, back_ref):
    scale = window_scale(x_ref, sq_ref, sum(spans))
    stacks = []
    base = 0
    for lags in spans:
        pieces = [x_ref[at : at + QUARTER] for at in range(base, base + 4 * QUARTER, QUARTER)]
        spectra = transform(pieces, forward_ref)
        parts = []
        for part, spectrum in enumerate(spectra):
            real, imag = spectrum[:GROUP], spectrum[GROUP:]
            at = (part - 1) % 4 * QUARTER
            wave_real, wave_imag = spec_ref[at : at + GROUP], spec_ref[at + GROUP : at + QUARTER]
            wave_last = wave_real if part else spec_ref[at + QUARTER : at + QUARTER + GROUP]
            product = [real * wave_real + imag * wave_imag, imag * wave_last - real * wave_imag]
            parts.append(dot3(back_ref, part, jnp.concatenate(product, axis=0)))
        first, second = combine(parts)
        corr = jnp.concatenate([first, second[: lags - QUARTER]], axis=0)
        corr = corr * scale[base : base + lags]
        folded = (corr[:, :GROUP] + corr[:, GROUP:]).T
        acc = folded[:BLOCK]
        for s in range(1, GROUP // BLOCK):
            acc = acc + folded[s * BLOCK : (s + 1) * BLOCK]
        stacks.append(acc)
        base += lags
    return stacks


def near_kernel(plane_ref, recv_ref, *refs):
    *refs, out_ref, x_ref, sq_ref = refs
    load_rows(recv_ref, plane_ref[0], x_ref, KEEP, HOP + 2 * HALF, 0)
    one, two = segments(x_ref, sq_ref, (HOP, HOP), *refs)
    out_ref[:, :HOP] = one
    out_ref[:, HOP:] = two


def back_kernel(plane_ref, recv_ref, tail_ref, *refs):
    *refs, send_ref, keep_ref, x_ref, sq_ref = refs
    x_ref[:BACK] = tail_ref[...]
    load_rows(recv_ref, plane_ref[0], x_ref, 0, 2 * HALF - BACK, BACK)
    (stack,) = segments(x_ref, sq_ref, (BACK + KEEP,), *refs)
    send_ref[...] = stack[:, :BACK]
    keep_ref[...] = stack[:, BACK:]


def last_kernel(plane_ref, recv_ref, head_ref, *refs):
    *refs, out_ref, x_ref, sq_ref = refs
    own = recv_ref.shape[0] * recv_ref.shape[1] - KEEP - 2 * HOP
    load_rows(recv_ref, plane_ref[0], x_ref, KEEP + 2 * HOP, own, 0)
    x_ref[own : own + NEXT] = head_ref[...]
    x_ref[own + NEXT : 2 * HALF] = jnp.zeros((2 * HALF - own - NEXT, LANES), F32)
    (out_ref[...],) = segments(x_ref, sq_ref, (MOST,), *refs)


def join_kernel(*refs):
    *parts, out_ref = refs
    at = 0
    for part in parts:
        out_ref[:, at : at + part.shape[1]] = part[...]
        at += part.shape[1]


def call(kernel, out_shape, scratch, flops, nbytes, mib, name, scalars=0):
    def run(*operands):
        smem = pl.BlockSpec(memory_space=pltpu.SMEM)
        vmem = pl.BlockSpec(memory_space=pltpu.VMEM)
        return pl.pallas_call(
            kernel,
            out_shape=out_shape,
            in_specs=[smem if i < scalars else vmem for i in range(len(operands))],
            scratch_shapes=scratch,
            compiler_params=pltpu.CompilerParams(vmem_limit_bytes=mib << 20),
            cost_estimate=pl.CostEstimate(flops=flops, bytes_accessed=nbytes, transcendentals=0),
            name=name,
        )(*operands)

    return run


def shards(record, channel_order, templates, group_of_slot, place_of_slot):
    blocks = lax.axis_size("tmpl")
    planes = lax.axis_size("chan")
    span = record.shape[1]
    lags = blocks * span
    forward, back = (jnp.asarray(t) for t in tables())
    across, along = [], []
    per_plane = blocks // planes
    for b in range(blocks):
        for z in range(planes):
            plane, lane = divmod(b, per_plane)
            keeper = route(lane * planes + z, plane)
            across.append((b * planes + z, keeper * planes + z))
            along.append((keeper * planes + z, keeper * planes + plane))
    raw = lax.ppermute(record.T, ("tmpl", "chan"), across)
    plane = lax.axis_index("chan").astype(jnp.int32).reshape(1)

    waves = templates.transpose(1, 0, 2).reshape(USED, TAPS)
    names = jax.ShapeDtypeStruct((blocks, LANES), jnp.int32)
    specs, high, low = call(
        template_kernel,
        (jax.ShapeDtypeStruct((3 * QUARTER + 3 * GROUP, LANES), F32), names, names),
        [
            pltpu.VMEM((LANES, 4 * QUARTER), F32),
            pltpu.VMEM((2, blocks, blocks * BLOCK), jnp.int32),
        ],
        2 * 3 * 4 * QUARTER * QUARTER * LANES,
        4 << 20,
        16,
        "template_spectra",
    )(
        waves,
        channel_order.reshape(-1, GROUP),
        group_of_slot.reshape(-1, SLOTS).T,
        place_of_slot.T,
        forward,
    )
    raw, high, low, plane, specs = lax.optimization_barrier((raw, high, low, plane, specs))
    raw = lax.ppermute(raw, ("tmpl", "chan"), along)
    sent = call(
        select_kernel,
        jax.ShapeDtypeStruct((blocks, span, LANES), F32),
        [],
        1 << 20,
        4 << 20,
        8,
        "select_channels",
    )(raw, high, low)
    recv = lax.all_to_all(sent, "tmpl", split_axis=0, concat_axis=0, tiled=True)
    rows = jax.ShapeDtypeStruct((BACK, LANES), F32), jax.ShapeDtypeStruct((NEXT, LANES), F32)
    head, tail = call(ends_kernel, rows[::-1], [], 0, 1 << 20, 8, "ends", 1)(plane, recv)
    up = [(z, (z + 1) % planes) for z in range(planes)]
    down = [(t, s) for s, t in up]
    after = lax.ppermute(head, "chan", down)
    before = lax.ppermute(tail, "chan", up)
    flops = 2 * 3 * (2 * HALF * HALF + HOP * 2 * HALF) * LANES
    shared = (specs, forward, back)

    def part(kernel, count, name, *lags):
        lines = pltpu.VMEM(((count - 1) * HOP + 2 * HALF + 8, LANES), F32)
        shape = tuple(jax.ShapeDtypeStruct((BLOCK, n), F32) for n in lags)
        return call(kernel, shape, [lines, lines], count * flops, 8 << 20, 24, name, 1)

    (middle,) = part(near_kernel, 2, "near_segments", 2 * HOP)(plane, recv, *shared)
    early, keep = part(back_kernel, 1, "back_segment", BACK, KEEP)(plane, recv, before, *shared)
    given = lax.ppermute(early, "chan", down)
    (last,) = part(last_kernel, 1, "last_segment", MOST)(plane, recv, after, *shared)
    joined = jax.ShapeDtypeStruct((BLOCK, blocks * span), F32)
    return call(join_kernel, joined, [], 0, 1 << 17, 8, "join")(keep, middle, last, given)


def solution(mesh):
    placed = (P(None, ("tmpl", "chan")), P(), P("tmpl", None, None), P(), P())
    return jax.shard_map(
        shards, mesh=mesh, in_specs=placed, out_specs=P("tmpl", "chan"), check_vma=False
    )
```

time: 81.8 us -> 74.1 us (0.906)
  Pallas kernels: 18.8 us -> 11.9 us
  blocking collectives: 36.9 us -> 35 us
  starting transfers between devices: 12.8 us -> 14.6 us
  local copies, waits for them, and re-layouts: 5.79 us -> 4.69 us
    pallas_call x6 -> x7, Pallas kernels: 18.8 us -> 11.9 us  [run(): pl.pallas_call(kernel, out_shape=out_shape, in_specs=[smem if i < scalars...]
    ppermute x1, starting transfers between devices: 1.91 us -> 5.73 us  [shards(): raw = lax.ppermute(raw, ('tmpl', 'chan'), along)]
    ppermute x1, waiting for transfers between devices: 1.25 us -> 4.68 us  [shards(): raw = lax.ppermute(raw, ('tmpl', 'chan'), along)]
    ppermute x1, waiting for transfers between devices: 3.25 us -> 0.01 us  [shards(): raw = lax.ppermute(record.T, ('tmpl', 'chan'), across)]
    ppermute x1, starting transfers between devices: 8.05 us -> 5.47 us  [shards(): raw = lax.ppermute(record.T, ('tmpl', 'chan'), across)]
    all_to_all x1, blocking collectives: 36.9 us -> 35 us  [shards(): recv = lax.all_to_all(sent, 'tmpl', split_axis=0, concat_axis=0, tiled=True)]
    unnamed x16 -> x13, local copies, waits for them, and re-layouts: 4.57 us -> 4.69 us
  transfers between devices with their start and end apart: 5 -> 5, of which waited for: 3 -> 2; matrix products, arithmetic and copies ran while one was open for 3% -> 1% of each run, Pallas kernels for 16% -> 12%
where the time goes in v3:
time: 74.1 us; the launch traced here: 73.7 us
  blocking collectives  35 us (47%)
  starting transfers between devices  14.6 us (20%)
  Pallas kernels  11.9 us (16%)
  waiting for transfers between devices  7.37 us (10%)
  local copies, waits for them, and re-layouts  4.69 us (6%)
    all_to_all x1, blocking collectives, shards(): recv = lax.all_to_all(sent, 'tmpl', split_axis=0, concat_axis=0, tiled=True)  35 us
    pallas_call x7, Pallas kernels, run(): pl.pallas_call(kernel, out_shape=out_shape, in_specs=[smem if i < scalars...  11.9 us
    ppermute x1, starting transfers between devices, shards(): raw = lax.ppermute(raw, ('tmpl', 'chan'), along)  5.73 us
    ppermute x1, starting transfers between devices, shards(): raw = lax.ppermute(record.T, ('tmpl', 'chan'), across)  5.47 us
    unnamed x13, local copies, waits for them, and re-layouts  4.69 us
    ppermute x1, waiting for transfers between devices, shards(): raw = lax.ppermute(raw, ('tmpl', 'chan'), along)  4.68 us
    ppermute x1, waiting for transfers between devices, shards(): before = lax.ppermute(tail, 'chan', up)  2.68 us
    ppermute x1, starting transfers between devices, shards(): after = lax.ppermute(head, 'chan', down)  2.66 us
  transfers between devices with their start and end apart: 5, of which 2 were waited for; matrix products, arithmetic and copies ran while one was open for 1% of the time, Pallas kernels for 12%

profile of v3, /device:TPU:1, one launch (start us, length us, event | category | flops | bytes accessed | tf_op | source)
XLA Modules:
  0.0 73.7 jit_solution(14997480388690129248)
XLA Ops:
  0.0 5.5 %collective-permute-start = (f32[48,1024]{1,0:T(8,128)}, f32[48,1024]{1,0:T(8,128)S(1)}, u32[]{:S(2)}, u32[]{:S(2)}) collective-permute-start(f32[48,1024]{1,0:T(8,128)} %bitcast.16), channel_id=1, source_target_pairs={{0,0},{1,49},{2,66},{3,115},{4,132},{5,181},{6,198},{7,247},{8,136... | collective-permute-start | bytes 589832 | tf_op jit(solution)/shard_map/ppermute | solution.py:316
  5.5 0.8 %copy.10 = s32[256,30,1]{0,1,2:T(8,128)S(1)} copy(s32[256,30,1]{0,2,1:T(1,128)} %param.10) | data formatting | bytes 61440
  6.2 0.0 copy-start
  6.2 1.4 %copy-done = bf16[1024,768]{1,0:T(8,128)(2,1)S(1)} copy-done((bf16[1024,768]{1,0:T(8,128)(2,1)S(1)}, bf16[1024,768]{1,0:T(8,128)(2,1)}, u32[]{:S(2)}) %copy-start) | copy-done | bytes 1572888
  7.6 0.0 copy-start.3
  7.6 1.1 %copy-done.3 = f32[8,30,600]{2,0,1:T(8,128)S(1)} copy-done((f32[8,30,600]{2,0,1:T(8,128)S(1)}, f32[8,30,600]{2,0,1:T(8,128)}, u32[]{:S(2)}) %copy-start.3) | copy-done | bytes 576024
  8.7 0.0 copy-start.4
  8.7 0.8 %copy-done.4 = s32[256,30]{0,1:T(8,128)S(1)} copy-done((s32[256,30]{0,1:T(8,128)S(1)}, s32[256,30]{0,1:T(8,128)}, u32[]{:S(2)}) %copy-start.4) | copy-done | bytes 30744
  9.5 0.0 copy-start.5
  9.5 0.7 copy-done.5
  10.2 1.4 %template_spectra.1 = (f32[1152,256]{1,0:T(8,128)S(1)}, s32[32,256]{1,0:T(8,128)S(1)}, s32[32,256]{1,0:T(8,128)S(1)}) custom-call(f32[240,600]{1,0:T(8,128)S(1)} %bitcast.12, s32[8,128]{1,0:T(8,128)S(1)} %bitcast.15, s32[30,256]{1,0:T(8,128)S(1)} %bitcast.13, s32[30,256]{1,0:T(8,128)S(1)} %bitcast.14, bf16[1024,768]{1,0:T(8,128)(2,1)S(1)} %copy-done), custom_call_target="tpu_custom_call" | custom-call | flops 402653184 | bytes 4194304 | tf_op jit(solution)/shard_map/template_spectra/pallas_call | solution.py:289
  11.6 0.0 collective-permute-done
  11.6 5.7 %collective-permute-start.1 = (f32[48,1024]{1,0:T(8,128)S(1)}, f32[48,1024]{1,0:T(8,128)S(1)}, u32[]{:S(2)}, u32[]{:S(2)}) collective-permute-start(f32[48,1024]{1,0:T(8,128)S(1)} %collective-permute-done), channel_id=1, source_target_pairs={{0,0},{49,48},{66,64},{115,112},{132,128},{181,176},{198,192},{247... | collective-permute-start | bytes 589832 | tf_op jit(solution)/shard_map/ppermute | solution.py:340
  17.3 4.7 %collective-permute-done.1.record_ref = f32[48,1024]{1,0:T(8,128)S(1)} collective-permute-done((f32[48,1024]{1,0:T(8,128)S(1)}, f32[48,1024]{1,0:T(8,128)S(1)}, u32[]{:S(2)}, u32[]{:S(2)}) %collective-permute-start.1) | collective-permute-done | bytes 196640 | tf_op jit(solution)/shard_map/ppermute | solution.py:340
  22.0 2.2 %select_channels.1 = f32[32,48,256]{2,1,0:T(8,128)S(1)} custom-call(f32[48,1024]{1,0:T(8,128)S(1)} %collective-permute-done.1.record_ref, s32[32,256]{1,0:T(8,128)S(1)} %get-tuple-element.22.high_ref, s32[32,256]{1,0:T(8,128)S(1)} %get-tuple-element.23.low_ref), custom_call_target="tpu_custom_call" | custom-call | flops 1048576 | bytes 4194304 | tf_op jit(solution)/shard_map/select_channels/pallas_call | solution.py:289
  24.3 0.0 copy-start.2
  24.3 35.0 %all_to_all.5.recv_ref = f32[32,48,256]{2,1,0:T(8,128)S(1)} all-to-all(f32[32,48,256]{2,1,0:T(8,128)S(1)} %select_channels.1), channel_id=1, replica_groups=mesh['tmpl'=32,'chan'=8] {'tmpl'}, dimensions={0} | all-to-all | bytes 3145728 | tf_op jit(solution)/shard_map/all_to_all | solution.py:350
  59.2 0.0 copy-start.1
  59.3 0.1 collective-permute-start.2
  59.4 2.7 %collective-permute-start.3 = (f32[368,256]{1,0:T(8,128)S(1)}, f32[368,256]{1,0:T(8,128)S(1)}, u32[]{:S(2)}, u32[]{:S(2)}) collective-permute-start(f32[368,256]{1,0:T(8,128)S(1)} %get-tuple-element.27), channel_id=1, source_target_pairs={{1,0},{2,1},{3,2},{4,3},{5,4},{6,5},{7,6},{0,7},{9,8},{10,9},{11,1... | collective-permute-start | bytes 1130504 | tf_op jit(solution)/shard_map/ppermute | solution.py:355
  62.0 0.0 copy-done.2
  62.0 0.0 copy-done.1
  62.0 3.4 %near_segments.1.refs_1_ = f32[8,768]{1,0:T(8,128)S(1)} custom-call(s32[1]{0:T(128)} %bitcast.6.plane_ref, f32[32,48,256]{2,1,0:T(8,128)S(1)} %all_to_all.5.recv_ref, f32[1152,256]{1,0:T(8,128)S(1)} %get-tuple-element.25.refs_0_, bf16[1024,768]{1,0:T(8,128)(2,1)S(1)} %copy-done.1, bf16[1024,768]{1,0:T(8,128)(2,1)S(1)} %copy-done.2), custom_call_target="tpu_custom_call" | custom-call | flops 2818572288 | bytes 8388608 | tf_op jit(solution)/shard_map/near_segments/pallas_call | solution.py:289
  65.5 2.7 %collective-permute-done.2.tail_ref = f32[232,256]{1,0:T(8,128)S(1)} collective-permute-done((f32[232,256]{1,0:T(8,128)S(1)}, f32[232,256]{1,0:T(8,128)S(1)}, u32[]{:S(2)}, u32[]{:S(2)}) %collective-permute-start.2) | collective-permute-done | bytes 237600 | tf_op jit(solution)/shard_map/ppermute | solution.py:356
  68.1 2.0 %back_segment.1 = (f32[8,232]{1,0:T(8,128)S(1)}, f32[8,128]{1,0:T(8,128)S(1)}) custom-call(s32[1]{0:T(128)} %bitcast.6.plane_ref, f32[32,48,256]{2,1,0:T(8,128)S(1)} %all_to_all.5.recv_ref, f32[232,256]{1,0:T(8,128)S(1)} %collective-permute-done.2.tail_ref, f32[1152,256]{1,0:T(8,128)S(1)} %get-tuple-element.25.refs_0_, bf16[1024,768]{1,0:T(8,128)(2,1)S(1)} %copy-done.1, ...), custom_call_target="tpu_custom_call" | custom-call | flops 1409286144 | bytes 8388608 | tf_op jit(solution)/shard_map/back_segment/pallas_call | solution.py:289
  70.2 0.7 collective-permute-start.4
  70.9 0.0 collective-permute-done.3.head_ref
  70.9 2.1 %last_segment.1.refs_2_ = f32[8,408]{1,0:T(8,128)S(1)} custom-call(s32[1]{0:T(128)} %bitcast.6.plane_ref, f32[32,48,256]{2,1,0:T(8,128)S(1)} %all_to_all.5.recv_ref, f32[368,256]{1,0:T(8,128)S(1)} %collective-permute-done.3.head_ref, f32[1152,256]{1,0:T(8,128)S(1)} %get-tuple-element.25.refs_0_, bf16[1024,768]{1,0:T(8,128)(2,1)S(1)} %copy-done.1, ...), custom_call_target="tpu_custom_call" | custom-call | flops 1409286144 | bytes 8388608 | tf_op jit(solution)/shard_map/last_segment/pallas_call | solution.py:289
  73.0 0.0 collective-permute-done.4.refs_3_
  73.0 0.7 join.1
  (1 shorter events, 0.0 us)
Async XLA Ops:
  0.0 11.6 %collective-permute-start = (f32[48,1024]{1,0:T(8,128)}, f32[48,1024]{1,0:T(8,128)S(1)}, u32[]{:S(2)}, u32[]{:S(2)}) collective-permute-start(f32[48,1024]{1,0:T(8,128)} %bitcast.16), channel_id=1, source_target_pairs={{0,0},{1,49},{2,66},{3,115},{4,132},{5,181},{6,198},{7,247},{8,136... | collective-permute-start | bytes 589832 | tf_op jit(solution)/shard_map/ppermute | solution.py:316
  6.2 1.4 %copy-start = (bf16[1024,768]{1,0:T(8,128)(2,1)S(1)}, bf16[1024,768]{1,0:T(8,128)(2,1)}, u32[]{:S(2)}) copy-start(bf16[1024,768]{1,0:T(8,128)(2,1)} %constant.8.clone.table_ref.refs_1_) | copy-start | bytes 4718596
  7.6 1.1 %copy-start.3 = (f32[8,30,600]{2,0,1:T(8,128)S(1)}, f32[8,30,600]{2,0,1:T(8,128)}, u32[]{:S(2)}) copy-start(f32[8,30,600]{2,0,1:T(8,128)} %param.9) | copy-start | bytes 1728004
  8.7 0.8 %copy-start.4 = (s32[256,30]{0,1:T(8,128)S(1)}, s32[256,30]{0,1:T(8,128)}, u32[]{:S(2)}) copy-start(s32[256,30]{0,1:T(8,128)} %param.11) | copy-start | bytes 92164
  9.5 0.7 copy-start.5
  11.6 10.4 %collective-permute-start.1 = (f32[48,1024]{1,0:T(8,128)S(1)}, f32[48,1024]{1,0:T(8,128)S(1)}, u32[]{:S(2)}, u32[]{:S(2)}) collective-permute-start(f32[48,1024]{1,0:T(8,128)S(1)} %collective-permute-done), channel_id=1, source_target_pairs={{0,0},{49,48},{66,64},{115,112},{132,128},{181,176},{198,192},{247... | collective-permute-start | bytes 589832 | tf_op jit(solution)/shard_map/ppermute | solution.py:340
  24.3 37.8 %copy-start.2 = (bf16[1024,768]{1,0:T(8,128)(2,1)S(1)}, bf16[1024,768]{1,0:T(8,128)(2,1)}, u32[]{:S(2)}) copy-start(bf16[1024,768]{1,0:T(8,128)(2,1)} %constant.9.clone.refs_2_) | copy-start | bytes 4718596
  59.2 2.8 %copy-start.1 = (bf16[1024,768]{1,0:T(8,128)(2,1)S(1)}, bf16[1024,768]{1,0:T(8,128)(2,1)}, u32[]{:S(2)}) copy-start(bf16[1024,768]{1,0:T(8,128)(2,1)} %constant.8.clone.table_ref.refs_1_) | copy-start | bytes 4718596
  59.3 8.9 %collective-permute-start.2 = (f32[232,256]{1,0:T(8,128)S(1)}, f32[232,256]{1,0:T(8,128)S(1)}, u32[]{:S(2)}, u32[]{:S(2)}) collective-permute-start(f32[232,256]{1,0:T(8,128)S(1)} %get-tuple-element.24), channel_id=1, source_target_pairs={{0,1},{1,2},{2,3},{3,4},{4,5},{5,6},{6,7},{7,0},{8,9},{9,10},{10,1... | collective-permute-start | bytes 712712 | tf_op jit(solution)/shard_map/ppermute | solution.py:356
  59.4 11.5 %collective-permute-start.3 = (f32[368,256]{1,0:T(8,128)S(1)}, f32[368,256]{1,0:T(8,128)S(1)}, u32[]{:S(2)}, u32[]{:S(2)}) collective-permute-start(f32[368,256]{1,0:T(8,128)S(1)} %get-tuple-element.27), channel_id=1, source_target_pairs={{1,0},{2,1},{3,2},{4,3},{5,4},{6,5},{7,6},{0,7},{9,8},{10,9},{11,1... | collective-permute-start | bytes 1130504 | tf_op jit(solution)/shard_map/ppermute | solution.py:355
  70.2 2.8 %collective-permute-start.4 = (f32[8,232]{1,0:T(8,128)S(1)}, f32[8,232]{1,0:T(8,128)S(1)}, u32[]{:S(2)}, u32[]{:S(2)}) collective-permute-start(f32[8,232]{1,0:T(8,128)S(1)} %get-tuple-element.28), channel_id=1, source_target_pairs={{1,0},{2,1},{3,2},{4,3},{5,4},{6,5},{7,6},{0,7},{9,8},{10,9},{11,1... | collective-permute-start | bytes 22280 | tf_op jit(solution)/shard_map/ppermute | solution.py:367

commit v4 on v3

--- a/solution.py
+++ b/solution.py
@@ -179,7 +179,8 @@
 
 def route(block, plane):
     low, core, z = block // 16, block // 8 % 2, block % 8
-    key = z ^ (4 * core)
+    far = plane ^ z
+    key = (far & 1) * 7 ^ (far >> 1 & 1) * 5 ^ (far >> 2 & 1) ^ (3 * core)
     return (plane ^ key) * 4 + (low ^ (key & 1)) * 2 + core
 
 

time: 74.1 us -> 73.3 us (0.989)
  starting transfers between devices: 14.6 us -> 20.3 us
  blocking collectives: 35 us -> 30.6 us
  waiting for transfers between devices: 7.37 us -> 5.27 us
    all_to_all x1, blocking collectives: 35 us -> 30.6 us  [shards(): recv = lax.all_to_all(sent, 'tmpl', split_axis=0, concat_axis=0, tiled=True)]
    ppermute x1, starting transfers between devices: 5.73 us -> 9.91 us  [shards(): raw = lax.ppermute(raw, ('tmpl', 'chan'), along)]
    ppermute x1, waiting for transfers between devices: 4.68 us -> 2.59 us  [shards(): raw = lax.ppermute(raw, ('tmpl', 'chan'), along)]
    ppermute x1, starting transfers between devices: 5.47 us -> 6.39 us  [shards(): raw = lax.ppermute(record.T, ('tmpl', 'chan'), across)]
where the time goes in v4:
time: 73.3 us; the launch traced here: 72.9 us
  blocking collectives  30.6 us (42%)
  starting transfers between devices  20.3 us (28%)
  Pallas kernels  11.9 us (16%)
  waiting for transfers between devices  5.27 us (7%)
  local copies, waits for them, and re-layouts  4.69 us (6%)
    all_to_all x1, blocking collectives, shards(): recv = lax.all_to_all(sent, 'tmpl', split_axis=0, concat_axis=0, tiled=True)  30.6 us
    pallas_call x7, Pallas kernels, run(): pl.pallas_call(kernel, out_shape=out_shape, in_specs=[smem if i < scalars...  11.9 us
    ppermute x1, starting transfers between devices, shards(): raw = lax.ppermute(raw, ('tmpl', 'chan'), along)  9.91 us
    ppermute x1, starting transfers between devices, shards(): raw = lax.ppermute(record.T, ('tmpl', 'chan'), across)  6.39 us
    unnamed x13, local copies, waits for them, and re-layouts  4.69 us
    ppermute x1, waiting for transfers between devices, shards(): before = lax.ppermute(tail, 'chan', up)  2.67 us
    ppermute x1, waiting for transfers between devices, shards(): raw = lax.ppermute(raw, ('tmpl', 'chan'), along)  2.59 us
    ppermute x1, starting transfers between devices, shards(): after = lax.ppermute(head, 'chan', down)  2 us
  transfers between devices with their start and end apart: 5, of which 2 were waited for; matrix products, arithmetic and copies ran while one was open for 1% of the time, Pallas kernels for 12%

profile of v4, /device:TPU:1, one launch (start us, length us, event | category | flops | bytes accessed | tf_op | source)
XLA Modules:
  0.0 72.9 jit_solution(653515884732135532)
XLA Ops:
  0.0 6.4 %collective-permute-start = (f32[48,1024]{1,0:T(8,128)}, f32[48,1024]{1,0:T(8,128)S(1)}, u32[]{:S(2)}, u32[]{:S(2)}) collective-permute-start(f32[48,1024]{1,0:T(8,128)} %bitcast.16), channel_id=1, source_target_pairs={{0,0},{1,241},{2,178},{3,67},{4,52},{5,197},{6,134},{7,119},{8,120... | collective-permute-start | bytes 589832 | tf_op jit(solution)/shard_map/ppermute | solution.py:317
  6.4 0.8 %copy.10 = s32[256,30,1]{0,1,2:T(8,128)S(1)} copy(s32[256,30,1]{0,2,1:T(1,128)} %param.10) | data formatting | bytes 61440
  7.2 0.0 copy-start
  7.2 1.4 %copy-done = bf16[1024,768]{1,0:T(8,128)(2,1)S(1)} copy-done((bf16[1024,768]{1,0:T(8,128)(2,1)S(1)}, bf16[1024,768]{1,0:T(8,128)(2,1)}, u32[]{:S(2)}) %copy-start) | copy-done | bytes 1572888
  8.6 0.0 copy-start.3
  8.6 1.1 %copy-done.3 = f32[8,30,600]{2,0,1:T(8,128)S(1)} copy-done((f32[8,30,600]{2,0,1:T(8,128)S(1)}, f32[8,30,600]{2,0,1:T(8,128)}, u32[]{:S(2)}) %copy-start.3) | copy-done | bytes 576024
  9.6 0.0 copy-start.4
  9.6 0.8 %copy-done.4 = s32[256,30]{0,1:T(8,128)S(1)} copy-done((s32[256,30]{0,1:T(8,128)S(1)}, s32[256,30]{0,1:T(8,128)}, u32[]{:S(2)}) %copy-start.4) | copy-done | bytes 30744
  10.4 0.0 copy-start.5
  10.4 0.7 copy-done.5
  11.1 1.4 %template_spectra.1 = (f32[1152,256]{1,0:T(8,128)S(1)}, s32[32,256]{1,0:T(8,128)S(1)}, s32[32,256]{1,0:T(8,128)S(1)}) custom-call(f32[240,600]{1,0:T(8,128)S(1)} %bitcast.12, s32[8,128]{1,0:T(8,128)S(1)} %bitcast.15, s32[30,256]{1,0:T(8,128)S(1)} %bitcast.13, s32[30,256]{1,0:T(8,128)S(1)} %bitcast.14, bf16[1024,768]{1,0:T(8,128)(2,1)S(1)} %copy-done), custom_call_target="tpu_custom_call" | custom-call | flops 402653184 | bytes 4194304 | tf_op jit(solution)/shard_map/template_spectra/pallas_call | solution.py:290
  12.5 0.0 collective-permute-done
  12.5 9.9 %collective-permute-start.1 = (f32[48,1024]{1,0:T(8,128)S(1)}, f32[48,1024]{1,0:T(8,128)S(1)}, u32[]{:S(2)}, u32[]{:S(2)}) collective-permute-start(f32[48,1024]{1,0:T(8,128)S(1)} %collective-permute-done), channel_id=1, source_target_pairs={{0,0},{241,240},{178,176},{67,64},{52,48},{197,192},{134,128},{119... | collective-permute-start | bytes 589832 | tf_op jit(solution)/shard_map/ppermute | solution.py:341
  22.4 2.6 %collective-permute-done.1.record_ref = f32[48,1024]{1,0:T(8,128)S(1)} collective-permute-done((f32[48,1024]{1,0:T(8,128)S(1)}, f32[48,1024]{1,0:T(8,128)S(1)}, u32[]{:S(2)}, u32[]{:S(2)}) %collective-permute-start.1) | collective-permute-done | bytes 196640 | tf_op jit(solution)/shard_map/ppermute | solution.py:341
  25.0 2.2 %select_channels.1 = f32[32,48,256]{2,1,0:T(8,128)S(1)} custom-call(f32[48,1024]{1,0:T(8,128)S(1)} %collective-permute-done.1.record_ref, s32[32,256]{1,0:T(8,128)S(1)} %get-tuple-element.22.high_ref, s32[32,256]{1,0:T(8,128)S(1)} %get-tuple-element.23.low_ref), custom_call_target="tpu_custom_call" | custom-call | flops 1048576 | bytes 4194304 | tf_op jit(solution)/shard_map/select_channels/pallas_call | solution.py:290
  27.3 0.0 copy-start.2
  27.3 30.6 %all_to_all.5.recv_ref = f32[32,48,256]{2,1,0:T(8,128)S(1)} all-to-all(f32[32,48,256]{2,1,0:T(8,128)S(1)} %select_channels.1), channel_id=1, replica_groups=mesh['tmpl'=32,'chan'=8] {'tmpl'}, dimensions={0} | all-to-all | bytes 3145728 | tf_op jit(solution)/shard_map/all_to_all | solution.py:351
  57.9 0.0 copy-start.1
  58.0 0.8 %collective-permute-start.2 = (f32[232,256]{1,0:T(8,128)S(1)}, f32[232,256]{1,0:T(8,128)S(1)}, u32[]{:S(2)}, u32[]{:S(2)}) collective-permute-start(f32[232,256]{1,0:T(8,128)S(1)} %get-tuple-element.24), channel_id=1, source_target_pairs={{0,1},{1,2},{2,3},{3,4},{4,5},{5,6},{6,7},{7,0},{8,9},{9,10},{10,1... | collective-permute-start | bytes 712712 | tf_op jit(solution)/shard_map/ppermute | solution.py:357
  58.7 2.0 %collective-permute-start.3 = (f32[368,256]{1,0:T(8,128)S(1)}, f32[368,256]{1,0:T(8,128)S(1)}, u32[]{:S(2)}, u32[]{:S(2)}) collective-permute-start(f32[368,256]{1,0:T(8,128)S(1)} %get-tuple-element.27), channel_id=1, source_target_pairs={{1,0},{2,1},{3,2},{4,3},{5,4},{6,5},{7,6},{0,7},{9,8},{10,9},{11,1... | collective-permute-start | bytes 1130504 | tf_op jit(solution)/shard_map/ppermute | solution.py:356
  60.7 0.0 copy-done.2
  60.7 0.0 copy-done.1
  60.7 3.4 %near_segments.1.refs_1_ = f32[8,768]{1,0:T(8,128)S(1)} custom-call(s32[1]{0:T(128)} %bitcast.6.plane_ref, f32[32,48,256]{2,1,0:T(8,128)S(1)} %all_to_all.5.recv_ref, f32[1152,256]{1,0:T(8,128)S(1)} %get-tuple-element.25.refs_0_, bf16[1024,768]{1,0:T(8,128)(2,1)S(1)} %copy-done.1, bf16[1024,768]{1,0:T(8,128)(2,1)S(1)} %copy-done.2), custom_call_target="tpu_custom_call" | custom-call | flops 2818572288 | bytes 8388608 | tf_op jit(solution)/shard_map/near_segments/pallas_call | solution.py:290
  64.2 2.7 %collective-permute-done.2.tail_ref = f32[232,256]{1,0:T(8,128)S(1)} collective-permute-done((f32[232,256]{1,0:T(8,128)S(1)}, f32[232,256]{1,0:T(8,128)S(1)}, u32[]{:S(2)}, u32[]{:S(2)}) %collective-permute-start.2) | collective-permute-done | bytes 237600 | tf_op jit(solution)/shard_map/ppermute | solution.py:357
  66.8 2.0 %back_segment.1 = (f32[8,232]{1,0:T(8,128)S(1)}, f32[8,128]{1,0:T(8,128)S(1)}) custom-call(s32[1]{0:T(128)} %bitcast.6.plane_ref, f32[32,48,256]{2,1,0:T(8,128)S(1)} %all_to_all.5.recv_ref, f32[232,256]{1,0:T(8,128)S(1)} %collective-permute-done.2.tail_ref, f32[1152,256]{1,0:T(8,128)S(1)} %get-tuple-element.25.refs_0_, bf16[1024,768]{1,0:T(8,128)(2,1)S(1)} %copy-done.1, ...), custom_call_target="tpu_custom_call" | custom-call | flops 1409286144 | bytes 8388608 | tf_op jit(solution)/shard_map/back_segment/pallas_call | solution.py:290
  68.9 1.2 %collective-permute-start.4 = (f32[8,232]{1,0:T(8,128)S(1)}, f32[8,232]{1,0:T(8,128)S(1)}, u32[]{:S(2)}, u32[]{:S(2)}) collective-permute-start(f32[8,232]{1,0:T(8,128)S(1)} %get-tuple-element.28), channel_id=1, source_target_pairs={{1,0},{2,1},{3,2},{4,3},{5,4},{6,5},{7,6},{0,7},{9,8},{10,9},{11,1... | collective-permute-start | bytes 22280 | tf_op jit(solution)/shard_map/ppermute | solution.py:368
  70.1 0.0 collective-permute-done.3.head_ref
  70.1 2.1 %last_segment.1.refs_2_ = f32[8,408]{1,0:T(8,128)S(1)} custom-call(s32[1]{0:T(128)} %bitcast.6.plane_ref, f32[32,48,256]{2,1,0:T(8,128)S(1)} %all_to_all.5.recv_ref, f32[368,256]{1,0:T(8,128)S(1)} %collective-permute-done.3.head_ref, f32[1152,256]{1,0:T(8,128)S(1)} %get-tuple-element.25.refs_0_, bf16[1024,768]{1,0:T(8,128)(2,1)S(1)} %copy-done.1, ...), custom_call_target="tpu_custom_call" | custom-call | flops 1409286144 | bytes 8388608 | tf_op jit(solution)/shard_map/last_segment/pallas_call | solution.py:290
  72.2 0.0 collective-permute-done.4.refs_3_
  72.2 0.7 join.1
  (1 shorter events, 0.0 us)
Async XLA Ops:
  0.0 12.5 %collective-permute-start = (f32[48,1024]{1,0:T(8,128)}, f32[48,1024]{1,0:T(8,128)S(1)}, u32[]{:S(2)}, u32[]{:S(2)}) collective-permute-start(f32[48,1024]{1,0:T(8,128)} %bitcast.16), channel_id=1, source_target_pairs={{0,0},{1,241},{2,178},{3,67},{4,52},{5,197},{6,134},{7,119},{8,120... | collective-permute-start | bytes 589832 | tf_op jit(solution)/shard_map/ppermute | solution.py:317
  7.2 1.4 %copy-start = (bf16[1024,768]{1,0:T(8,128)(2,1)S(1)}, bf16[1024,768]{1,0:T(8,128)(2,1)}, u32[]{:S(2)}) copy-start(bf16[1024,768]{1,0:T(8,128)(2,1)} %constant.8.clone.table_ref.refs_1_) | copy-start | bytes 4718596
  8.6 1.1 %copy-start.3 = (f32[8,30,600]{2,0,1:T(8,128)S(1)}, f32[8,30,600]{2,0,1:T(8,128)}, u32[]{:S(2)}) copy-start(f32[8,30,600]{2,0,1:T(8,128)} %param.9) | copy-start | bytes 1728004
  9.6 0.8 %copy-start.4 = (s32[256,30]{0,1:T(8,128)S(1)}, s32[256,30]{0,1:T(8,128)}, u32[]{:S(2)}) copy-start(s32[256,30]{0,1:T(8,128)} %param.11) | copy-start | bytes 92164
  10.4 0.7 copy-start.5
  12.5 12.5 %collective-permute-start.1 = (f32[48,1024]{1,0:T(8,128)S(1)}, f32[48,1024]{1,0:T(8,128)S(1)}, u32[]{:S(2)}, u32[]{:S(2)}) collective-permute-start(f32[48,1024]{1,0:T(8,128)S(1)} %collective-permute-done), channel_id=1, source_target_pairs={{0,0},{241,240},{178,176},{67,64},{52,48},{197,192},{134,128},{119... | collective-permute-start | bytes 589832 | tf_op jit(solution)/shard_map/ppermute | solution.py:341
  27.3 33.5 %copy-start.2 = (bf16[1024,768]{1,0:T(8,128)(2,1)S(1)}, bf16[1024,768]{1,0:T(8,128)(2,1)}, u32[]{:S(2)}) copy-start(bf16[1024,768]{1,0:T(8,128)(2,1)} %constant.9.clone.refs_2_) | copy-start | bytes 4718596
  57.9 2.8 %copy-start.1 = (bf16[1024,768]{1,0:T(8,128)(2,1)S(1)}, bf16[1024,768]{1,0:T(8,128)(2,1)}, u32[]{:S(2)}) copy-start(bf16[1024,768]{1,0:T(8,128)(2,1)} %constant.8.clone.table_ref.refs_1_) | copy-start | bytes 4718596
  58.0 8.9 %collective-permute-start.2 = (f32[232,256]{1,0:T(8,128)S(1)}, f32[232,256]{1,0:T(8,128)S(1)}, u32[]{:S(2)}, u32[]{:S(2)}) collective-permute-start(f32[232,256]{1,0:T(8,128)S(1)} %get-tuple-element.24), channel_id=1, source_target_pairs={{0,1},{1,2},{2,3},{3,4},{4,5},{5,6},{6,7},{7,0},{8,9},{9,10},{10,1... | collective-permute-start | bytes 712712 | tf_op jit(solution)/shard_map/ppermute | solution.py:357
  58.7 11.4 %collective-permute-start.3 = (f32[368,256]{1,0:T(8,128)S(1)}, f32[368,256]{1,0:T(8,128)S(1)}, u32[]{:S(2)}, u32[]{:S(2)}) collective-permute-start(f32[368,256]{1,0:T(8,128)S(1)} %get-tuple-element.27), channel_id=1, source_target_pairs={{1,0},{2,1},{3,2},{4,3},{5,4},{6,5},{7,6},{0,7},{9,8},{10,9},{11,1... | collective-permute-start | bytes 1130504 | tf_op jit(solution)/shard_map/ppermute | solution.py:356
  68.9 3.3 %collective-permute-start.4 = (f32[8,232]{1,0:T(8,128)S(1)}, f32[8,232]{1,0:T(8,128)S(1)}, u32[]{:S(2)}, u32[]{:S(2)}) collective-permute-start(f32[8,232]{1,0:T(8,128)S(1)} %get-tuple-element.28), channel_id=1, source_target_pairs={{1,0},{2,1},{3,2},{4,3},{5,4},{6,5},{7,6},{0,7},{9,8},{10,9},{11,1... | collective-permute-start | bytes 22280 | tf_op jit(solution)/shard_map/ppermute | solution.py:368

commit v5 on v4

--- a/solution.py
+++ b/solution.py
@@ -164,10 +164,12 @@
     for at in range(0, channels, width):
         parts.extend(split(record_ref[:, at : at + width]))
     parts = jnp.concatenate(parts, axis=0)
-    row = lax.broadcasted_iota(jnp.int32, (width, LANES), 0)
+    row = lax.broadcasted_iota(jnp.int32, (width, LANES), 0).astype(F32).astype(BF16)
+    one, zero = jnp.ones((), BF16), jnp.zeros((), BF16)
     for block in range(blocks):
         high = high_ref[block : block + 1, :]
-        hot = jnp.where(row == low_ref[block : block + 1, :], 1.0, 0.0).astype(BF16)
+        low = low_ref[block : block + 1, :].astype(F32).astype(BF16)
+        hot = jnp.where(row == low, one, zero)
         both = jnp.dot(parts, hot, preferred_element_type=F32)
         picked = jnp.zeros((span, LANES), F32)
         for g in range(channels // width):
@@ -318,6 +320,14 @@
     plane = lax.axis_index("chan").astype(jnp.int32).reshape(1)
 
     waves = templates.transpose(1, 0, 2).reshape(USED, TAPS)
+    small = (
+        waves,
+        channel_order.reshape(-1, GROUP),
+        group_of_slot.reshape(-1, SLOTS).T,
+        place_of_slot.T,
+    )
+    raw, plane, small = lax.optimization_barrier((raw, plane, small))
+    raw = lax.ppermute(raw, ("tmpl", "chan"), along)
     names = jax.ShapeDtypeStruct((blocks, LANES), jnp.int32)
     specs, high, low = call(
         template_kernel,
@@ -330,15 +340,8 @@
         4 << 20,
         16,
         "template_spectra",
-    )(
-        waves,
-        channel_order.reshape(-1, GROUP),
-        group_of_slot.reshape(-1, SLOTS).T,
-        place_of_slot.T,
-        forward,
-    )
-    raw, high, low, plane, specs = lax.optimization_barrier((raw, high, low, plane, specs))
-    raw = lax.ppermute(raw, ("tmpl", "chan"), along)
+    )(*small, forward)
+    raw, high, low, specs = lax.optimization_barrier((raw, high, low, specs))
     sent = call(
         select_kernel,
         jax.ShapeDtypeStruct((blocks, span, LANES), F32),

time: 73.3 us -> 72.7 us (level)
  blocking collectives: 30.6 us -> 29 us
  waiting for transfers between devices: 5.27 us -> 6.73 us
    ppermute x1, waiting for transfers between devices: 0.01 us -> 4.03 us  [shards(): raw = lax.ppermute(record.T, ('tmpl', 'chan'), across)]
    ppermute x1, waiting for transfers between devices: 2.59 us -> 0.01 us  [shards(): raw = lax.ppermute(raw, ('tmpl', 'chan'), along)]
    ppermute x1, starting transfers between devices: 0.75 us -> 2.82 us  [shards(): before = lax.ppermute(tail, 'chan', up)]
    ppermute x1, starting transfers between devices: 9.91 us -> 8.01 us  [shards(): raw = lax.ppermute(raw, ('tmpl', 'chan'), along)]
    all_to_all x1, blocking collectives: 30.6 us -> 29 us  [shards(): recv = lax.all_to_all(sent, 'tmpl', split_axis=0, concat_axis=0, tiled=True)]
where the time goes in v5:
time: 72.7 us; the launch traced here: 72.3 us
  blocking collectives  29 us (40%)
  starting transfers between devices  20.2 us (28%)
  Pallas kernels  11.5 us (16%)
  waiting for transfers between devices  6.73 us (9%)
  local copies, waits for them, and re-layouts  4.69 us (6%)
    all_to_all x1, blocking collectives, shards(): recv = lax.all_to_all(sent, 'tmpl', split_axis=0, concat_axis=0, tiled=True)  29 us
    pallas_call x7, Pallas kernels, run(): pl.pallas_call(kernel, out_shape=out_shape, in_specs=[smem if i < scalars...  11.5 us
    ppermute x1, starting transfers between devices, shards(): raw = lax.ppermute(raw, ('tmpl', 'chan'), along)  8.01 us
    ppermute x1, starting transfers between devices, shards(): raw = lax.ppermute(record.T, ('tmpl', 'chan'), across)  6.39 us
    unnamed x13, local copies, waits for them, and re-layouts  4.69 us
    ppermute x1, waiting for transfers between devices, shards(): raw = lax.ppermute(record.T, ('tmpl', 'chan'), across)  4.03 us
    ppermute x1, starting transfers between devices, shards(): before = lax.ppermute(tail, 'chan', up)  2.82 us
    ppermute x1, waiting for transfers between devices, shards(): before = lax.ppermute(tail, 'chan', up)  2.7 us
  transfers between devices with their start and end apart: 5, of which 2 were waited for; matrix products, arithmetic and copies ran while one was open for 1% of the time, Pallas kernels for 12%

profile of v5, /device:TPU:1, one launch (start us, length us, event | category | flops | bytes accessed | tf_op | source)
XLA Modules:
  0.0 72.3 jit_solution(5586218891237147734)
XLA Ops:
  0.0 6.4 %collective-permute-start = (f32[48,1024]{1,0:T(8,128)}, f32[48,1024]{1,0:T(8,128)S(1)}, u32[]{:S(2)}, u32[]{:S(2)}) collective-permute-start(f32[48,1024]{1,0:T(8,128)} %bitcast.16), channel_id=1, source_target_pairs={{0,0},{1,241},{2,178},{3,67},{4,52},{5,197},{6,134},{7,119},{8,120... | collective-permute-start | bytes 589832 | tf_op jit(solution)/shard_map/ppermute | solution.py:319
  6.4 0.8 %copy.10 = s32[256,30,1]{0,1,2:T(8,128)S(1)} copy(s32[256,30,1]{0,2,1:T(1,128)} %param.10) | data formatting | bytes 61440
  7.2 4.0 %collective-permute-done = f32[48,1024]{1,0:T(8,128)S(1)} collective-permute-done((f32[48,1024]{1,0:T(8,128)}, f32[48,1024]{1,0:T(8,128)S(1)}, u32[]{:S(2)}, u32[]{:S(2)}) %collective-permute-start) | collective-permute-done | bytes 196640 | tf_op jit(solution)/shard_map/ppermute | solution.py:319
  11.2 8.0 %collective-permute-start.1 = (f32[48,1024]{1,0:T(8,128)S(1)}, f32[48,1024]{1,0:T(8,128)S(1)}, u32[]{:S(2)}, u32[]{:S(2)}) collective-permute-start(f32[48,1024]{1,0:T(8,128)S(1)} %collective-permute-done), channel_id=1, source_target_pairs={{0,0},{241,240},{178,176},{67,64},{52,48},{197,192},{134,128},{119... | collective-permute-start | bytes 589832 | tf_op jit(solution)/shard_map/ppermute | solution.py:330
  19.2 0.0 copy-start
  19.2 1.4 %copy-done = bf16[1024,768]{1,0:T(8,128)(2,1)S(1)} copy-done((bf16[1024,768]{1,0:T(8,128)(2,1)S(1)}, bf16[1024,768]{1,0:T(8,128)(2,1)}, u32[]{:S(2)}) %copy-start) | copy-done | bytes 1572888
  20.6 0.0 copy-start.3
  20.6 1.1 %copy-done.3 = f32[8,30,600]{2,0,1:T(8,128)S(1)} copy-done((f32[8,30,600]{2,0,1:T(8,128)S(1)}, f32[8,30,600]{2,0,1:T(8,128)}, u32[]{:S(2)}) %copy-start.3) | copy-done | bytes 576024
  21.7 0.0 copy-start.4
  21.7 0.8 %copy-done.4 = s32[256,30]{0,1:T(8,128)S(1)} copy-done((s32[256,30]{0,1:T(8,128)S(1)}, s32[256,30]{0,1:T(8,128)}, u32[]{:S(2)}) %copy-start.4) | copy-done | bytes 30744
  22.4 0.0 copy-start.5
  22.5 0.7 copy-done.5
  23.1 1.4 %template_spectra.1 = (f32[1152,256]{1,0:T(8,128)S(1)}, s32[32,256]{1,0:T(8,128)S(1)}, s32[32,256]{1,0:T(8,128)S(1)}) custom-call(f32[240,600]{1,0:T(8,128)S(1)} %bitcast.12, s32[8,128]{1,0:T(8,128)S(1)} %bitcast.15, s32[30,256]{1,0:T(8,128)S(1)} %bitcast.13, s32[30,256]{1,0:T(8,128)S(1)} %bitcast.14, bf16[1024,768]{1,0:T(8,128)(2,1)S(1)} %copy-done), custom_call_target="tpu_custom_call" | custom-call | flops 402653184 | bytes 4194304 | tf_op jit(solution)/shard_map/template_spectra/pallas_call | solution.py:292
  24.5 0.0 collective-permute-done.1.record_ref
  24.5 1.8 %select_channels.1 = f32[32,48,256]{2,1,0:T(8,128)S(1)} custom-call(f32[48,1024]{1,0:T(8,128)S(1)} %collective-permute-done.1.record_ref, s32[32,256]{1,0:T(8,128)S(1)} %get-tuple-element.32.high_ref, s32[32,256]{1,0:T(8,128)S(1)} %get-tuple-element.33.low_ref), custom_call_target="tpu_custom_call" | custom-call | flops 1048576 | bytes 4194304 | tf_op jit(solution)/shard_map/select_channels/pallas_call | solution.py:292
  26.4 0.0 copy-start.2
  26.4 29.0 %all_to_all.5.recv_ref = f32[32,48,256]{2,1,0:T(8,128)S(1)} all-to-all(f32[32,48,256]{2,1,0:T(8,128)S(1)} %select_channels.1), channel_id=1, replica_groups=mesh['tmpl'=32,'chan'=8] {'tmpl'}, dimensions={0} | all-to-all | bytes 3145728 | tf_op jit(solution)/shard_map/all_to_all | solution.py:354
  55.4 0.0 copy-start.1
  55.5 2.8 %collective-permute-start.2 = (f32[232,256]{1,0:T(8,128)S(1)}, f32[232,256]{1,0:T(8,128)S(1)}, u32[]{:S(2)}, u32[]{:S(2)}) collective-permute-start(f32[232,256]{1,0:T(8,128)S(1)} %get-tuple-element.34), channel_id=1, source_target_pairs={{0,1},{1,2},{2,3},{3,4},{4,5},{5,6},{6,7},{7,0},{8,9},{9,10},{10,1... | collective-permute-start | bytes 712712 | tf_op jit(solution)/shard_map/ppermute | solution.py:360
  58.3 1.6 %collective-permute-start.3 = (f32[368,256]{1,0:T(8,128)S(1)}, f32[368,256]{1,0:T(8,128)S(1)}, u32[]{:S(2)}, u32[]{:S(2)}) collective-permute-start(f32[368,256]{1,0:T(8,128)S(1)} %get-tuple-element.37), channel_id=1, source_target_pairs={{1,0},{2,1},{3,2},{4,3},{5,4},{6,5},{7,6},{0,7},{9,8},{10,9},{11,1... | collective-permute-start | bytes 1130504 | tf_op jit(solution)/shard_map/ppermute | solution.py:359
  59.9 0.0 copy-done.2
  59.9 0.0 copy-done.1
  59.9 3.4 %near_segments.1.refs_1_ = f32[8,768]{1,0:T(8,128)S(1)} custom-call(s32[1]{0:T(128)} %bitcast.1.plane_ref, f32[32,48,256]{2,1,0:T(8,128)S(1)} %all_to_all.5.recv_ref, f32[1152,256]{1,0:T(8,128)S(1)} %get-tuple-element.35.refs_0_, bf16[1024,768]{1,0:T(8,128)(2,1)S(1)} %copy-done.1, bf16[1024,768]{1,0:T(8,128)(2,1)S(1)} %copy-done.2), custom_call_target="tpu_custom_call" | custom-call | flops 2818572288 | bytes 8388608 | tf_op jit(solution)/shard_map/near_segments/pallas_call | solution.py:292
  63.3 2.7 %collective-permute-done.2.tail_ref = f32[232,256]{1,0:T(8,128)S(1)} collective-permute-done((f32[232,256]{1,0:T(8,128)S(1)}, f32[232,256]{1,0:T(8,128)S(1)}, u32[]{:S(2)}, u32[]{:S(2)}) %collective-permute-start.2) | collective-permute-done | bytes 237600 | tf_op jit(solution)/shard_map/ppermute | solution.py:360
  66.0 2.0 %back_segment.1 = (f32[8,232]{1,0:T(8,128)S(1)}, f32[8,128]{1,0:T(8,128)S(1)}) custom-call(s32[1]{0:T(128)} %bitcast.1.plane_ref, f32[32,48,256]{2,1,0:T(8,128)S(1)} %all_to_all.5.recv_ref, f32[232,256]{1,0:T(8,128)S(1)} %collective-permute-done.2.tail_ref, f32[1152,256]{1,0:T(8,128)S(1)} %get-tuple-element.35.refs_0_, bf16[1024,768]{1,0:T(8,128)(2,1)S(1)} %copy-done.1, ...), custom_call_target="tpu_custom_call" | custom-call | flops 1409286144 | bytes 8388608 | tf_op jit(solution)/shard_map/back_segment/pallas_call | solution.py:292
  68.1 1.4 %collective-permute-start.4 = (f32[8,232]{1,0:T(8,128)S(1)}, f32[8,232]{1,0:T(8,128)S(1)}, u32[]{:S(2)}, u32[]{:S(2)}) collective-permute-start(f32[8,232]{1,0:T(8,128)S(1)} %get-tuple-element.38), channel_id=1, source_target_pairs={{1,0},{2,1},{3,2},{4,3},{5,4},{6,5},{7,6},{0,7},{9,8},{10,9},{11,1... | collective-permute-start | bytes 22280 | tf_op jit(solution)/shard_map/ppermute | solution.py:371
  69.5 0.0 collective-permute-done.3.head_ref
  69.5 2.1 %last_segment.1.refs_2_ = f32[8,408]{1,0:T(8,128)S(1)} custom-call(s32[1]{0:T(128)} %bitcast.1.plane_ref, f32[32,48,256]{2,1,0:T(8,128)S(1)} %all_to_all.5.recv_ref, f32[368,256]{1,0:T(8,128)S(1)} %collective-permute-done.3.head_ref, f32[1152,256]{1,0:T(8,128)S(1)} %get-tuple-element.35.refs_0_, bf16[1024,768]{1,0:T(8,128)(2,1)S(1)} %copy-done.1, ...), custom_call_target="tpu_custom_call" | custom-call | flops 1409286144 | bytes 8388608 | tf_op jit(solution)/shard_map/last_segment/pallas_call | solution.py:292
  71.6 0.0 collective-permute-done.4.refs_3_
  71.6 0.7 join.1
  (1 shorter events, 0.0 us)
Async XLA Ops:
  0.0 11.2 %collective-permute-start = (f32[48,1024]{1,0:T(8,128)}, f32[48,1024]{1,0:T(8,128)S(1)}, u32[]{:S(2)}, u32[]{:S(2)}) collective-permute-start(f32[48,1024]{1,0:T(8,128)} %bitcast.16), channel_id=1, source_target_pairs={{0,0},{1,241},{2,178},{3,67},{4,52},{5,197},{6,134},{7,119},{8,120... | collective-permute-start | bytes 589832 | tf_op jit(solution)/shard_map/ppermute | solution.py:319
  11.2 13.4 %collective-permute-start.1 = (f32[48,1024]{1,0:T(8,128)S(1)}, f32[48,1024]{1,0:T(8,128)S(1)}, u32[]{:S(2)}, u32[]{:S(2)}) collective-permute-start(f32[48,1024]{1,0:T(8,128)S(1)} %collective-permute-done), channel_id=1, source_target_pairs={{0,0},{241,240},{178,176},{67,64},{52,48},{197,192},{134,128},{119... | collective-permute-start | bytes 589832 | tf_op jit(solution)/shard_map/ppermute | solution.py:330
  19.2 1.4 %copy-start = (bf16[1024,768]{1,0:T(8,128)(2,1)S(1)}, bf16[1024,768]{1,0:T(8,128)(2,1)}, u32[]{:S(2)}) copy-start(bf16[1024,768]{1,0:T(8,128)(2,1)} %constant.8.clone.table_ref.refs_1_) | copy-start | bytes 4718596
  20.6 1.1 %copy-start.3 = (f32[8,30,600]{2,0,1:T(8,128)S(1)}, f32[8,30,600]{2,0,1:T(8,128)}, u32[]{:S(2)}) copy-start(f32[8,30,600]{2,0,1:T(8,128)} %param.9) | copy-start | bytes 1728004
  21.7 0.8 %copy-start.4 = (s32[256,30]{0,1:T(8,128)S(1)}, s32[256,30]{0,1:T(8,128)}, u32[]{:S(2)}) copy-start(s32[256,30]{0,1:T(8,128)} %param.11) | copy-start | bytes 92164
  22.4 0.7 copy-start.5
  26.4 33.5 %copy-start.2 = (bf16[1024,768]{1,0:T(8,128)(2,1)S(1)}, bf16[1024,768]{1,0:T(8,128)(2,1)}, u32[]{:S(2)}) copy-start(bf16[1024,768]{1,0:T(8,128)(2,1)} %constant.9.clone.refs_2_) | copy-start | bytes 4718596
  55.4 4.5 %copy-start.1 = (bf16[1024,768]{1,0:T(8,128)(2,1)S(1)}, bf16[1024,768]{1,0:T(8,128)(2,1)}, u32[]{:S(2)}) copy-start(bf16[1024,768]{1,0:T(8,128)(2,1)} %constant.8.clone.table_ref.refs_1_) | copy-start | bytes 4718596
  55.5 10.5 %collective-permute-start.2 = (f32[232,256]{1,0:T(8,128)S(1)}, f32[232,256]{1,0:T(8,128)S(1)}, u32[]{:S(2)}, u32[]{:S(2)}) collective-permute-start(f32[232,256]{1,0:T(8,128)S(1)} %get-tuple-element.34), channel_id=1, source_target_pairs={{0,1},{1,2},{2,3},{3,4},{4,5},{5,6},{6,7},{7,0},{8,9},{9,10},{10,1... | collective-permute-start | bytes 712712 | tf_op jit(solution)/shard_map/ppermute | solution.py:360
  58.3 11.2 %collective-permute-start.3 = (f32[368,256]{1,0:T(8,128)S(1)}, f32[368,256]{1,0:T(8,128)S(1)}, u32[]{:S(2)}, u32[]{:S(2)}) collective-permute-start(f32[368,256]{1,0:T(8,128)S(1)} %get-tuple-element.37), channel_id=1, source_target_pairs={{1,0},{2,1},{3,2},{4,3},{5,4},{6,5},{7,6},{0,7},{9,8},{10,9},{11,1... | collective-permute-start | bytes 1130504 | tf_op jit(solution)/shard_map/ppermute | solution.py:359
  68.1 3.5 %collective-permute-start.4 = (f32[8,232]{1,0:T(8,128)S(1)}, f32[8,232]{1,0:T(8,128)S(1)}, u32[]{:S(2)}, u32[]{:S(2)}) collective-permute-start(f32[8,232]{1,0:T(8,128)S(1)} %get-tuple-element.38), channel_id=1, source_target_pairs={{1,0},{2,1},{3,2},{4,3},{5,4},{6,5},{7,6},{0,7},{9,8},{10,9},{11,1... | collective-permute-start | bytes 22280 | tf_op jit(solution)/shard_map/ppermute | solution.py:371

commit v6 on v5

--- a/solution.py
+++ b/solution.py
@@ -205,23 +205,33 @@
 
 
 def window_scale(x_ref, sq_ref, lags):
-    rows = lags + TAPS
-    sq = x_ref[:rows] * x_ref[:rows]
+    span = TAPS // 8
+    starts = lags // 8 + 1
+    wide = 8 * starts
+
+    def square(group):
+        value = x_ref[8 * group : 8 * group + 8]
+        return value * value
+
+    for first in range(0, starts, 60):
+        end = min(first + 60, starts)
+        total = square(end - 1)
+        for group in range(end, first + span):
+            total = total + square(group)
+        for group in range(end - 1, first - 1, -1):
+            if group < end - 1:
+                total = total + square(group)
+            sq_ref[8 * group : 8 * group + 8] = total
+        total = jnp.zeros((8, LANES), F32)
+        for group in range(first + 1, end):
+            total = total + square(group + span - 1)
+            sq_ref[8 * group : 8 * group + 8] += total
+    sq_ref[wide : wide + 8] = jnp.zeros((8, LANES), F32)
     for step in (1, 2, 4):
-        sq_ref[:rows] = sq
-        sq_ref[rows : rows + 8] = jnp.zeros((8, LANES), F32)
-        sq = sq_ref[:rows] + sq_ref[step : rows + step]
-    total = sq[74 * 8 : 74 * 8 + lags]
-    length = 1
-    have = rows
-    at = {64: 0, 8: 64, 2: 72}
-    while length < 64:
-        have = have - 8 * length
-        sq = sq[:have] + sq[8 * length : 8 * length + have]
-        length *= 2
-        if length in at:
-            total = total + sq[8 * at[length] : 8 * at[length] + lags]
-    return lax.rsqrt(total * (1.0 / TAPS) + 1e-6)
+        total = sq_ref[:wide] + sq_ref[step : wide + step]
+        if step < 4:
+            sq_ref[:wide] = total
+    return lax.rsqrt(total[:lags] * (1.0 / TAPS) + 1e-6)
 
 
 def segments(x_ref, sq_ref, spans, spec_ref, forward_ref, back_ref):

time: 72.7 us -> 71.8 us (0.988)
  Pallas kernels: 11.5 us -> 10.1 us
    pallas_call x7, Pallas kernels: 11.5 us -> 10.1 us  [run(): pl.pallas_call(kernel, out_shape=out_shape, in_specs=[smem if i < scalars...]
  transfers between devices with their start and end apart: 5 -> 5, of which waited for: 2 -> 2; matrix products, arithmetic and copies ran while one was open for 1% -> 1% of each run, Pallas kernels for 12% -> 11%
where the time goes in v6:
time: 71.8 us; the launch traced here: 71.4 us
  blocking collectives  29 us (40%)
  starting transfers between devices  20.2 us (28%)
  Pallas kernels  10.1 us (14%)
  waiting for transfers between devices  7.24 us (10%)
  local copies, waits for them, and re-layouts  4.69 us (7%)
    all_to_all x1, blocking collectives, shards(): recv = lax.all_to_all(sent, 'tmpl', split_axis=0, concat_axis=0, tiled=True)  29 us
    pallas_call x7, Pallas kernels, run(): pl.pallas_call(kernel, out_shape=out_shape, in_specs=[smem if i < scalars...  10.1 us
    ppermute x1, starting transfers between devices, shards(): raw = lax.ppermute(raw, ('tmpl', 'chan'), along)  8.01 us
    ppermute x1, starting transfers between devices, shards(): raw = lax.ppermute(record.T, ('tmpl', 'chan'), across)  6.39 us
    unnamed x13, local copies, waits for them, and re-layouts  4.69 us
    ppermute x1, waiting for transfers between devices, shards(): raw = lax.ppermute(record.T, ('tmpl', 'chan'), across)  4.03 us
    ppermute x1, waiting for transfers between devices, shards(): before = lax.ppermute(tail, 'chan', up)  3.21 us
    ppermute x1, starting transfers between devices, shards(): before = lax.ppermute(tail, 'chan', up)  2.82 us
  transfers between devices with their start and end apart: 5, of which 2 were waited for; matrix products, arithmetic and copies ran while one was open for 1% of the time, Pallas kernels for 11%

profile of v6, /device:TPU:1, one launch (start us, length us, event | category | flops | bytes accessed | tf_op | source)
XLA Modules:
  0.0 71.4 jit_solution(11895437865056974915)
XLA Ops:
  0.0 6.4 %collective-permute-start = (f32[48,1024]{1,0:T(8,128)}, f32[48,1024]{1,0:T(8,128)S(1)}, u32[]{:S(2)}, u32[]{:S(2)}) collective-permute-start(f32[48,1024]{1,0:T(8,128)} %bitcast.16), channel_id=1, source_target_pairs={{0,0},{1,241},{2,178},{3,67},{4,52},{5,197},{6,134},{7,119},{8,120... | collective-permute-start | bytes 589832 | tf_op jit(solution)/shard_map/ppermute | solution.py:329
  6.4 0.8 %copy.10 = s32[256,30,1]{0,1,2:T(8,128)S(1)} copy(s32[256,30,1]{0,2,1:T(1,128)} %param.10) | data formatting | bytes 61440
  7.2 4.0 %collective-permute-done = f32[48,1024]{1,0:T(8,128)S(1)} collective-permute-done((f32[48,1024]{1,0:T(8,128)}, f32[48,1024]{1,0:T(8,128)S(1)}, u32[]{:S(2)}, u32[]{:S(2)}) %collective-permute-start) | collective-permute-done | bytes 196640 | tf_op jit(solution)/shard_map/ppermute | solution.py:329
  11.2 8.0 %collective-permute-start.1 = (f32[48,1024]{1,0:T(8,128)S(1)}, f32[48,1024]{1,0:T(8,128)S(1)}, u32[]{:S(2)}, u32[]{:S(2)}) collective-permute-start(f32[48,1024]{1,0:T(8,128)S(1)} %collective-permute-done), channel_id=1, source_target_pairs={{0,0},{241,240},{178,176},{67,64},{52,48},{197,192},{134,128},{119... | collective-permute-start | bytes 589832 | tf_op jit(solution)/shard_map/ppermute | solution.py:340
  19.2 0.0 copy-start
  19.2 1.4 %copy-done = bf16[1024,768]{1,0:T(8,128)(2,1)S(1)} copy-done((bf16[1024,768]{1,0:T(8,128)(2,1)S(1)}, bf16[1024,768]{1,0:T(8,128)(2,1)}, u32[]{:S(2)}) %copy-start) | copy-done | bytes 1572888
  20.6 0.0 copy-start.3
  20.6 1.1 %copy-done.3 = f32[8,30,600]{2,0,1:T(8,128)S(1)} copy-done((f32[8,30,600]{2,0,1:T(8,128)S(1)}, f32[8,30,600]{2,0,1:T(8,128)}, u32[]{:S(2)}) %copy-start.3) | copy-done | bytes 576024
  21.7 0.0 copy-start.4
  21.7 0.8 %copy-done.4 = s32[256,30]{0,1:T(8,128)S(1)} copy-done((s32[256,30]{0,1:T(8,128)S(1)}, s32[256,30]{0,1:T(8,128)}, u32[]{:S(2)}) %copy-start.4) | copy-done | bytes 30744
  22.4 0.0 copy-start.5
  22.5 0.7 copy-done.5
  23.1 1.4 %template_spectra.1 = (f32[1152,256]{1,0:T(8,128)S(1)}, s32[32,256]{1,0:T(8,128)S(1)}, s32[32,256]{1,0:T(8,128)S(1)}) custom-call(f32[240,600]{1,0:T(8,128)S(1)} %bitcast.12, s32[8,128]{1,0:T(8,128)S(1)} %bitcast.15, s32[30,256]{1,0:T(8,128)S(1)} %bitcast.13, s32[30,256]{1,0:T(8,128)S(1)} %bitcast.14, bf16[1024,768]{1,0:T(8,128)(2,1)S(1)} %copy-done), custom_call_target="tpu_custom_call" | custom-call | flops 402653184 | bytes 4194304 | tf_op jit(solution)/shard_map/template_spectra/pallas_call | solution.py:302
  24.5 0.0 collective-permute-done.1.record_ref
  24.5 1.8 %select_channels.1 = f32[32,48,256]{2,1,0:T(8,128)S(1)} custom-call(f32[48,1024]{1,0:T(8,128)S(1)} %collective-permute-done.1.record_ref, s32[32,256]{1,0:T(8,128)S(1)} %get-tuple-element.32.high_ref, s32[32,256]{1,0:T(8,128)S(1)} %get-tuple-element.33.low_ref), custom_call_target="tpu_custom_call" | custom-call | flops 1048576 | bytes 4194304 | tf_op jit(solution)/shard_map/select_channels/pallas_call | solution.py:302
  26.4 0.0 copy-start.2
  26.4 29.0 %all_to_all.5.recv_ref = f32[32,48,256]{2,1,0:T(8,128)S(1)} all-to-all(f32[32,48,256]{2,1,0:T(8,128)S(1)} %select_channels.1), channel_id=1, replica_groups=mesh['tmpl'=32,'chan'=8] {'tmpl'}, dimensions={0} | all-to-all | bytes 3145728 | tf_op jit(solution)/shard_map/all_to_all | solution.py:364
  55.4 0.0 copy-start.1
  55.5 2.8 %collective-permute-start.2 = (f32[232,256]{1,0:T(8,128)S(1)}, f32[232,256]{1,0:T(8,128)S(1)}, u32[]{:S(2)}, u32[]{:S(2)}) collective-permute-start(f32[232,256]{1,0:T(8,128)S(1)} %get-tuple-element.34), channel_id=1, source_target_pairs={{0,1},{1,2},{2,3},{3,4},{4,5},{5,6},{6,7},{7,0},{8,9},{9,10},{10,1... | collective-permute-start | bytes 712712 | tf_op jit(solution)/shard_map/ppermute | solution.py:370
  58.3 1.6 %collective-permute-start.3 = (f32[368,256]{1,0:T(8,128)S(1)}, f32[368,256]{1,0:T(8,128)S(1)}, u32[]{:S(2)}, u32[]{:S(2)}) collective-permute-start(f32[368,256]{1,0:T(8,128)S(1)} %get-tuple-element.37), channel_id=1, source_target_pairs={{1,0},{2,1},{3,2},{4,3},{5,4},{6,5},{7,6},{0,7},{9,8},{10,9},{11,1... | collective-permute-start | bytes 1130504 | tf_op jit(solution)/shard_map/ppermute | solution.py:369
  59.9 0.0 copy-done.2
  59.9 0.0 copy-done.1
  59.9 2.9 %near_segments.1.refs_1_ = f32[8,768]{1,0:T(8,128)S(1)} custom-call(s32[1]{0:T(128)} %bitcast.1.plane_ref, f32[32,48,256]{2,1,0:T(8,128)S(1)} %all_to_all.5.recv_ref, f32[1152,256]{1,0:T(8,128)S(1)} %get-tuple-element.35.refs_0_, bf16[1024,768]{1,0:T(8,128)(2,1)S(1)} %copy-done.1, bf16[1024,768]{1,0:T(8,128)(2,1)S(1)} %copy-done.2), custom_call_target="tpu_custom_call" | custom-call | flops 2818572288 | bytes 8388608 | tf_op jit(solution)/shard_map/near_segments/pallas_call | solution.py:302
  62.8 3.2 %collective-permute-done.2.tail_ref = f32[232,256]{1,0:T(8,128)S(1)} collective-permute-done((f32[232,256]{1,0:T(8,128)S(1)}, f32[232,256]{1,0:T(8,128)S(1)}, u32[]{:S(2)}, u32[]{:S(2)}) %collective-permute-start.2) | collective-permute-done | bytes 237600 | tf_op jit(solution)/shard_map/ppermute | solution.py:370
  66.0 1.6 %back_segment.1 = (f32[8,232]{1,0:T(8,128)S(1)}, f32[8,128]{1,0:T(8,128)S(1)}) custom-call(s32[1]{0:T(128)} %bitcast.1.plane_ref, f32[32,48,256]{2,1,0:T(8,128)S(1)} %all_to_all.5.recv_ref, f32[232,256]{1,0:T(8,128)S(1)} %collective-permute-done.2.tail_ref, f32[1152,256]{1,0:T(8,128)S(1)} %get-tuple-element.35.refs_0_, bf16[1024,768]{1,0:T(8,128)(2,1)S(1)} %copy-done.1, ...), custom_call_target="tpu_custom_call" | custom-call | flops 1409286144 | bytes 8388608 | tf_op jit(solution)/shard_map/back_segment/pallas_call | solution.py:302
  67.6 1.4 %collective-permute-start.4 = (f32[8,232]{1,0:T(8,128)S(1)}, f32[8,232]{1,0:T(8,128)S(1)}, u32[]{:S(2)}, u32[]{:S(2)}) collective-permute-start(f32[8,232]{1,0:T(8,128)S(1)} %get-tuple-element.38), channel_id=1, source_target_pairs={{1,0},{2,1},{3,2},{4,3},{5,4},{6,5},{7,6},{0,7},{9,8},{10,9},{11,1... | collective-permute-start | bytes 22280 | tf_op jit(solution)/shard_map/ppermute | solution.py:381
  69.1 0.0 collective-permute-done.3.head_ref
  69.1 1.6 %last_segment.1.refs_2_ = f32[8,408]{1,0:T(8,128)S(1)} custom-call(s32[1]{0:T(128)} %bitcast.1.plane_ref, f32[32,48,256]{2,1,0:T(8,128)S(1)} %all_to_all.5.recv_ref, f32[368,256]{1,0:T(8,128)S(1)} %collective-permute-done.3.head_ref, f32[1152,256]{1,0:T(8,128)S(1)} %get-tuple-element.35.refs_0_, bf16[1024,768]{1,0:T(8,128)(2,1)S(1)} %copy-done.1, ...), custom_call_target="tpu_custom_call" | custom-call | flops 1409286144 | bytes 8388608 | tf_op jit(solution)/shard_map/last_segment/pallas_call | solution.py:302
  70.7 0.0 collective-permute-done.4.refs_3_
  70.7 0.7 join.1
  (1 shorter events, 0.0 us)
Async XLA Ops:
  0.0 11.2 %collective-permute-start = (f32[48,1024]{1,0:T(8,128)}, f32[48,1024]{1,0:T(8,128)S(1)}, u32[]{:S(2)}, u32[]{:S(2)}) collective-permute-start(f32[48,1024]{1,0:T(8,128)} %bitcast.16), channel_id=1, source_target_pairs={{0,0},{1,241},{2,178},{3,67},{4,52},{5,197},{6,134},{7,119},{8,120... | collective-permute-start | bytes 589832 | tf_op jit(solution)/shard_map/ppermute | solution.py:329
  11.2 13.4 %collective-permute-start.1 = (f32[48,1024]{1,0:T(8,128)S(1)}, f32[48,1024]{1,0:T(8,128)S(1)}, u32[]{:S(2)}, u32[]{:S(2)}) collective-permute-start(f32[48,1024]{1,0:T(8,128)S(1)} %collective-permute-done), channel_id=1, source_target_pairs={{0,0},{241,240},{178,176},{67,64},{52,48},{197,192},{134,128},{119... | collective-permute-start | bytes 589832 | tf_op jit(solution)/shard_map/ppermute | solution.py:340
  19.2 1.4 %copy-start = (bf16[1024,768]{1,0:T(8,128)(2,1)S(1)}, bf16[1024,768]{1,0:T(8,128)(2,1)}, u32[]{:S(2)}) copy-start(bf16[1024,768]{1,0:T(8,128)(2,1)} %constant.8.clone.table_ref.refs_1_) | copy-start | bytes 4718596
  20.6 1.1 %copy-start.3 = (f32[8,30,600]{2,0,1:T(8,128)S(1)}, f32[8,30,600]{2,0,1:T(8,128)}, u32[]{:S(2)}) copy-start(f32[8,30,600]{2,0,1:T(8,128)} %param.9) | copy-start | bytes 1728004
  21.7 0.8 %copy-start.4 = (s32[256,30]{0,1:T(8,128)S(1)}, s32[256,30]{0,1:T(8,128)}, u32[]{:S(2)}) copy-start(s32[256,30]{0,1:T(8,128)} %param.11) | copy-start | bytes 92164
  22.4 0.7 copy-start.5
  26.4 33.5 %copy-start.2 = (bf16[1024,768]{1,0:T(8,128)(2,1)S(1)}, bf16[1024,768]{1,0:T(8,128)(2,1)}, u32[]{:S(2)}) copy-start(bf16[1024,768]{1,0:T(8,128)(2,1)} %constant.9.clone.refs_2_) | copy-start | bytes 4718596
  55.4 4.5 %copy-start.1 = (bf16[1024,768]{1,0:T(8,128)(2,1)S(1)}, bf16[1024,768]{1,0:T(8,128)(2,1)}, u32[]{:S(2)}) copy-start(bf16[1024,768]{1,0:T(8,128)(2,1)} %constant.8.clone.table_ref.refs_1_) | copy-start | bytes 4718596
  55.5 10.5 %collective-permute-start.2 = (f32[232,256]{1,0:T(8,128)S(1)}, f32[232,256]{1,0:T(8,128)S(1)}, u32[]{:S(2)}, u32[]{:S(2)}) collective-permute-start(f32[232,256]{1,0:T(8,128)S(1)} %get-tuple-element.34), channel_id=1, source_target_pairs={{0,1},{1,2},{2,3},{3,4},{4,5},{5,6},{6,7},{7,0},{8,9},{9,10},{10,1... | collective-permute-start | bytes 712712 | tf_op jit(solution)/shard_map/ppermute | solution.py:370
  58.3 10.8 %collective-permute-start.3 = (f32[368,256]{1,0:T(8,128)S(1)}, f32[368,256]{1,0:T(8,128)S(1)}, u32[]{:S(2)}, u32[]{:S(2)}) collective-permute-start(f32[368,256]{1,0:T(8,128)S(1)} %get-tuple-element.37), channel_id=1, source_target_pairs={{1,0},{2,1},{3,2},{4,3},{5,4},{6,5},{7,6},{0,7},{9,8},{10,9},{11,1... | collective-permute-start | bytes 1130504 | tf_op jit(solution)/shard_map/ppermute | solution.py:369
  67.6 3.1 %collective-permute-start.4 = (f32[8,232]{1,0:T(8,128)S(1)}, f32[8,232]{1,0:T(8,128)S(1)}, u32[]{:S(2)}, u32[]{:S(2)}) collective-permute-start(f32[8,232]{1,0:T(8,128)S(1)} %get-tuple-element.38), channel_id=1, source_target_pairs={{1,0},{2,1},{3,2},{4,3},{5,4},{6,5},{7,6},{0,7},{9,8},{10,9},{11,1... | collective-permute-start | bytes 22280 | tf_op jit(solution)/shard_map/ppermute | solution.py:381

commit v7 on v6

--- a/solution.py
+++ b/solution.py
@@ -204,13 +204,13 @@
     load_rows(recv_ref, plane, tail_ref, total - BACK, BACK, 0)
 
 
-def window_scale(x_ref, sq_ref, lags):
+def window_scale(rows, sq_ref, lags):
     span = TAPS // 8
     starts = lags // 8 + 1
     wide = 8 * starts
 
     def square(group):
-        value = x_ref[8 * group : 8 * group + 8]
+        value = rows(8 * group, 8)
         return value * value
 
     for first in range(0, starts, 60):
@@ -234,12 +234,12 @@
     return lax.rsqrt(total[:lags] * (1.0 / TAPS) + 1e-6)
 
 
-def segments(x_ref, sq_ref, spans, spec_ref, forward_ref, back_ref):
-    scale = window_scale(x_ref, sq_ref, sum(spans))
+def segments(rows, sq_ref, spans, spec_ref, forward_ref, back_ref):
+    scale = window_scale(rows, sq_ref, sum(spans))
     stacks = []
     base = 0
     for lags in spans:
-        pieces = [x_ref[at : at + QUARTER] for at in range(base, base + 4 * QUARTER, QUARTER)]
+        pieces = [rows(at, QUARTER) for at in range(base, base + 4 * QUARTER, QUARTER)]
         spectra = transform(pieces, forward_ref)
         parts = []
         for part, spectrum in enumerate(spectra):
@@ -261,30 +261,43 @@
     return stacks
 
 
+def chained(refs, first):
+    def rows(at, count):
+        at += first
+        parts = []
+        for ref in refs:
+            size = ref.shape[0]
+            low, high = min(at, size), min(at + count, size)
+            if low < high:
+                parts.append(ref[low:high])
+                count -= high - low
+            at = max(at - size, 0)
+        if count:
+            parts.append(jnp.zeros((count, LANES), F32))
+        return parts[0] if len(parts) == 1 else jnp.concatenate(parts, axis=0)
+
+    return rows
+
+
 def near_kernel(plane_ref, recv_ref, *refs):
     *refs, out_ref, x_ref, sq_ref = refs
-    load_rows(recv_ref, plane_ref[0], x_ref, KEEP, HOP + 2 * HALF, 0)
-    one, two = segments(x_ref, sq_ref, (HOP, HOP), *refs)
+    load_rows(recv_ref, plane_ref[0], x_ref, 0, x_ref.shape[0], 0)
+    one, two = segments(chained([x_ref], KEEP), sq_ref, (HOP, HOP), *refs)
     out_ref[:, :HOP] = one
     out_ref[:, HOP:] = two
 
 
-def back_kernel(plane_ref, recv_ref, tail_ref, *refs):
-    *refs, send_ref, keep_ref, x_ref, sq_ref = refs
-    x_ref[:BACK] = tail_ref[...]
-    load_rows(recv_ref, plane_ref[0], x_ref, 0, 2 * HALF - BACK, BACK)
-    (stack,) = segments(x_ref, sq_ref, (BACK + KEEP,), *refs)
+def back_kernel(x_ref, tail_ref, *refs):
+    *refs, send_ref, keep_ref, sq_ref = refs
+    (stack,) = segments(chained([tail_ref, x_ref], 0), sq_ref, (BACK + KEEP,), *refs)
     send_ref[...] = stack[:, :BACK]
     keep_ref[...] = stack[:, BACK:]
 
 
-def last_kernel(plane_ref, recv_ref, head_ref, *refs):
-    *refs, out_ref, x_ref, sq_ref = refs
-    own = recv_ref.shape[0] * recv_ref.shape[1] - KEEP - 2 * HOP
-    load_rows(recv_ref, plane_ref[0], x_ref, KEEP + 2 * HOP, own, 0)
-    x_ref[own : own + NEXT] = head_ref[...]
-    x_ref[own + NEXT : 2 * HALF] = jnp.zeros((2 * HALF - own - NEXT, LANES), F32)
-    (out_ref[...],) = segments(x_ref, sq_ref, (MOST,), *refs)
+def last_kernel(x_ref, head_ref, *refs):
+    *refs, out_ref, sq_ref = refs
+    rows = chained([x_ref, head_ref], KEEP + 2 * HOP)
+    (out_ref[...],) = segments(rows, sq_ref, (MOST,), *refs)
 
 
 def join_kernel(*refs):
@@ -371,15 +384,19 @@
     flops = 2 * 3 * (2 * HALF * HALF + HOP * 2 * HALF) * LANES
     shared = (specs, forward, back)
 
-    def part(kernel, count, name, *lags):
-        lines = pltpu.VMEM(((count - 1) * HOP + 2 * HALF + 8, LANES), F32)
-        shape = tuple(jax.ShapeDtypeStruct((BLOCK, n), F32) for n in lags)
-        return call(kernel, shape, [lines, lines], count * flops, 8 << 20, 24, name, 1)
-
-    (middle,) = part(near_kernel, 2, "near_segments", 2 * HOP)(plane, recv, *shared)
-    early, keep = part(back_kernel, 1, "back_segment", BACK, KEEP)(plane, recv, before, *shared)
+    def part(kernel, count, name, scalars, *shapes):
+        shapes = tuple(jax.ShapeDtypeStruct(shape, F32) for shape in shapes)
+        sums = [pltpu.VMEM((count * MOST + 16, LANES), F32)]
+        return call(kernel, shapes, sums, count * flops, 8 << 20, 24, name, scalars)
+
+    middle, own = part(
+        near_kernel, 2, "near_segments", 1, (BLOCK, 2 * HOP), (blocks * span, LANES)
+    )(plane, recv, *shared)
+    early, keep = part(back_kernel, 1, "back_segment", 0, (BLOCK, BACK), (BLOCK, KEEP))(
+        own, before, *shared
+    )
     given = lax.ppermute(early, "chan", down)
-    (last,) = part(last_kernel, 1, "last_segment", MOST)(plane, recv, after, *shared)
+    (last,) = part(last_kernel, 1, "last_segment", 0, (BLOCK, MOST))(own, after, *shared)
     joined = jax.ShapeDtypeStruct((BLOCK, blocks * span), F32)
     return call(join_kernel, joined, [], 0, 1 << 17, 8, "join")(keep, middle, last, given)
 

time: 71.8 us -> 71.8 us (level)
  no operation moved by 1% of the time
where the time goes in v7:
time: 71.8 us; the launch traced here: 71.3 us
  blocking collectives  29 us (40%)
  starting transfers between devices  20.2 us (28%)
  Pallas kernels  10.2 us (14%)
  waiting for transfers between devices  7.1 us (10%)
  local copies, waits for them, and re-layouts  4.69 us (7%)
    all_to_all x1, blocking collectives, shards(): recv = lax.all_to_all(sent, 'tmpl', split_axis=0, concat_axis=0, tiled=True)  29 us
    pallas_call x7, Pallas kernels, run(): pl.pallas_call(kernel, out_shape=out_shape, in_specs=[smem if i < scalars...  10.2 us
    ppermute x1, starting transfers between devices, shards(): raw = lax.ppermute(raw, ('tmpl', 'chan'), along)  8.01 us
    ppermute x1, starting transfers between devices, shards(): raw = lax.ppermute(record.T, ('tmpl', 'chan'), across)  6.39 us
    unnamed x13, local copies, waits for them, and re-layouts  4.69 us
    ppermute x1, waiting for transfers between devices, shards(): raw = lax.ppermute(record.T, ('tmpl', 'chan'), across)  4.03 us
    ppermute x1, waiting for transfers between devices, shards(): before = lax.ppermute(tail, 'chan', up)  3.07 us
    ppermute x1, starting transfers between devices, shards(): before = lax.ppermute(tail, 'chan', up)  2.82 us
  transfers between devices with their start and end apart: 5, of which 2 were waited for; matrix products, arithmetic and copies ran while one was open for 1% of the time, Pallas kernels for 11%

profile of v7, /device:TPU:1, one launch (start us, length us, event | category | flops | bytes accessed | tf_op | source)
XLA Modules:
  0.0 71.3 jit_solution(6888251846359076290)
XLA Ops:
  0.0 6.4 %collective-permute-start = (f32[48,1024]{1,0:T(8,128)}, f32[48,1024]{1,0:T(8,128)S(1)}, u32[]{:S(2)}, u32[]{:S(2)}) collective-permute-start(f32[48,1024]{1,0:T(8,128)} %bitcast.16), channel_id=1, source_target_pairs={{0,0},{1,241},{2,178},{3,67},{4,52},{5,197},{6,134},{7,119},{8,120... | collective-permute-start | bytes 589832 | tf_op jit(solution)/shard_map/ppermute | solution.py:342
  6.4 0.8 %copy.10 = s32[256,30,1]{0,1,2:T(8,128)S(1)} copy(s32[256,30,1]{0,2,1:T(1,128)} %param.10) | data formatting | bytes 61440
  7.2 4.0 %collective-permute-done = f32[48,1024]{1,0:T(8,128)S(1)} collective-permute-done((f32[48,1024]{1,0:T(8,128)}, f32[48,1024]{1,0:T(8,128)S(1)}, u32[]{:S(2)}, u32[]{:S(2)}) %collective-permute-start) | collective-permute-done | bytes 196640 | tf_op jit(solution)/shard_map/ppermute | solution.py:342
  11.2 8.0 %collective-permute-start.1 = (f32[48,1024]{1,0:T(8,128)S(1)}, f32[48,1024]{1,0:T(8,128)S(1)}, u32[]{:S(2)}, u32[]{:S(2)}) collective-permute-start(f32[48,1024]{1,0:T(8,128)S(1)} %collective-permute-done), channel_id=1, source_target_pairs={{0,0},{241,240},{178,176},{67,64},{52,48},{197,192},{134,128},{119... | collective-permute-start | bytes 589832 | tf_op jit(solution)/shard_map/ppermute | solution.py:353
  19.2 0.0 copy-start
  19.2 1.4 %copy-done = bf16[1024,768]{1,0:T(8,128)(2,1)S(1)} copy-done((bf16[1024,768]{1,0:T(8,128)(2,1)S(1)}, bf16[1024,768]{1,0:T(8,128)(2,1)}, u32[]{:S(2)}) %copy-start) | copy-done | bytes 1572888
  20.6 0.0 copy-start.3
  20.6 1.1 %copy-done.3 = f32[8,30,600]{2,0,1:T(8,128)S(1)} copy-done((f32[8,30,600]{2,0,1:T(8,128)S(1)}, f32[8,30,600]{2,0,1:T(8,128)}, u32[]{:S(2)}) %copy-start.3) | copy-done | bytes 576024
  21.7 0.0 copy-start.4
  21.7 0.8 %copy-done.4 = s32[256,30]{0,1:T(8,128)S(1)} copy-done((s32[256,30]{0,1:T(8,128)S(1)}, s32[256,30]{0,1:T(8,128)}, u32[]{:S(2)}) %copy-start.4) | copy-done | bytes 30744
  22.4 0.0 copy-start.5
  22.5 0.7 copy-done.5
  23.1 1.4 %template_spectra.1 = (f32[1152,256]{1,0:T(8,128)S(1)}, s32[32,256]{1,0:T(8,128)S(1)}, s32[32,256]{1,0:T(8,128)S(1)}) custom-call(f32[240,600]{1,0:T(8,128)S(1)} %bitcast.12, s32[8,128]{1,0:T(8,128)S(1)} %bitcast.15, s32[30,256]{1,0:T(8,128)S(1)} %bitcast.13, s32[30,256]{1,0:T(8,128)S(1)} %bitcast.14, bf16[1024,768]{1,0:T(8,128)(2,1)S(1)} %copy-done), custom_call_target="tpu_custom_call" | custom-call | flops 402653184 | bytes 4194304 | tf_op jit(solution)/shard_map/template_spectra/pallas_call | solution.py:315
  24.5 0.0 collective-permute-done.1.record_ref
  24.5 1.8 %select_channels.1 = f32[32,48,256]{2,1,0:T(8,128)S(1)} custom-call(f32[48,1024]{1,0:T(8,128)S(1)} %collective-permute-done.1.record_ref, s32[32,256]{1,0:T(8,128)S(1)} %get-tuple-element.34.high_ref, s32[32,256]{1,0:T(8,128)S(1)} %get-tuple-element.35.low_ref), custom_call_target="tpu_custom_call" | custom-call | flops 1048576 | bytes 4194304 | tf_op jit(solution)/shard_map/select_channels/pallas_call | solution.py:315
  26.4 0.0 copy-start.2
  26.4 29.0 %all_to_all.5.recv_ref = f32[32,48,256]{2,1,0:T(8,128)S(1)} all-to-all(f32[32,48,256]{2,1,0:T(8,128)S(1)} %select_channels.1), channel_id=1, replica_groups=mesh['tmpl'=32,'chan'=8] {'tmpl'}, dimensions={0} | all-to-all | bytes 3145728 | tf_op jit(solution)/shard_map/all_to_all | solution.py:377
  55.4 0.0 copy-start.1
  55.5 2.8 %collective-permute-start.2 = (f32[232,256]{1,0:T(8,128)S(1)}, f32[232,256]{1,0:T(8,128)S(1)}, u32[]{:S(2)}, u32[]{:S(2)}) collective-permute-start(f32[232,256]{1,0:T(8,128)S(1)} %get-tuple-element.38), channel_id=1, source_target_pairs={{0,1},{1,2},{2,3},{3,4},{4,5},{5,6},{6,7},{7,0},{8,9},{9,10},{10,1... | collective-permute-start | bytes 712712 | tf_op jit(solution)/shard_map/ppermute | solution.py:383
  58.3 1.6 %collective-permute-start.3 = (f32[368,256]{1,0:T(8,128)S(1)}, f32[368,256]{1,0:T(8,128)S(1)}, u32[]{:S(2)}, u32[]{:S(2)}) collective-permute-start(f32[368,256]{1,0:T(8,128)S(1)} %get-tuple-element.41), channel_id=1, source_target_pairs={{1,0},{2,1},{3,2},{4,3},{5,4},{6,5},{7,6},{0,7},{9,8},{10,9},{11,1... | collective-permute-start | bytes 1130504 | tf_op jit(solution)/shard_map/ppermute | solution.py:382
  59.9 0.0 copy-done.2
  59.9 0.0 copy-done.1
  59.9 3.1 %near_segments.1 = (f32[8,768]{1,0:T(8,128)S(1)}, f32[1536,256]{1,0:T(8,128)S(1)}) custom-call(s32[1]{0:T(128)} %bitcast.1.plane_ref, f32[32,48,256]{2,1,0:T(8,128)S(1)} %all_to_all.5.recv_ref, f32[1152,256]{1,0:T(8,128)S(1)} %get-tuple-element.36.refs_0_, bf16[1024,768]{1,0:T(8,128)(2,1)S(1)} %copy-done.1, bf16[1024,768]{1,0:T(8,128)(2,1)S(1)} %copy-done.2), custom_call_target="tpu_custom_call" | custom-call | flops 2818572288 | bytes 8388608 | tf_op jit(solution)/shard_map/near_segments/pallas_call | solution.py:315
  63.0 3.1 %collective-permute-done.2.tail_ref = f32[232,256]{1,0:T(8,128)S(1)} collective-permute-done((f32[232,256]{1,0:T(8,128)S(1)}, f32[232,256]{1,0:T(8,128)S(1)}, u32[]{:S(2)}, u32[]{:S(2)}) %collective-permute-start.2) | collective-permute-done | bytes 237600 | tf_op jit(solution)/shard_map/ppermute | solution.py:383
  66.0 1.6 %back_segment.1 = (f32[8,232]{1,0:T(8,128)S(1)}, f32[8,128]{1,0:T(8,128)S(1)}) custom-call(f32[1536,256]{1,0:T(8,128)S(1)} %get-tuple-element.37.x_ref, f32[232,256]{1,0:T(8,128)S(1)} %collective-permute-done.2.tail_ref, f32[1152,256]{1,0:T(8,128)S(1)} %get-tuple-element.36.refs_0_, bf16[1024,768]{1,0:T(8,128)(2,1)S(1)} %copy-done.1, ...), custom_call_target="tpu_custom_call" | custom-call | flops 1409286144 | bytes 8388608 | tf_op jit(solution)/shard_map/back_segment/pallas_call | solution.py:315
  67.6 1.4 %collective-permute-start.4 = (f32[8,232]{1,0:T(8,128)S(1)}, f32[8,232]{1,0:T(8,128)S(1)}, u32[]{:S(2)}, u32[]{:S(2)}) collective-permute-start(f32[8,232]{1,0:T(8,128)S(1)} %get-tuple-element.42), channel_id=1, source_target_pairs={{1,0},{2,1},{3,2},{4,3},{5,4},{6,5},{7,6},{0,7},{9,8},{10,9},{11,1... | collective-permute-start | bytes 22280 | tf_op jit(solution)/shard_map/ppermute | solution.py:398
  69.0 0.0 collective-permute-done.3.head_ref
  69.0 1.6 %last_segment.1.refs_2_ = f32[8,408]{1,0:T(8,128)S(1)} custom-call(f32[1536,256]{1,0:T(8,128)S(1)} %get-tuple-element.37.x_ref, f32[368,256]{1,0:T(8,128)S(1)} %collective-permute-done.3.head_ref, f32[1152,256]{1,0:T(8,128)S(1)} %get-tuple-element.36.refs_0_, bf16[1024,768]{1,0:T(8,128)(2,1)S(1)} %copy-done.1, bf16[1024,768]{1,0:T(8,128)(2,1)S(1)} %copy-done.2), custom_call_target="tpu_custom_call" | custom-call | flops 1409286144 | bytes 8388608 | tf_op jit(solution)/shard_map/last_segment/pallas_call | solution.py:315
  70.6 0.0 collective-permute-done.4.refs_3_
  70.7 0.7 join.1
  (1 shorter events, 0.0 us)
Async XLA Ops:
  0.0 11.2 %collective-permute-start = (f32[48,1024]{1,0:T(8,128)}, f32[48,1024]{1,0:T(8,128)S(1)}, u32[]{:S(2)}, u32[]{:S(2)}) collective-permute-start(f32[48,1024]{1,0:T(8,128)} %bitcast.16), channel_id=1, source_target_pairs={{0,0},{1,241},{2,178},{3,67},{4,52},{5,197},{6,134},{7,119},{8,120... | collective-permute-start | bytes 589832 | tf_op jit(solution)/shard_map/ppermute | solution.py:342
  11.2 13.4 %collective-permute-start.1 = (f32[48,1024]{1,0:T(8,128)S(1)}, f32[48,1024]{1,0:T(8,128)S(1)}, u32[]{:S(2)}, u32[]{:S(2)}) collective-permute-start(f32[48,1024]{1,0:T(8,128)S(1)} %collective-permute-done), channel_id=1, source_target_pairs={{0,0},{241,240},{178,176},{67,64},{52,48},{197,192},{134,128},{119... | collective-permute-start | bytes 589832 | tf_op jit(solution)/shard_map/ppermute | solution.py:353
  19.2 1.4 %copy-start = (bf16[1024,768]{1,0:T(8,128)(2,1)S(1)}, bf16[1024,768]{1,0:T(8,128)(2,1)}, u32[]{:S(2)}) copy-start(bf16[1024,768]{1,0:T(8,128)(2,1)} %constant.8.clone.table_ref.refs_1_) | copy-start | bytes 4718596
  20.6 1.1 %copy-start.3 = (f32[8,30,600]{2,0,1:T(8,128)S(1)}, f32[8,30,600]{2,0,1:T(8,128)}, u32[]{:S(2)}) copy-start(f32[8,30,600]{2,0,1:T(8,128)} %param.9) | copy-start | bytes 1728004
  21.7 0.8 %copy-start.4 = (s32[256,30]{0,1:T(8,128)S(1)}, s32[256,30]{0,1:T(8,128)}, u32[]{:S(2)}) copy-start(s32[256,30]{0,1:T(8,128)} %param.11) | copy-start | bytes 92164
  22.4 0.7 copy-start.5
  26.4 33.5 %copy-start.2 = (bf16[1024,768]{1,0:T(8,128)(2,1)S(1)}, bf16[1024,768]{1,0:T(8,128)(2,1)}, u32[]{:S(2)}) copy-start(bf16[1024,768]{1,0:T(8,128)(2,1)} %constant.9.clone.refs_2_) | copy-start | bytes 4718596
  55.4 4.5 %copy-start.1 = (bf16[1024,768]{1,0:T(8,128)(2,1)S(1)}, bf16[1024,768]{1,0:T(8,128)(2,1)}, u32[]{:S(2)}) copy-start(bf16[1024,768]{1,0:T(8,128)(2,1)} %constant.8.clone.table_ref.refs_1_) | copy-start | bytes 4718596
  55.5 10.5 %collective-permute-start.2 = (f32[232,256]{1,0:T(8,128)S(1)}, f32[232,256]{1,0:T(8,128)S(1)}, u32[]{:S(2)}, u32[]{:S(2)}) collective-permute-start(f32[232,256]{1,0:T(8,128)S(1)} %get-tuple-element.38), channel_id=1, source_target_pairs={{0,1},{1,2},{2,3},{3,4},{4,5},{5,6},{6,7},{7,0},{8,9},{9,10},{10,1... | collective-permute-start | bytes 712712 | tf_op jit(solution)/shard_map/ppermute | solution.py:383
  58.3 10.7 %collective-permute-start.3 = (f32[368,256]{1,0:T(8,128)S(1)}, f32[368,256]{1,0:T(8,128)S(1)}, u32[]{:S(2)}, u32[]{:S(2)}) collective-permute-start(f32[368,256]{1,0:T(8,128)S(1)} %get-tuple-element.41), channel_id=1, source_target_pairs={{1,0},{2,1},{3,2},{4,3},{5,4},{6,5},{7,6},{0,7},{9,8},{10,9},{11,1... | collective-permute-start | bytes 1130504 | tf_op jit(solution)/shard_map/ppermute | solution.py:382
  67.6 3.0 %collective-permute-start.4 = (f32[8,232]{1,0:T(8,128)S(1)}, f32[8,232]{1,0:T(8,128)S(1)}, u32[]{:S(2)}, u32[]{:S(2)}) collective-permute-start(f32[8,232]{1,0:T(8,128)S(1)} %get-tuple-element.42), channel_id=1, source_target_pairs={{1,0},{2,1},{3,2},{4,3},{5,4},{6,5},{7,6},{0,7},{9,8},{10,9},{11,1... | collective-permute-start | bytes 22280 | tf_op jit(solution)/shard_map/ppermute | solution.py:398

commit v8 on v7

--- a/solution.py
+++ b/solution.py
@@ -171,11 +171,13 @@
         low = low_ref[block : block + 1, :].astype(F32).astype(BF16)
         hot = jnp.where(row == low, one, zero)
         both = jnp.dot(parts, hot, preferred_element_type=F32)
-        picked = jnp.zeros((span, LANES), F32)
-        for g in range(channels // width):
-            at = 2 * span * g
-            quarter = both[at : at + span] + both[at + span : at + 2 * span]
-            picked = jnp.where(high == g, quarter, picked)
+        quarters = [
+            both[at : at + span] + both[at + span : at + 2 * span]
+            for at in range(0, both.shape[0], 2 * span)
+        ]
+        odd, late = jnp.bitwise_and(high, 1) == 1, high >= 2
+        early = jnp.where(odd, quarters[1], quarters[0])
+        picked = jnp.where(late, jnp.where(odd, quarters[3], quarters[2]), early)
         out_ref[block] = picked
 
 

time: 71.8 us -> 71.7 us (level)
  no operation moved by 1% of the time
where the time goes in v8:
time: 71.7 us; the launch traced here: 71.3 us
  blocking collectives  29 us (40%)
  starting transfers between devices  20.2 us (28%)
  Pallas kernels  10.2 us (14%)
  waiting for transfers between devices  7.1 us (10%)
  local copies, waits for them, and re-layouts  4.69 us (7%)
    all_to_all x1, blocking collectives, shards(): recv = lax.all_to_all(sent, 'tmpl', split_axis=0, concat_axis=0, tiled=True)  29 us
    pallas_call x7, Pallas kernels, run(): pl.pallas_call(kernel, out_shape=out_shape, in_specs=[smem if i < scalars...  10.2 us
    ppermute x1, starting transfers between devices, shards(): raw = lax.ppermute(raw, ('tmpl', 'chan'), along)  8.01 us
    ppermute x1, starting transfers between devices, shards(): raw = lax.ppermute(record.T, ('tmpl', 'chan'), across)  6.39 us
    unnamed x13, local copies, waits for them, and re-layouts  4.69 us
    ppermute x1, waiting for transfers between devices, shards(): raw = lax.ppermute(record.T, ('tmpl', 'chan'), across)  4.03 us
    ppermute x1, waiting for transfers between devices, shards(): before = lax.ppermute(tail, 'chan', up)  3.07 us
    ppermute x1, starting transfers between devices, shards(): before = lax.ppermute(tail, 'chan', up)  2.82 us
  transfers between devices with their start and end apart: 5, of which 2 were waited for; matrix products, arithmetic and copies ran while one was open for 1% of the time, Pallas kernels for 11%

profile of v8, /device:TPU:1, one launch (start us, length us, event | category | flops | bytes accessed | tf_op | source)
XLA Modules:
  0.0 71.3 jit_solution(14620655784284189023)
XLA Ops:
  0.0 6.4 %collective-permute-start = (f32[48,1024]{1,0:T(8,128)}, f32[48,1024]{1,0:T(8,128)S(1)}, u32[]{:S(2)}, u32[]{:S(2)}) collective-permute-start(f32[48,1024]{1,0:T(8,128)} %bitcast.16), channel_id=1, source_target_pairs={{0,0},{1,241},{2,178},{3,67},{4,52},{5,197},{6,134},{7,119},{8,120... | collective-permute-start | bytes 589832 | tf_op jit(solution)/shard_map/ppermute | solution.py:344
  6.4 0.8 %copy.10 = s32[256,30,1]{0,1,2:T(8,128)S(1)} copy(s32[256,30,1]{0,2,1:T(1,128)} %param.10) | data formatting | bytes 61440
  7.2 4.0 %collective-permute-done = f32[48,1024]{1,0:T(8,128)S(1)} collective-permute-done((f32[48,1024]{1,0:T(8,128)}, f32[48,1024]{1,0:T(8,128)S(1)}, u32[]{:S(2)}, u32[]{:S(2)}) %collective-permute-start) | collective-permute-done | bytes 196640 | tf_op jit(solution)/shard_map/ppermute | solution.py:344
  11.2 8.0 %collective-permute-start.1 = (f32[48,1024]{1,0:T(8,128)S(1)}, f32[48,1024]{1,0:T(8,128)S(1)}, u32[]{:S(2)}, u32[]{:S(2)}) collective-permute-start(f32[48,1024]{1,0:T(8,128)S(1)} %collective-permute-done), channel_id=1, source_target_pairs={{0,0},{241,240},{178,176},{67,64},{52,48},{197,192},{134,128},{119... | collective-permute-start | bytes 589832 | tf_op jit(solution)/shard_map/ppermute | solution.py:355
  19.2 0.0 copy-start
  19.2 1.4 %copy-done = bf16[1024,768]{1,0:T(8,128)(2,1)S(1)} copy-done((bf16[1024,768]{1,0:T(8,128)(2,1)S(1)}, bf16[1024,768]{1,0:T(8,128)(2,1)}, u32[]{:S(2)}) %copy-start) | copy-done | bytes 1572888
  20.6 0.0 copy-start.3
  20.6 1.1 %copy-done.3 = f32[8,30,600]{2,0,1:T(8,128)S(1)} copy-done((f32[8,30,600]{2,0,1:T(8,128)S(1)}, f32[8,30,600]{2,0,1:T(8,128)}, u32[]{:S(2)}) %copy-start.3) | copy-done | bytes 576024
  21.7 0.0 copy-start.4
  21.7 0.8 %copy-done.4 = s32[256,30]{0,1:T(8,128)S(1)} copy-done((s32[256,30]{0,1:T(8,128)S(1)}, s32[256,30]{0,1:T(8,128)}, u32[]{:S(2)}) %copy-start.4) | copy-done | bytes 30744
  22.4 0.0 copy-start.5
  22.5 0.7 copy-done.5
  23.1 1.4 %template_spectra.1 = (f32[1152,256]{1,0:T(8,128)S(1)}, s32[32,256]{1,0:T(8,128)S(1)}, s32[32,256]{1,0:T(8,128)S(1)}) custom-call(f32[240,600]{1,0:T(8,128)S(1)} %bitcast.12, s32[8,128]{1,0:T(8,128)S(1)} %bitcast.15, s32[30,256]{1,0:T(8,128)S(1)} %bitcast.13, s32[30,256]{1,0:T(8,128)S(1)} %bitcast.14, bf16[1024,768]{1,0:T(8,128)(2,1)S(1)} %copy-done), custom_call_target="tpu_custom_call" | custom-call | flops 402653184 | bytes 4194304 | tf_op jit(solution)/shard_map/template_spectra/pallas_call | solution.py:317
  24.5 0.0 collective-permute-done.1.record_ref
  24.5 1.8 %select_channels.1 = f32[32,48,256]{2,1,0:T(8,128)S(1)} custom-call(f32[48,1024]{1,0:T(8,128)S(1)} %collective-permute-done.1.record_ref, s32[32,256]{1,0:T(8,128)S(1)} %get-tuple-element.34.high_ref, s32[32,256]{1,0:T(8,128)S(1)} %get-tuple-element.35.low_ref), custom_call_target="tpu_custom_call" | custom-call | flops 1048576 | bytes 4194304 | tf_op jit(solution)/shard_map/select_channels/pallas_call | solution.py:317
  26.4 0.0 copy-start.2
  26.4 29.0 %all_to_all.5.recv_ref = f32[32,48,256]{2,1,0:T(8,128)S(1)} all-to-all(f32[32,48,256]{2,1,0:T(8,128)S(1)} %select_channels.1), channel_id=1, replica_groups=mesh['tmpl'=32,'chan'=8] {'tmpl'}, dimensions={0} | all-to-all | bytes 3145728 | tf_op jit(solution)/shard_map/all_to_all | solution.py:379
  55.4 0.0 copy-start.1
  55.5 2.8 %collective-permute-start.2 = (f32[232,256]{1,0:T(8,128)S(1)}, f32[232,256]{1,0:T(8,128)S(1)}, u32[]{:S(2)}, u32[]{:S(2)}) collective-permute-start(f32[232,256]{1,0:T(8,128)S(1)} %get-tuple-element.38), channel_id=1, source_target_pairs={{0,1},{1,2},{2,3},{3,4},{4,5},{5,6},{6,7},{7,0},{8,9},{9,10},{10,1... | collective-permute-start | bytes 712712 | tf_op jit(solution)/shard_map/ppermute | solution.py:385
  58.3 1.6 %collective-permute-start.3 = (f32[368,256]{1,0:T(8,128)S(1)}, f32[368,256]{1,0:T(8,128)S(1)}, u32[]{:S(2)}, u32[]{:S(2)}) collective-permute-start(f32[368,256]{1,0:T(8,128)S(1)} %get-tuple-element.41), channel_id=1, source_target_pairs={{1,0},{2,1},{3,2},{4,3},{5,4},{6,5},{7,6},{0,7},{9,8},{10,9},{11,1... | collective-permute-start | bytes 1130504 | tf_op jit(solution)/shard_map/ppermute | solution.py:384
  59.9 0.0 copy-done.2
  59.9 0.0 copy-done.1
  59.9 3.1 %near_segments.1 = (f32[8,768]{1,0:T(8,128)S(1)}, f32[1536,256]{1,0:T(8,128)S(1)}) custom-call(s32[1]{0:T(128)} %bitcast.1.plane_ref, f32[32,48,256]{2,1,0:T(8,128)S(1)} %all_to_all.5.recv_ref, f32[1152,256]{1,0:T(8,128)S(1)} %get-tuple-element.36.refs_0_, bf16[1024,768]{1,0:T(8,128)(2,1)S(1)} %copy-done.1, bf16[1024,768]{1,0:T(8,128)(2,1)S(1)} %copy-done.2), custom_call_target="tpu_custom_call" | custom-call | flops 2818572288 | bytes 8388608 | tf_op jit(solution)/shard_map/near_segments/pallas_call | solution.py:317
  62.9 3.1 %collective-permute-done.2.tail_ref = f32[232,256]{1,0:T(8,128)S(1)} collective-permute-done((f32[232,256]{1,0:T(8,128)S(1)}, f32[232,256]{1,0:T(8,128)S(1)}, u32[]{:S(2)}, u32[]{:S(2)}) %collective-permute-start.2) | collective-permute-done | bytes 237600 | tf_op jit(solution)/shard_map/ppermute | solution.py:385
  66.0 1.6 %back_segment.1 = (f32[8,232]{1,0:T(8,128)S(1)}, f32[8,128]{1,0:T(8,128)S(1)}) custom-call(f32[1536,256]{1,0:T(8,128)S(1)} %get-tuple-element.37.x_ref, f32[232,256]{1,0:T(8,128)S(1)} %collective-permute-done.2.tail_ref, f32[1152,256]{1,0:T(8,128)S(1)} %get-tuple-element.36.refs_0_, bf16[1024,768]{1,0:T(8,128)(2,1)S(1)} %copy-done.1, ...), custom_call_target="tpu_custom_call" | custom-call | flops 1409286144 | bytes 8388608 | tf_op jit(solution)/shard_map/back_segment/pallas_call | solution.py:317
  67.6 1.4 %collective-permute-start.4 = (f32[8,232]{1,0:T(8,128)S(1)}, f32[8,232]{1,0:T(8,128)S(1)}, u32[]{:S(2)}, u32[]{:S(2)}) collective-permute-start(f32[8,232]{1,0:T(8,128)S(1)} %get-tuple-element.42), channel_id=1, source_target_pairs={{1,0},{2,1},{3,2},{4,3},{5,4},{6,5},{7,6},{0,7},{9,8},{10,9},{11,1... | collective-permute-start | bytes 22280 | tf_op jit(solution)/shard_map/ppermute | solution.py:400
  69.0 0.0 collective-permute-done.3.head_ref
  69.0 1.6 %last_segment.1.refs_2_ = f32[8,408]{1,0:T(8,128)S(1)} custom-call(f32[1536,256]{1,0:T(8,128)S(1)} %get-tuple-element.37.x_ref, f32[368,256]{1,0:T(8,128)S(1)} %collective-permute-done.3.head_ref, f32[1152,256]{1,0:T(8,128)S(1)} %get-tuple-element.36.refs_0_, bf16[1024,768]{1,0:T(8,128)(2,1)S(1)} %copy-done.1, bf16[1024,768]{1,0:T(8,128)(2,1)S(1)} %copy-done.2), custom_call_target="tpu_custom_call" | custom-call | flops 1409286144 | bytes 8388608 | tf_op jit(solution)/shard_map/last_segment/pallas_call | solution.py:317
  70.6 0.0 collective-permute-done.4.refs_3_
  70.6 0.7 join.1
  (1 shorter events, 0.0 us)
Async XLA Ops:
  0.0 11.2 %collective-permute-start = (f32[48,1024]{1,0:T(8,128)}, f32[48,1024]{1,0:T(8,128)S(1)}, u32[]{:S(2)}, u32[]{:S(2)}) collective-permute-start(f32[48,1024]{1,0:T(8,128)} %bitcast.16), channel_id=1, source_target_pairs={{0,0},{1,241},{2,178},{3,67},{4,52},{5,197},{6,134},{7,119},{8,120... | collective-permute-start | bytes 589832 | tf_op jit(solution)/shard_map/ppermute | solution.py:344
  11.2 13.4 %collective-permute-start.1 = (f32[48,1024]{1,0:T(8,128)S(1)}, f32[48,1024]{1,0:T(8,128)S(1)}, u32[]{:S(2)}, u32[]{:S(2)}) collective-permute-start(f32[48,1024]{1,0:T(8,128)S(1)} %collective-permute-done), channel_id=1, source_target_pairs={{0,0},{241,240},{178,176},{67,64},{52,48},{197,192},{134,128},{119... | collective-permute-start | bytes 589832 | tf_op jit(solution)/shard_map/ppermute | solution.py:355
  19.2 1.4 %copy-start = (bf16[1024,768]{1,0:T(8,128)(2,1)S(1)}, bf16[1024,768]{1,0:T(8,128)(2,1)}, u32[]{:S(2)}) copy-start(bf16[1024,768]{1,0:T(8,128)(2,1)} %constant.8.clone.table_ref.refs_1_) | copy-start | bytes 4718596
  20.6 1.1 %copy-start.3 = (f32[8,30,600]{2,0,1:T(8,128)S(1)}, f32[8,30,600]{2,0,1:T(8,128)}, u32[]{:S(2)}) copy-start(f32[8,30,600]{2,0,1:T(8,128)} %param.9) | copy-start | bytes 1728004
  21.7 0.8 %copy-start.4 = (s32[256,30]{0,1:T(8,128)S(1)}, s32[256,30]{0,1:T(8,128)}, u32[]{:S(2)}) copy-start(s32[256,30]{0,1:T(8,128)} %param.11) | copy-start | bytes 92164
  22.4 0.7 copy-start.5
  26.4 33.5 %copy-start.2 = (bf16[1024,768]{1,0:T(8,128)(2,1)S(1)}, bf16[1024,768]{1,0:T(8,128)(2,1)}, u32[]{:S(2)}) copy-start(bf16[1024,768]{1,0:T(8,128)(2,1)} %constant.9.clone.refs_2_) | copy-start | bytes 4718596
  55.4 4.5 %copy-start.1 = (bf16[1024,768]{1,0:T(8,128)(2,1)S(1)}, bf16[1024,768]{1,0:T(8,128)(2,1)}, u32[]{:S(2)}) copy-start(bf16[1024,768]{1,0:T(8,128)(2,1)} %constant.8.clone.table_ref.refs_1_) | copy-start | bytes 4718596
  55.5 10.5 %collective-permute-start.2 = (f32[232,256]{1,0:T(8,128)S(1)}, f32[232,256]{1,0:T(8,128)S(1)}, u32[]{:S(2)}, u32[]{:S(2)}) collective-permute-start(f32[232,256]{1,0:T(8,128)S(1)} %get-tuple-element.38), channel_id=1, source_target_pairs={{0,1},{1,2},{2,3},{3,4},{4,5},{5,6},{6,7},{7,0},{8,9},{9,10},{10,1... | collective-permute-start | bytes 712712 | tf_op jit(solution)/shard_map/ppermute | solution.py:385
  58.3 10.7 %collective-permute-start.3 = (f32[368,256]{1,0:T(8,128)S(1)}, f32[368,256]{1,0:T(8,128)S(1)}, u32[]{:S(2)}, u32[]{:S(2)}) collective-permute-start(f32[368,256]{1,0:T(8,128)S(1)} %get-tuple-element.41), channel_id=1, source_target_pairs={{1,0},{2,1},{3,2},{4,3},{5,4},{6,5},{7,6},{0,7},{9,8},{10,9},{11,1... | collective-permute-start | bytes 1130504 | tf_op jit(solution)/shard_map/ppermute | solution.py:384
  67.6 3.0 %collective-permute-start.4 = (f32[8,232]{1,0:T(8,128)S(1)}, f32[8,232]{1,0:T(8,128)S(1)}, u32[]{:S(2)}, u32[]{:S(2)}) collective-permute-start(f32[8,232]{1,0:T(8,128)S(1)} %get-tuple-element.42), channel_id=1, source_target_pairs={{1,0},{2,1},{3,2},{4,3},{5,4},{6,5},{7,6},{0,7},{9,8},{10,9},{11,1... | collective-permute-start | bytes 22280 | tf_op jit(solution)/shard_map/ppermute | solution.py:400
